TPU v7x, 32 devices: a whole 2x2x4 slice. The times are simulated.
32 devices in a mesh: row: 8 (over y, x, core), col: 4 (over z).
Axes of the slice: x: 2, y: 2, z: 4, core: 2. Of those that a mesh axis runs over, the one named last changes fastest.
Arguments:
- points: bfloat16 [32768, 256], P(('row', 'col'))
- centres: bfloat16 [2048, 256], replicated, may hold values from -1.5 to 1.5
- picks: int32 [2, 1024], replicated, may hold values from 0 to 32767, as said below
- assign_pts: int32 [32768], P(('row', 'col')), may hold values from 0 to 4095
- cand_assign: int32 [4096, 1], replicated, may hold values from 0 to 1023
Outputs:
- relative_cost: float32 [32768], P(('row', 'col'))
- new_centres: float32 [1024, 256], P('row')
Inputs may be any that keep to these rules, and one draw needn't show every extreme that they name: Each row of picks holds 1024 distinct point indices; in each row the points of one device, the block of 1024 consecutive indices, appear at most 64 times, and some device appears exactly 64 times.
All inputs are finite; a program needn't handle non-finite values.
Results may differ from a plain program's by a relative error of at most 0.0005.
Values may be sent and summed in bfloat16 or wider, within the bound.
No kernel may reach another device: no remote copies, remote signals or barrier semaphores. Data moves between devices by JAX's collectives and lax.ppermute only.
A program may use at most 64 MiB of HBM per device.

v0:
```python
import jax
import jax.numpy as jnp
from jax import lax
from jax.sharding import PartitionSpec as P

K_FINAL = 1024


def squared_norms(matrix):
    return jnp.einsum("nd,nd->n", matrix, matrix, preferred_element_type=jnp.float32)


def nearest_distance(points, point_norms, cand_table, keep_mask):
    total_rows = cand_table.shape[0]
    block_rows = min(512, total_rows)
    blocks = cand_table.reshape(-1, block_rows, cand_table.shape[1])
    keep_blocks = keep_mask.reshape(-1, block_rows)

    def visit_block(carried, inputs):
        block_table, block_keep = inputs
        products = lax.dot_general(
            points, block_table, (((1,), (1,)), ((), ())), preferred_element_type=jnp.float32
        )
        distance = point_norms[:, None] + squared_norms(block_table)[None, :] - 2.0 * products
        distance = jnp.where(block_keep[None, :], distance, jnp.inf)
        return (jnp.minimum(carried, jnp.min(distance, axis=1)), None)

    start_value = jnp.full((points.shape[0],), jnp.inf, jnp.float32)
    result, unused = lax.scan(visit_block, start_value, (blocks, keep_blocks))
    return result


def shards(points, centres, picks, assign_pts, cand_assign):
    point_count = points.shape[0]
    feature_count = points.shape[1]
    device_count = lax.axis_size("row") * lax.axis_size("col")
    device_index = lax.axis_index("row") * lax.axis_size("col") + lax.axis_index("col")
    round_count, sample_count = picks.shape
    first_count = centres.shape[0]
    cand_count = first_count + round_count * sample_count
    local_index = picks - device_index * point_count
    owned = (local_index >= 0) & (local_index < point_count)
    clipped = jnp.clip(local_index, 0, point_count - 1)
    tally = jax.ops.segment_sum(
        jnp.ones((point_count,), jnp.float32), assign_pts, num_segments=cand_count
    )
    point_norms = squared_norms(points)
    picked = jnp.where(
        owned[:, :, None], points[clipped].astype(jnp.float32), jnp.zeros((), jnp.float32)
    )
    summed = lax.psum(picked.reshape(-1, feature_count), ("row", "col"))
    cand_table = jnp.concatenate([centres, summed.astype(jnp.bfloat16)], axis=0)
    slot_ids = jnp.arange(cand_count, dtype=jnp.int32)
    keep_mask = slot_ids >= 0
    nearest = nearest_distance(points, point_norms, cand_table, keep_mask)
    best = jnp.maximum(nearest, 0.0)
    total_cost, counts = lax.psum((jnp.sum(best), tally), ("row", "col"))
    relative_cost = best * (point_count * device_count) / total_cost
    safe_ids = jnp.clip(slot_ids, 0, cand_count - 1)
    weights = jnp.where(keep_mask, 1.0 + counts[safe_ids], 0.0)
    owners = cand_assign[:, 0][safe_ids]
    block_final = K_FINAL // lax.axis_size("row")
    targets = lax.axis_index("row") * block_final + jnp.arange(block_final, dtype=jnp.int32)
    member = jnp.where(owners[None, :] == targets[:, None], weights[None, :], 0.0)
    numerator = jnp.dot(member, cand_table.astype(jnp.float32), precision=lax.Precision.HIGHEST)
    denominator = jnp.sum(member, axis=1)
    new_centres = numerator / denominator[:, None]
    return (relative_cost, new_centres)


def solution(mesh):
    placed = (P(("row", "col"), None), P(), P(), P(("row", "col")), P())
    return jax.shard_map(
        shards,
        mesh=mesh,
        in_specs=placed,
        out_specs=(P(("row", "col")), P("row", None)),
        check_vma=False,
    )
```

profile of v0, /device:TPU:0, one launch (start us, length us, event | category | flops | bytes accessed | tf_op | source)
XLA Modules:
  0.0 177.2 jit_solution(14300699518341671426)
XLA Ops:
  0.7 0.7 fusion.16
  1.4 7.8 %gather_fusion = bf16[2048,256]{1,0:T(8,128)(2,1)S(1)} fusion(bf16[1024,256]{1,0:T(8,128)(2,1)} %param.7, s32[2048]{0:T(1024)S(1)} %bitcast_clamp_fusion), kind=kCustom, calls=%fused_computation | custom fusion | bytes 2105344 | tf_op jit(solution)/shard_map/gather | solution.py:49
  9.2 0.3 convert_select_fusion
  9.5 64.3 %all-reduce.2 = bf16[2048,256]{1,0:T(8,128)(2,1)} all-reduce(f32[2048,256]{1,0:T(8,128)S(1)} %convert_select_fusion), channel_id=1, replica_groups=mesh['row'=8,'col'=4] {'row','col'}, use_global_device_ids=true, to_apply=%region_0.1 | all-reduce | flops 524288 | bytes 3145728 | tf_op jit(solution)/shard_map/psum | solution.py:51
  73.9 1.7 pad_maximum_fusion
  75.6 0.2 fusion.11
  75.8 5.4 %while.12 = (s32[]{:T(128)}, f32[1024]{0:T(1024)S(1)}, f32[1024]{0:T(1024)S(1)}, bf16[8,512,256]{2,1,0:T(8,128)(2,1)S(1)}, bf16[1024,256]{1,0:T(8,128)(2,1)S(1)}, /*index=5*/s32[]{:T(128)}, s32[]{:T(128)}) while((s32[]{:T(128)}, f32[1024]{0:T(1024)S(1)}, f32[1024]{0:T(1024)S(1)}, bf16[8,512,256]{2,1,0:T(8,128)(2,1)S(1)}, ...), condition=%wide.region_3.4_spmd.clone, body=%wide.region_1.3_spmd.clone.sunk | while | flops 270926336 | bytes 1073247 | solution.py:29
  76.0 0.5 fusion.28
  76.5 0.2 fusion.27
  76.7 0.5 fusion.28
  77.4 0.5 fusion.28
  78.1 0.5 fusion.28
  78.7 0.5 fusion.28
  79.4 0.5 fusion.28
  80.1 0.5 fusion.28
  80.8 0.5 fusion.28
  81.3 0.6 maximum_reduce_fusion
  81.9 6.1 %scatter_custom_fusion = f32[4096]{0:T(1024)S(1)} fusion(s32[1024]{0:T(1024)} %param.10, f32[1024]{0:T(1024)S(1)} %broadcast.73, f32[]{:T(128)} %constant.54.clone.1), kind=kCustom, calls=%fused_computation.32 | custom fusion | flops 1024 | bytes 16896 | tf_op jit(solution)/shard_map/scatter-add | solution.py:44
  88.0 39.5 %all-reduce = (f32[]{:T(128)}, f32[4096]{0:T(1024)S(1)}) all-reduce(f32[]{:T(128)} %maximum_reduce_fusion, f32[4096]{0:T(1024)S(1)} %scatter_custom_fusion), channel_id=1, replica_groups=mesh['row'=8,'col'=4] {'row','col'}, use_global_device_ids=true, to_apply=%region_5.6 | all-reduce | flops 4097 | bytes 32776 | tf_op jit(solution)/shard_map/psum | solution.py:57
  127.5 23.0 %gather_fusion.2 = f32[4096]{0:T(1024)S(1)} fusion(f32[4096]{0:T(1024)S(1)} %get-tuple-element.79, s32[4096]{0:T(1024)S(1)} %broadcast_clamp_fusion), kind=kCustom, calls=%fused_computation.2 | custom fusion | bytes 49152 | tf_op jit(solution)/shard_map/gather | solution.py:60
  150.6 23.0 %gather_fusion.1 = s32[4096]{0:T(1024)S(1)} fusion(s32[4096]{0:T(1024)S(1)} %bitcast.24, s32[4096]{0:T(1024)S(1)} %broadcast_clamp_fusion), kind=kCustom, calls=%fused_computation.1 | custom fusion | bytes 49152 | tf_op jit(solution)/shard_map/gather | solution.py:61
  173.7 0.4 select_reduce_fusion
  174.0 1.9 %fusion.8 = f32[128,256]{1,0:T(8,128)} fusion(f32[4096]{0:T(1024)S(1)} %broadcast_add_fusion, s32[4096]{0:T(1024)S(1)} %gather_fusion.1, s32[128]{0:T(128)S(1)} %iota_add_fusion, f32[128]{0:T(128)S(1)} %select_reduce_fusion, bf16[2048,256]{1,0:T(8,128)(2,1)S(1)} %copy-done.2, bf16[2048,256]{1,0:T(8,128)(2,1)S(1)} %copy-done.3), kind=kOutput, calls=%fused_computation.18 | convolution fusion | flops 1615888384 | bytes 2262016 | tf_op jit(solution)/shard_map/dot_general | solution.py:65
  175.9 1.3 multiply_divide_fusion
  (34 shorter events, 1.2 us)
Async XLA Ops:
  0.6 150.0 %copy-start = (s32[4096,1]{0,1:T(1,128)S(1)}, s32[4096,1]{0,1:T(1,128)}, u32[]{:S(2)}) copy-start(s32[4096,1]{0,1:T(1,128)} %param.11) | copy-start | bytes 49156
  1.4 7.8 %copy-start.4 = (s32[2,1024]{1,0:T(2,128)S(1)}, s32[2,1024]{1,0:T(2,128)}, u32[]{:S(2)}) copy-start(s32[2,1024]{1,0:T(2,128)} %param.9) | copy-start | bytes 24580
  73.9 1.8 copy-start.1
  150.6 23.4 %copy-start.2 = (bf16[2048,256]{1,0:T(8,128)(2,1)S(1)}, bf16[2048,256]{1,0:T(8,128)(2,1)}, u32[]{:S(2)}) copy-start(bf16[2048,256]{1,0:T(8,128)(2,1)} %all-reduce.2) | copy-start | bytes 3145732
  150.6 23.4 %copy-start.3 = (bf16[2048,256]{1,0:T(8,128)(2,1)S(1)}, bf16[2048,256]{1,0:T(8,128)(2,1)}, u32[]{:S(2)}) copy-start(bf16[2048,256]{1,0:T(8,128)(2,1)} %param.8) | copy-start | bytes 3145732
where the time goes:
time: 178 us; the launch traced here: 177 us
  blocking collectives  104 us (58%)
  local copies, waits for them, and re-layouts  53.9 us (30%)
  other arithmetic  12.6 us (7%)
  matrix products  5.76 us (3%)
    psum x1, blocking collectives, shards(): summed = lax.psum(picked.reshape(-1, feature_count), ('row', 'col'))  64.3 us
    psum x1, blocking collectives, shards(): total_cost, counts = lax.psum((jnp.sum(best), tally), ('row', 'col'))  39.5 us
    gather x1, local copies, waits for them, and re-layouts, shards(): weights = jnp.where(keep_mask, 1.0 + counts[safe_ids], 0.0)  23 us
    gather x1, local copies, waits for them, and re-layouts, shards(): owners = cand_assign[:, 0][safe_ids]  23 us
    gather x1, local copies, waits for them, and re-layouts, shards(): points[clipped].astype(jnp.float32)  7.75 us
    scatter-add x1, other arithmetic, shards(): jax.ops.segment_sum(jnp.ones((point_count,), jnp.float32), assign_pts, nu...  6.06 us
    dot_general x8, matrix products, visit_block(): lax.dot_general(points, block_table, (((1,), (1,)), ((), ())), preferred_...  3.88 us

commit v1 on v0

v1 whole, which is shorter than its diff:
```python
import functools

import jax
import jax.numpy as jnp
from jax import lax
from jax.experimental import pallas as pl
from jax.experimental.pallas import tpu as pltpu
from jax.sharding import PartitionSpec as P

K_FINAL = 1024
AXES = ("row", "col")
LANES = 128
VMEM_LIMIT = 48 * 1024 * 1024
F32 = jnp.float32
BF16 = jnp.bfloat16

CORE = 4
ORDERS = ((2, 1, 16, 8), (8, 2, 1, 16))


def nt_dot(left, right):
    return lax.dot_general(left, right, (((1,), (1,)), ((), ())), preferred_element_type=F32)


def iota(shape, axis):
    return lax.broadcasted_iota(jnp.int32, shape, axis)


def device_index():
    return lax.axis_index("row") * lax.axis_size("col") + lax.axis_index("col")


def whole_spec():
    return pl.BlockSpec(memory_space=pltpu.VMEM)


def local_call(kernel, out_shape, operands, name, flops=0):
    moved = sum(x.size * x.dtype.itemsize for x in operands)
    return pl.pallas_call(
        kernel,
        out_shape=out_shape,
        in_specs=[whole_spec()] * len(operands),
        out_specs=jax.tree.map(lambda _: whole_spec(), out_shape),
        compiler_params=pltpu.CompilerParams(vmem_limit_bytes=VMEM_LIMIT),
        cost_estimate=pl.CostEstimate(flops=flops, bytes_accessed=moved, transcendentals=0),
        name=name,
    )(*operands)


def pick_kernel(rounds, cap, picks_ref, points_ref, centres_ref, out_ref):
    chunks = picks_ref.shape[0]
    per_round = chunks // rounds
    point_count = points_ref.shape[0]
    slots = out_ref.shape[0]
    local = picks_ref[...] - device_index() * point_count
    owned = (local >= 0) & (local < point_count)
    flags = owned.astype(F32).astype(BF16)
    lower = (iota((LANES, LANES), 0) <= iota((LANES, LANES), 1)).astype(F32).astype(BF16)
    inside = jnp.dot(flags, lower, preferred_element_type=F32)
    sums = jnp.dot(flags, jnp.ones((LANES, LANES), BF16), preferred_element_type=F32)
    first, second = iota((chunks, chunks), 0), iota((chunks, chunks), 1)
    same = lax.div(first, per_round) == lax.div(second, per_round)
    earlier = (same & (second < first)).astype(F32).astype(BF16)
    before = jnp.dot(earlier, sums.astype(BF16), preferred_element_type=F32)
    round_of = lax.div(iota((chunks, LANES), 0), per_round)
    slot = (inside + before).astype(jnp.int32) - 1 + round_of * cap
    slot = jnp.where(owned, slot, -1)
    slot_ids = iota((slots, LANES), 0)
    found = jnp.zeros((slots, LANES), jnp.int32)
    for t in range(chunks):
        found = found + jnp.where(slot[t : t + 1, :] == slot_ids, local[t : t + 1, :] + 1, 0)
    place = jnp.sum(found.astype(F32), axis=1, keepdims=True).astype(jnp.int32)
    chosen = (iota((slots, point_count), 1) + 1 == place).astype(F32).astype(BF16)
    rows = jnp.dot(chosen, points_ref[...], preferred_element_type=F32)
    filler = centres_ref[0:1, :].astype(F32)
    out_ref[...] = jnp.where(place > 0, rows, filler).astype(BF16)


def meta_kernel(rounds, cap, slots, picks_ref, assign_ref, owner_ref, block_ref, count_ref, place_ref, slot_owner_ref):
    chunks = picks_ref.shape[0]
    per_round = chunks // rounds
    cand_chunks = owner_ref.shape[0]
    device_count = block_ref.shape[0]
    slot_chunks = slot_owner_ref.shape[0]
    lane_rows = iota((LANES, LANES), 0)
    tally = jnp.zeros((cand_chunks, LANES), F32)
    for t in range(assign_ref.shape[0]):
        ids = assign_ref[t : t + 1, :]
        high = (lax.div(ids, LANES) == iota((cand_chunks, LANES), 0)).astype(F32).astype(BF16)
        low = (lax.rem(ids, LANES) == lane_rows).astype(F32).astype(BF16)
        tally = tally + nt_dot(high, low)
    count_ref[...] = tally

    lower = (lane_rows <= iota((LANES, LANES), 1)).astype(F32).astype(BF16)
    ones = jnp.ones((LANES, LANES), BF16)
    device_ids = iota((device_count, LANES), 0)
    point_count = assign_ref.shape[0] * LANES
    first_chunk = cand_chunks - chunks
    owners = jnp.zeros((2 * slot_chunks, LANES), F32)
    for r in range(rounds):
        carry = jnp.zeros((device_count, LANES), F32)
        for u in range(per_round):
            t = r * per_round + u
            holder = lax.div(picks_ref[t : t + 1, :], point_count)
            held = (holder == device_ids).astype(F32)
            running = jnp.dot(held.astype(BF16), lower, preferred_element_type=F32) + carry
            carry = carry + jnp.dot(held.astype(BF16), ones, preferred_element_type=F32)
            rank = jnp.sum(held * running, axis=0, keepdims=True).astype(jnp.int32) - 1
            block = jnp.sum(jnp.where(block_ref[...] == holder, device_ids, 0), axis=0, keepdims=True)
            place = block * slots + r * cap + rank
            place_ref[t : t + 1, :] = place
            high = lax.div(place, LANES) == iota((slot_chunks, LANES), 0)
            low = (lax.rem(place, LANES) == lane_rows).astype(F32).astype(BF16)
            tag = owner_ref[first_chunk + t : first_chunk + t + 1, :] + 1
            coarse = jnp.where(high, lax.div(tag, 32).astype(F32), 0.0)
            fine = jnp.where(high, lax.rem(tag, 32).astype(F32), 0.0)
            owners = owners + nt_dot(jnp.concatenate([coarse, fine], axis=0).astype(BF16), low)
    slot_owner_ref[...] = (owners[:slot_chunks] * 32.0 + owners[slot_chunks:]).astype(jnp.int32) - 1


def scan_pieces(points_ref, piece_refs, best):
    points = points_ref[...]
    for piece_ref in piece_refs:
        rows = piece_ref.shape[0]
        step = min(256, rows)

        def visit(i, best, piece_ref=piece_ref, step=step):
            piece = piece_ref[pl.ds(pl.multiple_of(i * step, step), step), :]
            wide = piece.astype(F32)
            half = 0.5 * jnp.sum(wide * wide, axis=1, keepdims=True)
            score = nt_dot(piece, points) - half
            for k in range(step // 8):
                best = jnp.maximum(best, score[k * 8 : k * 8 + 8, :])
            return best

        best = lax.fori_loop(0, rows // step, visit, best)
    return best


def first_scan_kernel(points_ref, *refs):
    best = jnp.full((8, points_ref.shape[0]), -jnp.inf, F32)
    refs[-1][...] = scan_pieces(points_ref, refs[:-1], best)


def next_scan_kernel(points_ref, best_ref, *refs):
    refs[-1][...] = scan_pieces(points_ref, refs[:-1], best_ref[...])


def last_scan_kernel(points_ref, best_ref, *refs):
    near_ref, share_ref = refs[-2:]
    best = scan_pieces(points_ref, refs[:-2], best_ref[...])
    best = jnp.max(best, axis=0, keepdims=True)
    wide = points_ref[...].astype(F32)
    square = wide * wide
    top = square.astype(BF16)
    rest = (square - top.astype(F32)).astype(BF16)
    ones = jnp.ones((8, square.shape[1]), BF16)
    norm = (nt_dot(ones, top) + nt_dot(ones, rest))[0:1, :]
    near = jnp.maximum(norm - 2.0 * best, 0.0)
    near_ref[...] = near
    share_ref[...] = jnp.broadcast_to(jnp.sum(near, axis=1, keepdims=True)[None], share_ref.shape)


def scale_kernel(total_points, near_ref, share_ref, out_ref):
    total = jnp.sum(share_ref[...], axis=0)[0:1, 0:1]
    out_ref[...] = near_ref[...] * total_points / total


def lloyd_kernel(count_ref, owner_ref, place_ref, slot_owner_ref, centres_ref, *refs):
    piece_refs, out_ref = refs[:-1], refs[-1]
    finals = out_ref.shape[0]
    slot_chunks = slot_owner_ref.shape[0]
    chunks = place_ref.shape[0]
    first_chunks = owner_ref.shape[0] - chunks
    weights = 1.0 + count_ref[...]
    weight_top = weights.astype(BF16).astype(F32)
    weight_rest = (weights - weight_top).astype(BF16).astype(F32)
    lane_rows = iota((LANES, LANES), 0)
    placed = jnp.zeros((2 * slot_chunks, LANES), F32)
    for t in range(chunks):
        place = place_ref[t : t + 1, :]
        high = lax.div(place, LANES) == iota((slot_chunks, LANES), 0)
        low = (lax.rem(place, LANES) == lane_rows).astype(F32).astype(BF16)
        c = first_chunks + t
        both = [jnp.where(high, w[c : c + 1, :], 0.0) for w in (weight_top, weight_rest)]
        placed = placed + nt_dot(jnp.concatenate(both, axis=0).astype(BF16), low)
    targets = iota((finals, LANES), 0) + lax.axis_index("row") * finals

    def add_rows(carried, rows_ref, owners, tops, rests):
        total, mass = carried
        parts = []
        for b in range(owners.shape[0]):
            mine = owners[b : b + 1, :] == targets
            top = jnp.where(mine, tops[b : b + 1, :], 0.0)
            rest = jnp.where(mine, rests[b : b + 1, :], 0.0)
            mass = mass + (top + rest)
            parts.append(jnp.concatenate([top, rest], axis=0).astype(BF16))
        member = jnp.concatenate(parts, axis=1)
        return total + jnp.dot(member, rows_ref[...], preferred_element_type=F32), mass

    carried = (jnp.zeros((2 * finals, centres_ref.shape[1]), F32), jnp.zeros((finals, LANES), F32))
    carried = add_rows(
        carried, centres_ref, owner_ref[:first_chunks, :], weight_top[:first_chunks], weight_rest[:first_chunks]
    )
    start = 0
    for piece_ref in piece_refs:
        stop = start + piece_ref.shape[0] // LANES
        carried = add_rows(
            carried,
            piece_ref,
            slot_owner_ref[start:stop, :],
            placed[start:stop],
            placed[slot_chunks + start : slot_chunks + stop],
        )
        start = stop
    total, mass = carried
    out_ref[...] = (total[:finals] + total[finals:]) / jnp.sum(mass, axis=1, keepdims=True)


def xor_pairs(masks):
    return [(d, d ^ masks[(d // CORE) % 2]) for d in range(32)]


def block_order(doubling):
    device_count = lax.axis_size("row") * lax.axis_size("col")
    ids = jnp.arange(device_count, dtype=jnp.int32)
    if not doubling:
        return ids
    me = device_index()
    tables = []
    for mine in (0, 1):
        table = []
        for other in (0, 1):
            for q in range(16):
                mask = CORE * other
                for k in range(4):
                    if (q >> k) & 1:
                        mask ^= ORDERS[mine ^ other][k]
                table.append(mask)
        tables.append([table[i] for i in range(32)])
    core = lax.rem(lax.div(me, CORE), 2)
    return jnp.where(core == 0, jnp.array(tables[0], jnp.int32), jnp.array(tables[1], jnp.int32)) ^ me


def shards(points, centres, picks, assign_pts, cand_assign):
    point_count, feature_count = points.shape
    row_count, col_count = lax.axis_size("row"), lax.axis_size("col")
    device_count = row_count * col_count
    doubling = (row_count, col_count) == (8, 4)
    round_count, sample_count = picks.shape
    cand_count = centres.shape[0] + round_count * sample_count
    cap = min(point_count, sample_count, -(-2 * sample_count // device_count))
    slots = -(-round_count * cap // 16) * 16
    slot_chunks = device_count * slots // LANES
    pick_rows = picks.reshape(-1, LANES)
    chunks = pick_rows.shape[0]
    shape = jax.ShapeDtypeStruct

    block = local_call(
        functools.partial(pick_kernel, round_count, cap),
        shape((slots, feature_count), BF16),
        (pick_rows, points, centres[:16]),
        "pick_rows",
    )
    order = jnp.broadcast_to(block_order(doubling)[:, None], (device_count, LANES))
    owner_rows = cand_assign.reshape(-1, LANES)
    counts, places, slot_owners = local_call(
        functools.partial(meta_kernel, round_count, cap, slots),
        (
            shape((cand_count // LANES, LANES), F32),
            shape((chunks, LANES), jnp.int32),
            shape((slot_chunks, LANES), jnp.int32),
        ),
        (pick_rows, assign_pts.reshape(-1, LANES), owner_rows, order),
        "slot_owners",
    )
    best_shape = shape((8, point_count), F32)
    scan_flops = 2 * point_count * feature_count

    def first_scan(pieces):
        rows = sum(p.shape[0] for p in pieces)
        return local_call(first_scan_kernel, best_shape, (points, *pieces), "scan_centres", scan_flops * rows)

    def next_scan(best, pieces):
        rows = sum(p.shape[0] for p in pieces)
        return local_call(next_scan_kernel, best_shape, (points, best, *pieces), "scan_sampled", scan_flops * rows)

    def last_scan(best, pieces):
        rows = sum(p.shape[0] for p in pieces)
        return local_call(
            last_scan_kernel,
            (shape((1, point_count), F32), shape((device_count, 8, LANES), F32)),
            (points, best, *pieces),
            "scan_last",
            scan_flops * rows,
        )

    best = first_scan([centres])
    if doubling:
        buffer = block
        for k in range(4):
            pairs = xor_pairs((ORDERS[0][k], ORDERS[1][k]))
            received = lax.ppermute(buffer, AXES, pairs)
            counts = counts + lax.ppermute(counts, AXES, pairs)
            if k < 3:
                buffer = jnp.concatenate([buffer, received], axis=0)
        swap = xor_pairs((CORE, CORE))
        counts = counts + lax.ppermute(counts, AXES, swap)
        early = lax.ppermute(buffer, AXES, swap)
        late = lax.ppermute(received, AXES, swap)
        pieces = [buffer, received, early, late]
        best = next_scan(best, [buffer, early])
        best = next_scan(best, [received])
        near, share = last_scan(best, [late])
        shares = lax.all_to_all(share, AXES, 0, 0)
    else:
        counts = lax.psum(counts, AXES)
        pieces = [lax.all_gather(block, AXES, tiled=True)]
        near, share = last_scan(best, pieces)
        shares = lax.psum(share[:1], AXES)
    relative = local_call(
        functools.partial(scale_kernel, float(point_count * device_count)),
        shape((1, point_count), F32),
        (near, shares),
        "relative",
    )
    new_centres = local_call(
        lloyd_kernel,
        shape((K_FINAL // row_count, feature_count), F32),
        (counts, owner_rows, places, slot_owners, centres, *pieces),
        "lloyd",
        4 * K_FINAL // row_count * feature_count * cand_count,
    )
    return (relative.reshape(-1), new_centres)


def solution(mesh):
    placed = (P(AXES, None), P(), P(), P(AXES), P())
    return jax.shard_map(
        shards,
        mesh=mesh,
        in_specs=placed,
        out_specs=(P(AXES), P("row", None)),
        check_vma=False,
    )
```

time: 178 us -> 71.5 us (0.40)
  blocking collectives: 104 us -> 0 us
  local copies, waits for them, and re-layouts: 53.9 us -> 4.19 us
  waiting for transfers between devices: 0 us -> 27.2 us
  starting transfers between devices: 0 us -> 24 us
  Pallas kernels: 0 us -> 14.7 us
  other arithmetic: 12.6 us -> 0.09 us
  matrix products: 5.76 us -> 0 us
    psum x2 -> x0, blocking collectives: 104 us -> none  [the longest x1 64.3 us: shards(): summed = lax.psum(picked.reshape(-1, feature_count), ('row', 'col'))]
    gather x3 -> x0, local copies, waits for them, and re-layouts: 53.8 us -> none  [the longest x1 23 us: shards(): weights = jnp.where(keep_mask, 1.0 + counts[safe_ids], 0.0)]
    ppermute x0 -> x11, waiting for transfers between devices: none -> 27.2 us  [the longest x4 17.3 us: shards(): received = lax.ppermute(buffer, AXES, pairs)]
    ppermute x0 -> x11, starting transfers between devices: none -> 17.4 us  [the longest x4 9.98 us: shards(): received = lax.ppermute(buffer, AXES, pairs)]
    pallas_call x0 -> x8, Pallas kernels: none -> 14.7 us  [local_call(): pl.pallas_call(kernel, out_shape=out_shape, in_specs=[whole_spec()] * len...]
    all_to_all x0 -> x1, starting transfers between devices: none -> 6.65 us  [shards(): shares = lax.all_to_all(share, AXES, 0, 0)]
    scatter-add x1 -> x0, other arithmetic: 6.06 us -> none  [shards(): jax.ops.segment_sum(jnp.ones((point_count,), jnp.float32), assign_pts, nu...]
    dot_general x9 -> x0, matrix products: 5.76 us -> none  [the longest x8 3.88 us: visit_block(): lax.dot_general(points, block_table, (((1,), (1,)), ((), ())), preferred_...]
  transfers between devices with their start and end apart: 0 -> 12, of which waited for: 0 -> 9; matrix products, arithmetic and copies ran while one was open for 0% -> 0% of each run, Pallas kernels for 0% -> 15%
where the time goes in v1:
time: 71.5 us; the launch traced here: 71.1 us
  waiting for transfers between devices  27.2 us (38%)
  starting transfers between devices  24 us (34%)
  Pallas kernels  14.7 us (21%)
  local copies, waits for them, and re-layouts  4.19 us (6%)
  between operations  0.78 us (1%)
    ppermute x4, waiting for transfers between devices, shards(): received = lax.ppermute(buffer, AXES, pairs)  17.3 us
    pallas_call x8, Pallas kernels, local_call(): pl.pallas_call(kernel, out_shape=out_shape, in_specs=[whole_spec()] * len...  14.7 us
    ppermute x4, starting transfers between devices, shards(): received = lax.ppermute(buffer, AXES, pairs)  9.98 us
    ppermute x4, waiting for transfers between devices, shards(): counts = counts + lax.ppermute(counts, AXES, pairs)  8.74 us
    ppermute x4, starting transfers between devices, shards(): counts = counts + lax.ppermute(counts, AXES, pairs)  7.4 us
    all_to_all x1, starting transfers between devices, shards(): shares = lax.all_to_all(share, AXES, 0, 0)  6.65 us
    unnamed x14, local copies, waits for them, and re-layouts  2.72 us
  transfers between devices with their start and end apart: 12, of which 9 were waited for; matrix products, arithmetic and copies ran while one was open for 0% of the time, Pallas kernels for 15%

profile of v1, /device:TPU:0, one launch (start us, length us, event | category | flops | bytes accessed | tf_op | source)
XLA Modules:
  0.0 71.1 jit_solution(990654584479205264)
XLA Ops:
  3.7 4.1 %collective-permute-start = (bf16[128,256]{1,0:T(8,128)(2,1)S(1)}, bf16[128,256]{1,0:T(8,128)(2,1)S(1)}, u32[]{:S(2)}, u32[]{:S(2)}) collective-permute-start(bf16[128,256]{1,0:T(8,128)(2,1)S(1)} %pick_rows.1), channel_id=1, source_target_pairs={{0,2},{1,3},{2,0},{3,1},{4,12},{5,13},{6,14},{7,15},{8,10},{9,11},... | collective-permute-start | bytes 196616 | tf_op jit(solution)/shard_map/ppermute | solution.py:303
  7.8 2.2 %collective-permute-done = bf16[128,256]{1,0:T(8,128)(2,1)S(1)} collective-permute-done((bf16[128,256]{1,0:T(8,128)(2,1)S(1)}, bf16[128,256]{1,0:T(8,128)(2,1)S(1)}, u32[]{:S(2)}, u32[]{:S(2)}) %collective-permute-start) | collective-permute-done | bytes 65568 | tf_op jit(solution)/shard_map/ppermute | solution.py:303
  10.1 2.0 %collective-permute-start.1 = (bf16[256,256]{1,0:T(8,128)(2,1)S(1)}, bf16[256,256]{1,0:T(8,128)(2,1)S(1)}, u32[]{:S(2)}, u32[]{:S(2)}) collective-permute-start(bf16[256,256]{1,0:T(8,128)(2,1)S(1)} %pad_maximum_fusion.2), channel_id=1, source_target_pairs={{0,1},{1,0},{2,3},{3,2},{4,6},{5,7},{6,4},{7,5},{8,9},{9,8},{10,11... | collective-permute-start | bytes 393224 | tf_op jit(solution)/shard_map/ppermute | solution.py:303
  12.1 3.3 %collective-permute-done.1 = bf16[256,256]{1,0:T(8,128)(2,1)S(1)} collective-permute-done((bf16[256,256]{1,0:T(8,128)(2,1)S(1)}, bf16[256,256]{1,0:T(8,128)(2,1)S(1)}, u32[]{:S(2)}, u32[]{:S(2)}) %collective-permute-start.1) | collective-permute-done | bytes 131104 | tf_op jit(solution)/shard_map/ppermute | solution.py:303
  15.4 2.0 %collective-permute-start.2 = (bf16[512,256]{1,0:T(8,128)(2,1)S(1)}, bf16[512,256]{1,0:T(8,128)(2,1)S(1)}, u32[]{:S(2)}, u32[]{:S(2)}) collective-permute-start(bf16[512,256]{1,0:T(8,128)(2,1)S(1)} %pad_maximum_fusion.1), channel_id=1, source_target_pairs={{0,16},{1,17},{2,18},{3,19},{4,5},{5,4},{6,7},{7,6},{8,24},{9,25},... | collective-permute-start | bytes 786440 | tf_op jit(solution)/shard_map/ppermute | solution.py:303
  17.3 4.5 %collective-permute-done.2 = bf16[512,256]{1,0:T(8,128)(2,1)S(1)} collective-permute-done((bf16[512,256]{1,0:T(8,128)(2,1)S(1)}, bf16[512,256]{1,0:T(8,128)(2,1)S(1)}, u32[]{:S(2)}, u32[]{:S(2)}) %collective-permute-start.2) | collective-permute-done | bytes 262176 | tf_op jit(solution)/shard_map/ppermute | solution.py:303
  21.9 1.9 %collective-permute-start.4 = (bf16[1024,256]{1,0:T(8,128)(2,1)S(1)}, bf16[1024,256]{1,0:T(8,128)(2,1)S(1)}, u32[]{:S(2)}, u32[]{:S(2)}) collective-permute-start(bf16[1024,256]{1,0:T(8,128)(2,1)S(1)} %pad_maximum_fusion.refs_0_), channel_id=1, source_target_pairs={{0,8},{1,9},{2,10},{3,11},{4,20},{5,21},{6,22},{7,23},{8,0},{9,1},... | collective-permute-start | bytes 1572872 | tf_op jit(solution)/shard_map/ppermute | solution.py:303
  23.8 7.3 %collective-permute-done.4.refs_0_.refs_1_ = bf16[1024,256]{1,0:T(8,128)(2,1)S(1)} collective-permute-done((bf16[1024,256]{1,0:T(8,128)(2,1)S(1)}, bf16[1024,256]{1,0:T(8,128)(2,1)S(1)}, u32[]{:S(2)}, u32[]{:S(2)}) %collective-permute-start.4) | collective-permute-done | bytes 524320 | tf_op jit(solution)/shard_map/ppermute | solution.py:303
  32.1 2.8 %scan_centres.1.best_ref = f32[8,1024]{1,0:T(8,128)S(1)} custom-call(bf16[1024,256]{1,0:T(8,128)(2,1)S(1)} %copy-done.2, bf16[2048,256]{1,0:T(8,128)(2,1)S(1)} %copy-done), custom_call_target="tpu_custom_call" | custom-call | flops 1073741824 | bytes 1572864 | tf_op jit(solution)/shard_map/scan_centres/pallas_call | solution.py:39
  35.0 2.8 %scan_sampled.2.best_ref = f32[8,1024]{1,0:T(8,128)S(1)} custom-call(bf16[1024,256]{1,0:T(8,128)(2,1)S(1)} %copy-done.2, f32[8,1024]{1,0:T(8,128)S(1)} %scan_centres.1.best_ref, bf16[1024,256]{1,0:T(8,128)(2,1)S(1)} %pad_maximum_fusion.refs_0_, bf16[1024,256]{1,0:T(8,128)(2,1)S(1)} %collective-permute-done.3.refs_1_.refs_2_), custom_call_target="tpu_custom_call" | custom-call | flops 1073741824 | bytes 1605632 | tf_op jit(solution)/shard_map/scan_sampled/pallas_call | solution.py:39
  37.8 1.4 %scan_sampled.3.best_ref = f32[8,1024]{1,0:T(8,128)S(1)} custom-call(bf16[1024,256]{1,0:T(8,128)(2,1)S(1)} %copy-done.2, f32[8,1024]{1,0:T(8,128)S(1)} %scan_sampled.2.best_ref, bf16[1024,256]{1,0:T(8,128)(2,1)S(1)} %collective-permute-done.4.refs_0_.refs_1_), custom_call_target="tpu_custom_call" | custom-call | flops 536870912 | bytes 1081344 | tf_op jit(solution)/shard_map/scan_sampled/pallas_call | solution.py:39
  39.2 2.6 %scan_last.1 = (f32[1,1024]{1,0:T(1,128)S(1)}, f32[32,8,128]{2,1,0:T(8,128)}) custom-call(bf16[1024,256]{1,0:T(8,128)(2,1)S(1)} %copy-done.2, f32[8,1024]{1,0:T(8,128)S(1)} %scan_sampled.3.best_ref, bf16[1024,256]{1,0:T(8,128)(2,1)S(1)} %collective-permute-done.5.refs_0_.refs_3_), custom_call_target="tpu_custom_call" | custom-call | flops 536870912 | bytes 1081344 | tf_op jit(solution)/shard_map/scan_last/pallas_call | solution.py:39
  41.8 6.6 %all-to-all-start = ((f32[32,8,128]{2,1,0:T(8,128)}), f32[32,8,128]{2,1,0:T(8,128)S(1)}, u32[]{:S(2)}, u32[]{:S(2)}) async-start(f32[32,8,128]{2,1,0:T(8,128)} %get-tuple-element.8), calls=%async_computation | async-start | bytes 262144 | tf_op jit(solution)/shard_map/all_to_all | solution.py:315
  49.2 1.2 %slot_owners.1 = (f32[32,128]{1,0:T(8,128)S(1)}, s32[16,128]{1,0:T(8,128)S(1)}, s32[32,128]{1,0:T(8,128)S(1)}) custom-call(s32[16,128]{1,0:T(8,128)S(1)} %reshape.17.picks_ref, s32[8,128]{1,0:T(8,128)S(1)} %bitcast.5, s32[32,128]{1,0:T(8,128)S(1)} %bitcast.3, s32[32,128]{1,0:T(8,128)S(1)} %broadcast_in_dim.2.block_ref), custom_call_target="tpu_custom_call" | custom-call | bytes 45056 | tf_op jit(solution)/shard_map/slot_owners/pallas_call | solution.py:39
  50.4 2.7 %collective-permute-start.6 = (f32[32,128]{1,0:T(8,128)S(1)}, f32[32,128]{1,0:T(8,128)S(1)}, u32[]{:S(2)}, u32[]{:S(2)}) collective-permute-start(f32[32,128]{1,0:T(8,128)S(1)} %get-tuple-element.9), channel_id=1, source_target_pairs={{0,2},{1,3},{2,0},{3,1},{4,12},{5,13},{6,14},{7,15},{8,10},{9,11},... | collective-permute-start | bytes 49160 | tf_op jit(solution)/shard_map/ppermute | solution.py:304
  53.1 2.2 %collective-permute-done.6 = f32[32,128]{1,0:T(8,128)S(1)} collective-permute-done((f32[32,128]{1,0:T(8,128)S(1)}, f32[32,128]{1,0:T(8,128)S(1)}, u32[]{:S(2)}, u32[]{:S(2)}) %collective-permute-start.6) | collective-permute-done | bytes 16416 | tf_op jit(solution)/shard_map/ppermute | solution.py:304
  55.3 1.6 %collective-permute-start.7 = (f32[32,128]{1,0:T(8,128)S(1)}, f32[32,128]{1,0:T(8,128)S(1)}, u32[]{:S(2)}, u32[]{:S(2)}) collective-permute-start(f32[32,128]{1,0:T(8,128)S(1)} %add.19), channel_id=1, source_target_pairs={{0,1},{1,0},{2,3},{3,2},{4,6},{5,7},{6,4},{7,5},{8,9},{9,8},{10,11... | collective-permute-start | bytes 49160 | tf_op jit(solution)/shard_map/ppermute | solution.py:304
  56.9 2.2 %collective-permute-done.7 = f32[32,128]{1,0:T(8,128)S(1)} collective-permute-done((f32[32,128]{1,0:T(8,128)S(1)}, f32[32,128]{1,0:T(8,128)S(1)}, u32[]{:S(2)}, u32[]{:S(2)}) %collective-permute-start.7) | collective-permute-done | bytes 16416 | tf_op jit(solution)/shard_map/ppermute | solution.py:304
  59.1 1.6 %collective-permute-start.8 = (f32[32,128]{1,0:T(8,128)S(1)}, f32[32,128]{1,0:T(8,128)S(1)}, u32[]{:S(2)}, u32[]{:S(2)}) collective-permute-start(f32[32,128]{1,0:T(8,128)S(1)} %add.20), channel_id=1, source_target_pairs={{0,16},{1,17},{2,18},{3,19},{4,5},{5,4},{6,7},{7,6},{8,24},{9,25},... | collective-permute-start | bytes 49160 | tf_op jit(solution)/shard_map/ppermute | solution.py:304
  60.6 2.2 %collective-permute-done.8 = f32[32,128]{1,0:T(8,128)S(1)} collective-permute-done((f32[32,128]{1,0:T(8,128)S(1)}, f32[32,128]{1,0:T(8,128)S(1)}, u32[]{:S(2)}, u32[]{:S(2)}) %collective-permute-start.8) | collective-permute-done | bytes 16416 | tf_op jit(solution)/shard_map/ppermute | solution.py:304
  62.8 1.5 %collective-permute-start.9 = (f32[32,128]{1,0:T(8,128)S(1)}, f32[32,128]{1,0:T(8,128)S(1)}, u32[]{:S(2)}, u32[]{:S(2)}) collective-permute-start(f32[32,128]{1,0:T(8,128)S(1)} %add.21), channel_id=1, source_target_pairs={{0,8},{1,9},{2,10},{3,11},{4,20},{5,21},{6,22},{7,23},{8,0},{9,1},... | collective-permute-start | bytes 49160 | tf_op jit(solution)/shard_map/ppermute | solution.py:304
  64.4 2.2 %collective-permute-done.9 = f32[32,128]{1,0:T(8,128)S(1)} collective-permute-done((f32[32,128]{1,0:T(8,128)S(1)}, f32[32,128]{1,0:T(8,128)S(1)}, u32[]{:S(2)}, u32[]{:S(2)}) %collective-permute-start.9) | collective-permute-done | bytes 16416 | tf_op jit(solution)/shard_map/ppermute | solution.py:304
  66.6 1.2 %collective-permute-done.10 = f32[32,128]{1,0:T(8,128)S(1)} collective-permute-done((f32[32,128]{1,0:T(8,128)S(1)}, f32[32,128]{1,0:T(8,128)S(1)}, u32[]{:S(2)}, u32[]{:S(2)}) %collective-permute-start.10) | collective-permute-done | bytes 16416 | tf_op jit(solution)/shard_map/ppermute | solution.py:308
  67.7 2.6 %lloyd.1 = f32[128,256]{1,0:T(8,128)} custom-call(f32[32,128]{1,0:T(8,128)S(1)} %add.23.count_ref, s32[32,128]{1,0:T(8,128)S(1)} %bitcast.4, s32[16,128]{1,0:T(8,128)S(1)} %get-tuple-element.10.place_ref, s32[32,128]{1,0:T(8,128)S(1)} %get-tuple-element.11.slot_owner_ref, bf16[2048,256]{1,0:T(8,128)(2,1)S(1)} %copy-done, ...), custom_call_target="tpu_custom_call" | custom-call | flops 536870912 | bytes 3203072 | tf_op jit(solution)/shard_map/lloyd/pallas_call | solution.py:39
  (34 shorter events, 5.6 us)
Async XLA Ops:
  2.0 1.0 %copy-start.1 = (bf16[1024,256]{1,0:T(8,128)(2,1)S(1)}, bf16[1024,256]{1,0:T(8,128)(2,1)}, u32[]{:S(2)}) copy-start(bf16[1024,256]{1,0:T(8,128)(2,1)} %points_ref.9) | copy-start | bytes 1572868
  3.7 27.4 %copy-start = (bf16[2048,256]{1,0:T(8,128)(2,1)S(1)}, bf16[2048,256]{1,0:T(8,128)(2,1)}, u32[]{:S(2)}) copy-start(bf16[2048,256]{1,0:T(8,128)(2,1)} %centres_ref.1) | copy-start | bytes 3145732
  3.7 6.3 %collective-permute-start = (bf16[128,256]{1,0:T(8,128)(2,1)S(1)}, bf16[128,256]{1,0:T(8,128)(2,1)S(1)}, u32[]{:S(2)}, u32[]{:S(2)}) collective-permute-start(bf16[128,256]{1,0:T(8,128)(2,1)S(1)} %pick_rows.1), channel_id=1, source_target_pairs={{0,2},{1,3},{2,0},{3,1},{4,12},{5,13},{6,14},{7,15},{8,10},{9,11},... | collective-permute-start | bytes 196616 | tf_op jit(solution)/shard_map/ppermute | solution.py:303
  10.1 5.3 %collective-permute-start.1 = (bf16[256,256]{1,0:T(8,128)(2,1)S(1)}, bf16[256,256]{1,0:T(8,128)(2,1)S(1)}, u32[]{:S(2)}, u32[]{:S(2)}) collective-permute-start(bf16[256,256]{1,0:T(8,128)(2,1)S(1)} %pad_maximum_fusion.2), channel_id=1, source_target_pairs={{0,1},{1,0},{2,3},{3,2},{4,6},{5,7},{6,4},{7,5},{8,9},{9,8},{10,11... | collective-permute-start | bytes 393224 | tf_op jit(solution)/shard_map/ppermute | solution.py:303
  15.4 6.4 %collective-permute-start.2 = (bf16[512,256]{1,0:T(8,128)(2,1)S(1)}, bf16[512,256]{1,0:T(8,128)(2,1)S(1)}, u32[]{:S(2)}, u32[]{:S(2)}) collective-permute-start(bf16[512,256]{1,0:T(8,128)(2,1)S(1)} %pad_maximum_fusion.1), channel_id=1, source_target_pairs={{0,16},{1,17},{2,18},{3,19},{4,5},{5,4},{6,7},{7,6},{8,24},{9,25},... | collective-permute-start | bytes 786440 | tf_op jit(solution)/shard_map/ppermute | solution.py:303
  21.9 9.2 %collective-permute-start.4 = (bf16[1024,256]{1,0:T(8,128)(2,1)S(1)}, bf16[1024,256]{1,0:T(8,128)(2,1)S(1)}, u32[]{:S(2)}, u32[]{:S(2)}) collective-permute-start(bf16[1024,256]{1,0:T(8,128)(2,1)S(1)} %pad_maximum_fusion.refs_0_), channel_id=1, source_target_pairs={{0,8},{1,9},{2,10},{3,11},{4,20},{5,21},{6,22},{7,23},{8,0},{9,1},... | collective-permute-start | bytes 1572872 | tf_op jit(solution)/shard_map/ppermute | solution.py:303
  23.8 11.2 %collective-permute-start.3 = (bf16[1024,256]{1,0:T(8,128)(2,1)S(1)}, bf16[1024,256]{1,0:T(8,128)(2,1)S(1)}, u32[]{:S(2)}, u32[]{:S(2)}) collective-permute-start(bf16[1024,256]{1,0:T(8,128)(2,1)S(1)} %pad_maximum_fusion.refs_0_), channel_id=1, source_target_pairs={{0,4},{1,5},{2,6},{3,7},{4,0},{5,1},{6,2},{7,3},{8,12},{9,13},{10,... | collective-permute-start | bytes 1572872 | tf_op jit(solution)/shard_map/ppermute | solution.py:309
  31.1 8.1 %collective-permute-start.5 = (bf16[1024,256]{1,0:T(8,128)(2,1)S(1)}, bf16[1024,256]{1,0:T(8,128)(2,1)S(1)}, u32[]{:S(2)}, u32[]{:S(2)}) collective-permute-start(bf16[1024,256]{1,0:T(8,128)(2,1)S(1)} %collective-permute-done.4.refs_0_.refs_1_), channel_id=1, source_target_pairs={{0,4},{1,5},{2,6},{3,7},{4,0},{5,1},{6,2},{7,3},{8,12},{9,13},{10,... | collective-permute-start | bytes 1572872 | tf_op jit(solution)/shard_map/ppermute | solution.py:310
  31.1 1.0 %copy-start.2 = (bf16[1024,256]{1,0:T(8,128)(2,1)S(1)}, bf16[1024,256]{1,0:T(8,128)(2,1)}, u32[]{:S(2)}) copy-start(bf16[1024,256]{1,0:T(8,128)(2,1)} %points_ref.9) | copy-start | bytes 1572868
  41.8 6.7 %copy-start.5 = (s32[32]{0:T(128)S(1)}, s32[32]{0:T(128)}, u32[]{:S(2)}) copy-start(s32[32]{0:T(128)} %constant.24.clone) | copy-start | bytes 388
  41.8 6.7 %copy-start.6 = (s32[32]{0:T(128)S(1)}, s32[32]{0:T(128)}, u32[]{:S(2)}) copy-start(s32[32]{0:T(128)} %constant.25.clone) | copy-start | bytes 388
  41.8 28.6 %all-to-all-start = ((f32[32,8,128]{2,1,0:T(8,128)}), f32[32,8,128]{2,1,0:T(8,128)S(1)}, u32[]{:S(2)}, u32[]{:S(2)}) async-start(f32[32,8,128]{2,1,0:T(8,128)} %get-tuple-element.8), calls=%async_computation | async-start | bytes 262144 | tf_op jit(solution)/shard_map/all_to_all | solution.py:315
  48.5 0.7 %copy-start.3 = (s32[4096,1]{0,1:T(1,128)S(1)}, s32[4096,1]{0,1:T(1,128)}, u32[]{:S(2)}) copy-start(s32[4096,1]{0,1:T(1,128)} %param.11) | copy-start | bytes 49156
  48.5 0.7 copy-start.4
  50.4 4.9 %collective-permute-start.6 = (f32[32,128]{1,0:T(8,128)S(1)}, f32[32,128]{1,0:T(8,128)S(1)}, u32[]{:S(2)}, u32[]{:S(2)}) collective-permute-start(f32[32,128]{1,0:T(8,128)S(1)} %get-tuple-element.9), channel_id=1, source_target_pairs={{0,2},{1,3},{2,0},{3,1},{4,12},{5,13},{6,14},{7,15},{8,10},{9,11},... | collective-permute-start | bytes 49160 | tf_op jit(solution)/shard_map/ppermute | solution.py:304
  55.3 3.7 %collective-permute-start.7 = (f32[32,128]{1,0:T(8,128)S(1)}, f32[32,128]{1,0:T(8,128)S(1)}, u32[]{:S(2)}, u32[]{:S(2)}) collective-permute-start(f32[32,128]{1,0:T(8,128)S(1)} %add.19), channel_id=1, source_target_pairs={{0,1},{1,0},{2,3},{3,2},{4,6},{5,7},{6,4},{7,5},{8,9},{9,8},{10,11... | collective-permute-start | bytes 49160 | tf_op jit(solution)/shard_map/ppermute | solution.py:304
  59.1 3.7 %collective-permute-start.8 = (f32[32,128]{1,0:T(8,128)S(1)}, f32[32,128]{1,0:T(8,128)S(1)}, u32[]{:S(2)}, u32[]{:S(2)}) collective-permute-start(f32[32,128]{1,0:T(8,128)S(1)} %add.20), channel_id=1, source_target_pairs={{0,16},{1,17},{2,18},{3,19},{4,5},{5,4},{6,7},{7,6},{8,24},{9,25},... | collective-permute-start | bytes 49160 | tf_op jit(solution)/shard_map/ppermute | solution.py:304
  62.8 3.7 %collective-permute-start.9 = (f32[32,128]{1,0:T(8,128)S(1)}, f32[32,128]{1,0:T(8,128)S(1)}, u32[]{:S(2)}, u32[]{:S(2)}) collective-permute-start(f32[32,128]{1,0:T(8,128)S(1)} %add.21), channel_id=1, source_target_pairs={{0,8},{1,9},{2,10},{3,11},{4,20},{5,21},{6,22},{7,23},{8,0},{9,1},... | collective-permute-start | bytes 49160 | tf_op jit(solution)/shard_map/ppermute | solution.py:304
  66.6 1.2 %collective-permute-start.10 = (f32[32,128]{1,0:T(8,128)S(1)}, f32[32,128]{1,0:T(8,128)S(1)}, u32[]{:S(2)}, u32[]{:S(2)}) collective-permute-start(f32[32,128]{1,0:T(8,128)S(1)} %add.22), channel_id=1, source_target_pairs={{0,4},{1,5},{2,6},{3,7},{4,0},{5,1},{6,2},{7,3},{8,12},{9,13},{10,... | collective-permute-start | bytes 49160 | tf_op jit(solution)/shard_map/ppermute | solution.py:308

commit v2 on v1

v2 whole, which is shorter than its diff:
```python
import functools

import jax
import jax.numpy as jnp
from jax import lax
from jax.experimental import pallas as pl
from jax.experimental.pallas import tpu as pltpu
from jax.sharding import PartitionSpec as P

K_FINAL = 1024
AXES = ("row", "col")
LANES = 128
VMEM_LIMIT = 20 * 1024 * 1024
FLOPS_PER_US = 1.0e9
F32 = jnp.float32
BF16 = jnp.bfloat16

CORE = 4
FAN = ((1, 2), (8, 1))
SPREAD = ((8, 16), (16, 2))


def nt_dot(left, right):
    return lax.dot_general(left, right, (((1,), (1,)), ((), ())), preferred_element_type=F32)


def iota(shape, axis):
    return lax.broadcasted_iota(jnp.int32, shape, axis)


def device_index():
    return lax.axis_index("row") * lax.axis_size("col") + lax.axis_index("col")


def whole_spec():
    return pl.BlockSpec(memory_space=pltpu.VMEM)


def local_call(kernel, out_shape, operands, name, cost, after=(), unread=(), scratch=(), vmem=VMEM_LIMIT):
    specs = [whole_spec()] * len(operands) + [pl.BlockSpec(memory_space=pl.ANY)] * len(after)
    operands = list(operands)
    for place in unread:
        specs[place] = pl.BlockSpec(memory_space=pltpu.HBM)
        operands[place] = pltpu.with_memory_space_constraint(operands[place], pltpu.HBM)
    count = len(operands)

    def body(*refs):
        kernel(*refs[:count], *refs[count + len(after) :])

    return pl.pallas_call(
        body,
        out_shape=out_shape,
        in_specs=specs,
        out_specs=jax.tree.map(lambda _: whole_spec(), out_shape),
        scratch_shapes=list(scratch),
        compiler_params=pltpu.CompilerParams(vmem_limit_bytes=vmem),
        cost_estimate=pl.CostEstimate(flops=int(cost * FLOPS_PER_US), bytes_accessed=0, transcendentals=0),
        name=name,
    )(*operands, *after)


def chunk_rows(ref):
    rounds, samples = ref.shape
    return jnp.concatenate(
        [ref[r : r + 1, k : k + LANES] for r in range(rounds) for k in range(0, samples, LANES)], axis=0
    )


FAR = 2.0**64


def pick_kernel(cap, slots, picks_hbm, points_hbm, assign_hbm, out_ref, picks_ref, points_ref, assign_ref, sems):
    picks_copy = pltpu.make_async_copy(picks_hbm, picks_ref, sems.at[0])
    assign_copy = pltpu.make_async_copy(assign_hbm, assign_ref, sems.at[1])
    points_copy = pltpu.make_async_copy(points_hbm, points_ref, sems.at[2])
    picks_copy.start()
    assign_copy.start()
    points_copy.start()
    picks_copy.wait()
    rounds = picks_ref.shape[0]
    per_round = picks_ref.shape[1] // LANES
    chunks = rounds * per_round
    point_count = points_ref.shape[0]
    local = chunk_rows(picks_ref) - device_index() * point_count
    owned = (local >= 0) & (local < point_count)
    flags = owned.astype(F32).astype(BF16)
    lower = (iota((LANES, LANES), 0) <= iota((LANES, LANES), 1)).astype(F32).astype(BF16)
    inside = jnp.dot(flags, lower, preferred_element_type=F32)
    sums = jnp.dot(flags, jnp.ones((LANES, LANES), BF16), preferred_element_type=F32)
    first, second = iota((chunks, chunks), 0), iota((chunks, chunks), 1)
    same = lax.div(first, per_round) == lax.div(second, per_round)
    earlier = (same & (second < first)).astype(F32).astype(BF16)
    before = jnp.dot(earlier, sums.astype(BF16), preferred_element_type=F32)
    round_of = lax.div(iota((chunks, LANES), 0), per_round)
    slot = (inside + before).astype(jnp.int32) - 1 + round_of * cap
    slot = jnp.where(owned, slot, -1)
    slot_ids = iota((slots, LANES), 0)
    found = jnp.zeros((slots, LANES), jnp.int32)
    for t in range(chunks):
        found = found + jnp.where(slot[t : t + 1, :] == slot_ids, local[t : t + 1, :] + 1, 0)
    place = jnp.sum(found.astype(F32), axis=1, keepdims=True).astype(jnp.int32)
    chosen = (iota((slots, point_count), 1) + 1 == place).astype(F32).astype(BF16)
    assign_copy.wait()
    ids = assign_ref[...]
    ids = jnp.concatenate([lax.div(ids, LANES), lax.rem(ids, LANES)], axis=1).astype(F32)
    spare = jnp.zeros((out_ref.shape[0] - slots - ids.shape[0], ids.shape[1]), F32)
    points_copy.wait()
    rows = jnp.dot(chosen, points_ref[...], preferred_element_type=F32)
    rows = jnp.where(place > 0, rows, FAR)
    out_ref[...] = jnp.concatenate([rows, ids, spare], axis=0).astype(BF16)


def add_tally(count, piece_ref, slots, id_rows):
    block_rows = slots + -(-id_rows // 16) * 16
    cand_chunks = count.shape[0]
    lane_rows = iota((LANES, LANES), 0).astype(F32)
    chunk_ids = iota((cand_chunks, LANES), 0).astype(F32)
    for start in range(slots, piece_ref.shape[0], block_rows):
        ids = piece_ref[start : start + block_rows - slots, :].astype(F32)
        high = [(ids[t : t + 1, :LANES] == chunk_ids).astype(F32) for t in range(id_rows)]
        low = [(ids[t : t + 1, LANES:] == lane_rows).astype(F32) for t in range(id_rows)]
        high = jnp.concatenate(high, axis=1).astype(BF16)
        low = jnp.concatenate(low, axis=1).astype(BF16)
        count = count + nt_dot(high, low)
    return count


def tally_kernel(slots, id_rows, piece_ref, count_ref):
    count_ref[...] = add_tally(jnp.zeros(count_ref.shape, F32), piece_ref, slots, id_rows)


def holders_in_order(doubling, device_ids):
    if not doubling:
        return device_ids
    me = device_index()
    core = lax.rem(lax.div(me, CORE), 2)
    other = lax.div(device_ids, 16)
    kind = core ^ other
    mask = other * CORE
    for bit, masks in enumerate((*zip(*FAN), *zip(*SPREAD))):
        present = lax.rem(lax.div(device_ids, 1 << bit), 2)
        mask = mask ^ (present * jnp.where(kind == 0, masks[0], masks[1]))
    return me ^ mask


def slot_kernel(doubling, cap, slots, device_count, point_count, picks_ref, owner_ref, start_ref, place_ref, slot_owner_ref, token_ref):
    token_ref[...] = start_ref[...]
    picks = chunk_rows(picks_ref)
    chunks = picks.shape[0]
    rounds = picks_ref.shape[0]
    per_round = chunks // rounds
    cand_chunks = owner_ref.shape[0]
    slot_chunks = slot_owner_ref.shape[0]
    lane_rows = iota((LANES, LANES), 0)
    lower = (lane_rows <= iota((LANES, LANES), 1)).astype(F32).astype(BF16)
    ones = jnp.ones((LANES, LANES), BF16)
    device_ids = iota((device_count, LANES), 0)
    first_chunk = cand_chunks - chunks
    holders = holders_in_order(doubling, device_ids)
    owners = jnp.zeros((2 * slot_chunks, LANES), F32)
    for r in range(rounds):
        carry = jnp.zeros((device_count, LANES), F32)
        for u in range(per_round):
            t = r * per_round + u
            holder = lax.div(picks[t : t + 1, :], point_count)
            held = (holder == device_ids).astype(F32)
            running = jnp.dot(held.astype(BF16), lower, preferred_element_type=F32) + carry
            carry = carry + jnp.dot(held.astype(BF16), ones, preferred_element_type=F32)
            rank = jnp.sum(held * running, axis=0, keepdims=True).astype(jnp.int32) - 1
            block = jnp.sum(jnp.where(holders == holder, device_ids, 0), axis=0, keepdims=True)
            place = block * slots + r * cap + rank
            place_ref[t : t + 1, :] = place
            high = lax.div(place, LANES) == iota((slot_chunks, LANES), 0)
            low = (lax.rem(place, LANES) == lane_rows).astype(F32).astype(BF16)
            tag = owner_ref[first_chunk + t : first_chunk + t + 1, :] + 1
            coarse = jnp.where(high, lax.div(tag, 32).astype(F32), 0.0)
            fine = jnp.where(high, lax.rem(tag, 32).astype(F32), 0.0)
            owners = owners + nt_dot(jnp.concatenate([coarse, fine], axis=0).astype(BF16), low)
    slot_owner_ref[...] = (owners[:slot_chunks] * 32.0 + owners[slot_chunks:]).astype(jnp.int32) - 1


def scan_rows(points, piece, best):
    wide = piece.astype(F32)
    half = 0.5 * jnp.sum(wide * wide, axis=1, keepdims=True)
    score = nt_dot(piece, points) - half
    for k in range(0, piece.shape[0], 8):
        best = jnp.maximum(best, score[k : k + 8, :])
    return best


def slot_rows(piece_ref, slots, block_rows):
    return [piece_ref[k : k + slots, :] for k in range(0, piece_ref.shape[0], block_rows)]


def scan_table(points_ref, table_ref, best):
    points = points_ref[...]
    rows = table_ref.shape[0]
    step = min(256, rows)
    if rows <= 4096:
        for start in range(0, rows, step):
            best = scan_rows(points, table_ref[start : start + step, :], best)
        return best

    def visit(i, best):
        return scan_rows(points, table_ref[pl.ds(pl.multiple_of(i * step, step), step), :], best)

    return lax.fori_loop(0, rows // step, visit, best)


def scan_pieces(points_ref, piece_refs, best, slots, block_rows):
    points = points_ref[...]
    for piece_ref in piece_refs:
        blocks = slot_rows(piece_ref, slots, block_rows)
        for k in range(0, len(blocks), 2):
            best = scan_rows(points, jnp.concatenate(blocks[k : k + 2], axis=0), best)
    return best


def first_scan_kernel(points_ref, centres_ref, best_ref, norm_ref, token_ref):
    token_ref[...] = jnp.zeros(token_ref.shape, F32)
    best_ref[...] = scan_table(points_ref, centres_ref, jnp.full(best_ref.shape, -jnp.inf, F32))
    wide = points_ref[...].astype(F32)
    square = wide * wide
    top = square.astype(BF16)
    rest = (square - top.astype(F32)).astype(BF16)
    ones = jnp.ones((8, square.shape[1]), BF16)
    norm_ref[...] = nt_dot(ones, top) + nt_dot(ones, rest)


def next_scan_kernel(slots, block_rows, id_rows, points_ref, best_ref, count_ref, *refs):
    next_ref, next_count_ref, token_ref = refs[-3:]
    token_ref[...] = jnp.zeros(token_ref.shape, F32)
    next_ref[...] = scan_pieces(points_ref, refs[:-3], best_ref[...], slots, block_rows)
    count = count_ref[...]
    if id_rows:
        for piece_ref in refs[:-3]:
            count = add_tally(count, piece_ref, slots, id_rows)
    next_count_ref[...] = count


def last_scan_kernel(slots, block_rows, points_ref, best_ref, norm_ref, piece_ref, near_ref, share_ref):
    if block_rows:
        best = scan_pieces(points_ref, [piece_ref], best_ref[...], slots, block_rows)
    else:
        best = scan_table(points_ref, piece_ref, best_ref[...])
    near = jnp.maximum(norm_ref[0:1, :] - 2.0 * jnp.max(best, axis=0, keepdims=True), 0.0)
    near_ref[...] = near
    share_ref[...] = jnp.broadcast_to(jnp.sum(near, axis=1, keepdims=True)[None], share_ref.shape)


def lloyd_kernel(slots, block_rows, id_rows, count_ref, owner_ref, place_ref, slot_owner_ref, centres_ref, *refs):
    piece_refs, out_ref = refs[:-1], refs[-1]
    finals = out_ref.shape[0]
    slot_chunks = slot_owner_ref.shape[0]
    chunks = place_ref.shape[0]
    first_chunks = owner_ref.shape[0] - chunks
    count = count_ref[...]
    for k in id_rows:
        count = add_tally(count, piece_refs[k], slots, id_rows[k])
    weights = 1.0 + count
    weight_top = weights.astype(BF16).astype(F32)
    weight_rest = (weights - weight_top).astype(BF16).astype(F32)
    lane_rows = iota((LANES, LANES), 0)
    placed = jnp.zeros((2 * slot_chunks, LANES), F32)
    for t in range(chunks):
        place = place_ref[t : t + 1, :]
        high = lax.div(place, LANES) == iota((slot_chunks, LANES), 0)
        low = (lax.rem(place, LANES) == lane_rows).astype(F32).astype(BF16)
        c = first_chunks + t
        both = [jnp.where(high, w[c : c + 1, :], 0.0) for w in (weight_top, weight_rest)]
        placed = placed + nt_dot(jnp.concatenate(both, axis=0).astype(BF16), low)
    targets = iota((finals, LANES), 0) + lax.axis_index("row") * finals

    def members(owners, tops, rests, mass):
        parts = []
        for b in range(owners.shape[0]):
            mine = owners[b : b + 1, :] == targets
            top = jnp.where(mine, tops[b : b + 1, :], 0.0)
            rest = jnp.where(mine, rests[b : b + 1, :], 0.0)
            mass = mass + (top + rest)
            parts.append(jnp.concatenate([top, rest], axis=0).astype(BF16))
        return jnp.concatenate(parts, axis=1), mass

    mass = jnp.zeros((finals, LANES), F32)
    member, mass = members(owner_ref[:first_chunks, :], weight_top[:first_chunks], weight_rest[:first_chunks], mass)
    total = jnp.dot(member, centres_ref[...], preferred_element_type=F32)
    start = 0
    for piece_ref in piece_refs:
        rows = jnp.concatenate(slot_rows(piece_ref, slots, block_rows), axis=0) if block_rows else piece_ref[...]
        stop = start + rows.shape[0] // LANES
        member, mass = members(
            slot_owner_ref[start:stop, :], placed[start:stop], placed[slot_chunks + start : slot_chunks + stop], mass
        )
        total = total + jnp.dot(member, rows, preferred_element_type=F32)
        start = stop
    out_ref[...] = (total[:finals] + total[finals:]) / jnp.sum(mass, axis=1, keepdims=True)


def finish_kernel(total_points, near_ref, share_ref, relative_ref):
    cost = jnp.sum(share_ref[...], axis=0)[0:1, 0:1]
    relative_ref[...] = near_ref[...] * total_points / cost


def permute(value, masks):
    pairs = [(d, d ^ masks[(d // CORE) % 2]) for d in range(lax.axis_size(AXES))]
    return lax.ppermute(value, AXES, pairs)


def hop(index):
    masks = tuple(zip(*FAN)) + tuple(zip(*SPREAD))
    return masks[index]


def done_after(value, *tokens):
    ready = tokens[0] >= 0.0
    for token in tokens[1:]:
        ready = ready & (token >= 0.0)
    return jnp.where(ready[:, : value.shape[1]], value, jnp.zeros_like(value))


def both_hops(first, second):
    return tuple(a ^ b for a, b in zip(first, second))


def shards(points, centres, picks, assign_pts, cand_assign):
    point_count, feature_count = points.shape
    row_count, col_count = lax.axis_size("row"), lax.axis_size("col")
    device_count = row_count * col_count
    doubling = (row_count, col_count) == (8, 4)
    round_count, sample_count = picks.shape
    cand_count = centres.shape[0] + round_count * sample_count
    cap = min(point_count, sample_count, -(-2 * sample_count // device_count))
    slots = -(-round_count * cap // 16) * 16
    slot_chunks = device_count * slots // LANES
    chunks = round_count * sample_count // LANES
    finals = K_FINAL // row_count
    shape = jax.ShapeDtypeStruct

    token = shape((1, feature_count), F32)
    id_rows = point_count // LANES
    block_rows = slots + -(-id_rows // 16) * 16
    block = local_call(
        functools.partial(pick_kernel, cap, slots),
        shape((block_rows, feature_count), BF16),
        (picks, points, assign_pts.reshape(id_rows, LANES)),
        "pick_rows",
        0.8,
        unread=(0, 1, 2),
        scratch=(
            pltpu.VMEM(picks.shape, jnp.int32),
            pltpu.VMEM(points.shape, BF16),
            pltpu.VMEM((id_rows, LANES), jnp.int32),
            pltpu.SemaphoreType.DMA((3,)),
        ),
    )
    count_shape = shape((cand_count // LANES, LANES), F32)
    owner_rows = cand_assign.reshape(-1, LANES)

    def find_slots(start):
        results = (shape((chunks, LANES), jnp.int32), shape((slot_chunks, LANES), jnp.int32), token)
        kernel = functools.partial(slot_kernel, doubling, cap, slots, device_count, point_count)
        return local_call(kernel, results, (picks, owner_rows, start), "slot_owners", 1.0)

    best_shape = shape((8, point_count), F32)

    best, norms, scanned = local_call(
        first_scan_kernel, (best_shape, best_shape, token), (points, centres), "scan_centres", 1.6
    )

    def next_scan(best, counts, tallied, *pieces):
        cost = 0.1 + 0.8e-3 * sum(p.shape[0] for p in pieces)
        kernel = functools.partial(next_scan_kernel, slots, block_rows, id_rows if tallied else 0)
        results = (best_shape, count_shape, token)
        return local_call(kernel, results, (points, best, counts, *pieces), "scan_sampled", cost)

    def last_scan(best, piece, split):
        cost = 0.5 + 0.8e-3 * piece.shape[0]
        kernel = functools.partial(last_scan_kernel, slots, block_rows if split else 0)
        results = (shape((1, point_count), F32), shape((device_count, 1, LANES), F32))
        return local_call(kernel, results, (points, best, norms, piece), "scan_last", cost)

    if doubling:
        swap = (CORE, CORE)
        near = [block, *(permute(block, m) for m in (hop(0), hop(1), both_hops(hop(0), hop(1))))]
        own = done_after(jnp.concatenate(near, axis=0), scanned)
        first = permute(own, hop(2))
        second = permute(own, hop(3))
        swapped = [permute(own, swap)]
        places, slot_owners, found = find_slots(scanned)
        counts = jnp.zeros(count_shape.shape, F32)
        best, counts, scanned = next_scan(best, counts, True, own, swapped[0])
        third = permute(done_after(first, scanned, found), hop(3))
        swapped += [permute(first, swap), permute(second, swap)]
        best, counts, scanned = next_scan(best, counts, True, first, second, swapped[1], swapped[2])
        swapped.append(permute(done_after(third, scanned), swap))
        best, counts, scanned = next_scan(best, counts, False, third)
        near, share = last_scan(best, swapped[3], True)
        shares = lax.all_to_all(share, AXES, 0, 0)
        pieces = (own, first, second, third, *swapped)
        untold = {3: id_rows, 7: id_rows}
    else:
        places, slot_owners, found = find_slots(scanned)
        counts = local_call(
            functools.partial(tally_kernel, slots, id_rows), count_shape, (block,), "tally", 0.3
        )
        counts = lax.psum(counts, AXES)
        pieces = (lax.all_gather(block[:slots], AXES, tiled=True),)
        near, share = last_scan(best, pieces[0], False)
        shares = lax.psum(share[:1], AXES)
        untold = {}
    new_centres = local_call(
        functools.partial(lloyd_kernel, slots, block_rows if doubling else 0, untold),
        shape((finals, feature_count), F32),
        (counts, owner_rows, places, slot_owners, centres, *pieces),
        "lloyd",
        2.6,
    )
    relative = local_call(
        functools.partial(finish_kernel, float(point_count * device_count)),
        shape((1, point_count), F32),
        (near, shares),
        "finish",
        0.6,
    )
    return (relative.reshape(-1), new_centres)


def solution(mesh):
    placed = (P(AXES, None), P(), P(), P(AXES), P())
    return jax.shard_map(
        shards,
        mesh=mesh,
        in_specs=placed,
        out_specs=(P(AXES), P("row", None)),
        check_vma=False,
    )
```

time: 71.5 us -> 46.5 us (0.65)
  waiting for transfers between devices: 27.2 us -> 13.6 us
  starting transfers between devices: 24 us -> 17.3 us
  local copies, waits for them, and re-layouts: 4.19 us -> 0.02 us
    ppermute x11 -> x10, waiting for transfers between devices: 27.2 us -> 10.1 us  [permute(): return lax.ppermute(value, AXES, pairs)]
    all_to_all x1, starting transfers between devices: 6.65 us -> 3.07 us  [shards(): shares = lax.all_to_all(share, AXES, 0, 0)]
    all_to_all x1, waiting for transfers between devices: 0.01 us -> 3.52 us  [shards(): shares = lax.all_to_all(share, AXES, 0, 0)]
    ppermute x11 -> x10, starting transfers between devices: 17.4 us -> 14.3 us  [permute(): return lax.ppermute(value, AXES, pairs)]
    unnamed x14 -> x8, local copies, waits for them, and re-layouts: 2.72 us -> 0.02 us
    pallas_call x8 -> x9, Pallas kernels: 14.7 us -> 14.4 us  [local_call(): pl.pallas_call(body, out_shape=out_shape, in_specs=specs, out_specs=jax.t...]
  transfers between devices with their start and end apart: 12 -> 11, of which waited for: 9 -> 6; matrix products, arithmetic and copies ran while one was open for 0% -> 0% of each run, Pallas kernels for 15% -> 24%
where the time goes in v2:
time: 46.5 us; the launch traced here: 46.3 us
  starting transfers between devices  17.3 us (37%)
  Pallas kernels  14.4 us (31%)
  waiting for transfers between devices  13.6 us (29%)
  between operations  0.73 us (2%)
    pallas_call x9, Pallas kernels, local_call(): pl.pallas_call(body, out_shape=out_shape, in_specs=specs, out_specs=jax.t...  14.4 us
    ppermute x10, starting transfers between devices, permute(): return lax.ppermute(value, AXES, pairs)  14.3 us
    ppermute x10, waiting for transfers between devices, permute(): return lax.ppermute(value, AXES, pairs)  10.1 us
    all_to_all x1, waiting for transfers between devices, shards(): shares = lax.all_to_all(share, AXES, 0, 0)  3.52 us
    all_to_all x1, starting transfers between devices, shards(): shares = lax.all_to_all(share, AXES, 0, 0)  3.07 us
  transfers between devices with their start and end apart: 11, of which 6 were waited for; matrix products, arithmetic and copies ran while one was open for 0% of the time, Pallas kernels for 24%

profile of v2, /device:TPU:0, one launch (start us, length us, event | category | flops | bytes accessed | tf_op | source)
XLA Modules:
  0.0 46.3 jit_solution(12651847851529163602)
XLA Ops:
  0.6 1.6 %pick_rows.1 = bf16[144,256]{1,0:T(8,128)(2,1)S(1)} custom-call(s32[2,1024]{1,0:T(2,128)} %refs_0_.11, bf16[1024,256]{1,0:T(8,128)(2,1)} %refs_0_.13, s32[8,128]{1,0:T(8,128)} %bitcast.5), custom_call_target="tpu_custom_call" | custom-call | flops 800000000 | tf_op jit(solution)/shard_map/pick_rows/pallas_call | solution.py:50
  2.2 5.1 %collective-permute-start.2 = (bf16[144,256]{1,0:T(8,128)(2,1)S(1)}, bf16[144,256]{1,0:T(8,128)(2,1)S(1)}, u32[]{:S(2)}, u32[]{:S(2)}) collective-permute-start(bf16[144,256]{1,0:T(8,128)(2,1)S(1)} %pick_rows.1), channel_id=1, source_target_pairs={{0,3},{1,2},{2,1},{3,0},{4,13},{5,12},{6,15},{7,14},{8,11},{9,10},... | collective-permute-start | bytes 221192 | tf_op jit(solution)/shard_map/ppermute | solution.py:306
  7.3 0.6 %collective-permute-start = (bf16[144,256]{1,0:T(8,128)(2,1)S(1)}, bf16[144,256]{1,0:T(8,128)(2,1)S(1)}, u32[]{:S(2)}, u32[]{:S(2)}) collective-permute-start(bf16[144,256]{1,0:T(8,128)(2,1)S(1)} %pick_rows.1), channel_id=1, source_target_pairs={{0,1},{1,0},{2,3},{3,2},{4,12},{5,13},{6,14},{7,15},{8,9},{9,8},{1... | collective-permute-start | bytes 221192 | tf_op jit(solution)/shard_map/ppermute | solution.py:306
  8.0 1.7 %scan_centres.1 = (f32[8,1024]{1,0:T(8,128)S(1)}, f32[8,1024]{1,0:T(8,128)S(1)}, f32[1,256]{1,0:T(1,128)S(1)}) custom-call(bf16[1024,256]{1,0:T(8,128)(2,1)S(1)} %copy-done.1, bf16[2048,256]{1,0:T(8,128)(2,1)S(1)} %copy-done), custom_call_target="tpu_custom_call" | custom-call | flops 1600000000 | tf_op jit(solution)/shard_map/scan_centres/pallas_call | solution.py:50
  9.8 0.5 %collective-permute-done.2 = bf16[144,256]{1,0:T(8,128)(2,1)S(1)} collective-permute-done((bf16[144,256]{1,0:T(8,128)(2,1)S(1)}, bf16[144,256]{1,0:T(8,128)(2,1)S(1)}, u32[]{:S(2)}, u32[]{:S(2)}) %collective-permute-start.2) | collective-permute-done | bytes 73760 | tf_op jit(solution)/shard_map/ppermute | solution.py:306
  10.2 2.6 %collective-permute-done.1 = bf16[144,256]{1,0:T(8,128)(2,1)S(1)} collective-permute-done((bf16[144,256]{1,0:T(8,128)(2,1)S(1)}, bf16[144,256]{1,0:T(8,128)(2,1)S(1)}, u32[]{:S(2)}, u32[]{:S(2)}) %collective-permute-start.1) | collective-permute-done | bytes 73760 | tf_op jit(solution)/shard_map/ppermute | solution.py:306
  12.8 0.1 maximum_select_fusion.refs_3_.refs_5_
  12.9 1.7 %collective-permute-start.5 = (bf16[576,256]{1,0:T(8,128)(2,1)S(1)}, bf16[576,256]{1,0:T(8,128)(2,1)S(1)}, u32[]{:S(2)}, u32[]{:S(2)}) collective-permute-start(bf16[576,256]{1,0:T(8,128)(2,1)S(1)} %maximum_select_fusion.refs_3_.refs_5_), channel_id=1, source_target_pairs={{0,16},{1,17},{2,18},{3,19},{4,6},{5,7},{6,4},{7,5},{8,24},{9,25},... | collective-permute-start | bytes 884744 | tf_op jit(solution)/shard_map/ppermute | solution.py:306
  14.5 1.5 %collective-permute-start.4 = (bf16[576,256]{1,0:T(8,128)(2,1)S(1)}, bf16[576,256]{1,0:T(8,128)(2,1)S(1)}, u32[]{:S(2)}, u32[]{:S(2)}) collective-permute-start(bf16[576,256]{1,0:T(8,128)(2,1)S(1)} %maximum_select_fusion.refs_3_.refs_5_), channel_id=1, source_target_pairs={{0,8},{1,9},{2,10},{3,11},{4,20},{5,21},{6,22},{7,23},{8,0},{9,1},... | collective-permute-start | bytes 884744 | tf_op jit(solution)/shard_map/ppermute | solution.py:306
  16.1 1.0 %slot_owners.1 = (s32[16,128]{1,0:T(8,128)S(1)}, s32[32,128]{1,0:T(8,128)S(1)}, f32[1,256]{1,0:T(1,128)S(1)}) custom-call(s32[2,1024]{1,0:T(2,128)S(1)} %copy-done.3, s32[32,128]{1,0:T(8,128)S(1)} %bitcast.3, f32[1,256]{1,0:T(1,128)S(1)} %get-tuple-element.19.refs_2_), custom_call_target="tpu_custom_call" | custom-call | flops 1000000000 | tf_op jit(solution)/shard_map/slot_owners/pallas_call | solution.py:50
  17.1 4.2 %collective-permute-done.5.refs_4_.refs_7_ = bf16[576,256]{1,0:T(8,128)(2,1)S(1)} collective-permute-done((bf16[576,256]{1,0:T(8,128)(2,1)S(1)}, bf16[576,256]{1,0:T(8,128)(2,1)S(1)}, u32[]{:S(2)}, u32[]{:S(2)}) %collective-permute-start.5) | collective-permute-done | bytes 294944 | tf_op jit(solution)/shard_map/ppermute | solution.py:306
  21.3 0.5 %collective-permute-start.6 = (bf16[576,256]{1,0:T(8,128)(2,1)S(1)}, bf16[576,256]{1,0:T(8,128)(2,1)S(1)}, u32[]{:S(2)}, u32[]{:S(2)}) collective-permute-start(bf16[576,256]{1,0:T(8,128)(2,1)S(1)} %collective-permute-done.4.refs_3_.refs_6_), channel_id=1, source_target_pairs={{0,4},{1,5},{2,6},{3,7},{4,0},{5,1},{6,2},{7,3},{8,12},{9,13},{10,... | collective-permute-start | bytes 884744 | tf_op jit(solution)/shard_map/ppermute | solution.py:306
  21.8 1.3 %scan_sampled.3 = (f32[8,1024]{1,0:T(8,128)S(1)}, f32[32,128]{1,0:T(8,128)S(1)}, f32[1,256]{1,0:T(1,128)S(1)}) custom-call(bf16[1024,256]{1,0:T(8,128)(2,1)S(1)} %copy-done.1, f32[8,1024]{1,0:T(8,128)S(1)} %get-tuple-element.18.refs_1_, f32[32,128]{1,0:T(8,128)S(1)} %broadcast_in_dim.27.refs_2_, bf16[576,256]{1,0:T(8,128)(2,1)S(1)} %maximum_select_fusion.refs_3_.refs_5_, ...), custom_call_target="tpu_custom_call" | custom-call | flops 1021600000 | tf_op jit(solution)/shard_map/scan_sampled/pallas_call | solution.py:50
  23.2 1.8 %collective-permute-start.8 = (bf16[576,256]{1,0:T(8,128)(2,1)S(1)}, bf16[576,256]{1,0:T(8,128)(2,1)S(1)}, u32[]{:S(2)}, u32[]{:S(2)}) collective-permute-start(bf16[576,256]{1,0:T(8,128)(2,1)S(1)} %broadcast_select_fusion.1), channel_id=1, source_target_pairs={{0,16},{1,17},{2,18},{3,19},{4,6},{5,7},{6,4},{7,5},{8,24},{9,25},... | collective-permute-start | bytes 884744 | tf_op jit(solution)/shard_map/ppermute | solution.py:306
  25.0 2.4 %scan_sampled.4 = (f32[8,1024]{1,0:T(8,128)S(1)}, f32[32,128]{1,0:T(8,128)S(1)}, f32[1,256]{1,0:T(1,128)S(1)}) custom-call(bf16[1024,256]{1,0:T(8,128)(2,1)S(1)} %copy-done.1, f32[8,1024]{1,0:T(8,128)S(1)} %get-tuple-element.20.refs_1_, f32[32,128]{1,0:T(8,128)S(1)} %get-tuple-element.21.refs_2_, ...), custom_call_target="tpu_custom_call" | custom-call | flops 1943200000 | tf_op jit(solution)/shard_map/scan_sampled/pallas_call | solution.py:50
  27.4 2.6 %collective-permute-done.8.refs_3_.refs_8_ = bf16[576,256]{1,0:T(8,128)(2,1)S(1)} collective-permute-done((bf16[576,256]{1,0:T(8,128)(2,1)S(1)}, bf16[576,256]{1,0:T(8,128)(2,1)S(1)}, u32[]{:S(2)}, u32[]{:S(2)}) %collective-permute-start.8) | collective-permute-done | bytes 294944 | tf_op jit(solution)/shard_map/ppermute | solution.py:306
  30.0 3.0 %collective-permute-start.9 = (bf16[576,256]{1,0:T(8,128)(2,1)S(1)}, bf16[576,256]{1,0:T(8,128)(2,1)S(1)}, u32[]{:S(2)}, u32[]{:S(2)}) collective-permute-start(bf16[576,256]{1,0:T(8,128)(2,1)S(1)} %broadcast_select_fusion), channel_id=1, source_target_pairs={{0,4},{1,5},{2,6},{3,7},{4,0},{5,1},{6,2},{7,3},{8,12},{9,13},{10,... | collective-permute-start | bytes 884744 | tf_op jit(solution)/shard_map/ppermute | solution.py:306
  33.0 1.0 %scan_sampled.5 = (f32[8,1024]{1,0:T(8,128)S(1)}, f32[32,128]{1,0:T(8,128)S(1)}, f32[1,256]{1,0:T(1,128)}) custom-call(bf16[1024,256]{1,0:T(8,128)(2,1)S(1)} %copy-done.1, f32[8,1024]{1,0:T(8,128)S(1)} %get-tuple-element.22.refs_1_, f32[32,128]{1,0:T(8,128)S(1)} %get-tuple-element.23.refs_2_, bf16[576,256]{1,0:T(8,128)(2,1)S(1)} %collective-permute-done.8.refs_3_.refs_8_), custom_call_target="tpu_custom_call" | custom-call | flops 560800000 | tf_op jit(solution)/shard_map/scan_sampled/pallas_call | solution.py:50
  33.9 0.2 collective-permute-done.9.refs_3_.refs_12_
  34.2 1.2 %scan_last.1 = (f32[1,1024]{1,0:T(1,128)S(1)}, f32[32,1,128]{2,1,0:T(1,128)}) custom-call(bf16[1024,256]{1,0:T(8,128)(2,1)S(1)} %copy-done.1, f32[8,1024]{1,0:T(8,128)S(1)} %get-tuple-element.26.refs_1_, f32[8,1024]{1,0:T(8,128)S(1)} %get-tuple-element.27.refs_2_, bf16[576,256]{1,0:T(8,128)(2,1)S(1)} %collective-permute-done.9.refs_3_.refs_12_), custom_call_target="tpu_custom_call" | custom-call | flops 960800000 | tf_op jit(solution)/shard_map/scan_last/pallas_call | solution.py:50
  35.4 3.1 %all-to-all-start = ((f32[32,1,128]{2,1,0:T(1,128)}), f32[32,1,128]{2,1,0:T(1,128)S(1)}, u32[]{:S(2)}, u32[]{:S(2)}) async-start(f32[32,1,128]{2,1,0:T(1,128)} %get-tuple-element.30), calls=%async_computation | async-start | bytes 32768 | tf_op jit(solution)/shard_map/all_to_all | solution.py:398
  38.4 3.7 %lloyd.1 = f32[128,256]{1,0:T(8,128)} custom-call(f32[32,128]{1,0:T(8,128)S(1)} %get-tuple-element.31.refs_0_, s32[32,128]{1,0:T(8,128)S(1)} %bitcast.4, s32[16,128]{1,0:T(8,128)S(1)} %get-tuple-element.32.refs_2_, s32[32,128]{1,0:T(8,128)S(1)} %get-tuple-element.33.refs_3_, bf16[2048,256]{1,0:T(8,128)(2,1)S(1)} %copy-done, ...), custom_call_target="tpu_custom_call" | custom-call | flops 2600000000 | tf_op jit(solution)/shard_map/lloyd/pallas_call | solution.py:50
  42.1 3.5 %all-to-all-done.refs_1_ = f32[32,1,128]{2,1,0:T(1,128)S(1)} async-done(((f32[32,1,128]{2,1,0:T(1,128)}), f32[32,1,128]{2,1,0:T(1,128)S(1)}, u32[]{:S(2)}, u32[]{:S(2)}) %all-to-all-start) | async-done | bytes 16416 | tf_op jit(solution)/shard_map/all_to_all | solution.py:398
  45.6 0.7 %finish.1 = f32[1,1024]{1,0:T(1,128)} custom-call(f32[1,1024]{1,0:T(1,128)S(1)} %get-tuple-element.29.refs_0_, f32[32,1,128]{2,1,0:T(1,128)S(1)} %all-to-all-done.refs_1_), custom_call_target="tpu_custom_call" | custom-call | flops 600000000 | tf_op jit(solution)/shard_map/finish/pallas_call | solution.py:50
  (22 shorter events, 0.2 us)
Async XLA Ops:
  0.6 7.3 %copy-start = (bf16[2048,256]{1,0:T(8,128)(2,1)S(1)}, bf16[2048,256]{1,0:T(8,128)(2,1)}, u32[]{:S(2)}) copy-start(bf16[2048,256]{1,0:T(8,128)(2,1)} %refs_4_.1) | copy-start | bytes 3145732
  0.6 7.3 %copy-start.1 = (bf16[1024,256]{1,0:T(8,128)(2,1)S(1)}, bf16[1024,256]{1,0:T(8,128)(2,1)}, u32[]{:S(2)}) copy-start(bf16[1024,256]{1,0:T(8,128)(2,1)} %refs_0_.13) | copy-start | bytes 1572868
  2.2 8.0 %collective-permute-start.2 = (bf16[144,256]{1,0:T(8,128)(2,1)S(1)}, bf16[144,256]{1,0:T(8,128)(2,1)S(1)}, u32[]{:S(2)}, u32[]{:S(2)}) collective-permute-start(bf16[144,256]{1,0:T(8,128)(2,1)S(1)} %pick_rows.1), channel_id=1, source_target_pairs={{0,3},{1,2},{2,1},{3,0},{4,13},{5,12},{6,15},{7,14},{8,11},{9,10},... | collective-permute-start | bytes 221192 | tf_op jit(solution)/shard_map/ppermute | solution.py:306
  7.3 5.5 %collective-permute-start.1 = (bf16[144,256]{1,0:T(8,128)(2,1)S(1)}, bf16[144,256]{1,0:T(8,128)(2,1)S(1)}, u32[]{:S(2)}, u32[]{:S(2)}) collective-permute-start(bf16[144,256]{1,0:T(8,128)(2,1)S(1)} %pick_rows.1), channel_id=1, source_target_pairs={{0,2},{1,3},{2,0},{3,1},{4,5},{5,4},{6,7},{7,6},{8,10},{9,11},{10,... | collective-permute-start | bytes 221192 | tf_op jit(solution)/shard_map/ppermute | solution.py:306
  7.3 5.5 %collective-permute-start = (bf16[144,256]{1,0:T(8,128)(2,1)S(1)}, bf16[144,256]{1,0:T(8,128)(2,1)S(1)}, u32[]{:S(2)}, u32[]{:S(2)}) collective-permute-start(bf16[144,256]{1,0:T(8,128)(2,1)S(1)} %pick_rows.1), channel_id=1, source_target_pairs={{0,1},{1,0},{2,3},{3,2},{4,12},{5,13},{6,14},{7,15},{8,9},{9,8},{1... | collective-permute-start | bytes 221192 | tf_op jit(solution)/shard_map/ppermute | solution.py:306
  9.7 6.4 %copy-start.2 = (s32[4096,1]{0,1:T(1,128)S(1)}, s32[4096,1]{0,1:T(1,128)}, u32[]{:S(2)}) copy-start(s32[4096,1]{0,1:T(1,128)} %param.9) | copy-start | bytes 49156
  9.7 6.4 %copy-start.3 = (s32[2,1024]{1,0:T(2,128)S(1)}, s32[2,1024]{1,0:T(2,128)}, u32[]{:S(2)}) copy-start(s32[2,1024]{1,0:T(2,128)} %refs_0_.11) | copy-start | bytes 24580
  12.9 8.4 %collective-permute-start.5 = (bf16[576,256]{1,0:T(8,128)(2,1)S(1)}, bf16[576,256]{1,0:T(8,128)(2,1)S(1)}, u32[]{:S(2)}, u32[]{:S(2)}) collective-permute-start(bf16[576,256]{1,0:T(8,128)(2,1)S(1)} %maximum_select_fusion.refs_3_.refs_5_), channel_id=1, source_target_pairs={{0,16},{1,17},{2,18},{3,19},{4,6},{5,7},{6,4},{7,5},{8,24},{9,25},... | collective-permute-start | bytes 884744 | tf_op jit(solution)/shard_map/ppermute | solution.py:306
  14.5 6.7 %collective-permute-start.4 = (bf16[576,256]{1,0:T(8,128)(2,1)S(1)}, bf16[576,256]{1,0:T(8,128)(2,1)S(1)}, u32[]{:S(2)}, u32[]{:S(2)}) collective-permute-start(bf16[576,256]{1,0:T(8,128)(2,1)S(1)} %maximum_select_fusion.refs_3_.refs_5_), channel_id=1, source_target_pairs={{0,8},{1,9},{2,10},{3,11},{4,20},{5,21},{6,22},{7,23},{8,0},{9,1},... | collective-permute-start | bytes 884744 | tf_op jit(solution)/shard_map/ppermute | solution.py:306
  16.1 5.7 %collective-permute-start.3 = (bf16[576,256]{1,0:T(8,128)(2,1)S(1)}, bf16[576,256]{1,0:T(8,128)(2,1)S(1)}, u32[]{:S(2)}, u32[]{:S(2)}) collective-permute-start(bf16[576,256]{1,0:T(8,128)(2,1)S(1)} %maximum_select_fusion.refs_3_.refs_5_), channel_id=1, source_target_pairs={{0,4},{1,5},{2,6},{3,7},{4,0},{5,1},{6,2},{7,3},{8,12},{9,13},{10,... | collective-permute-start | bytes 884744 | tf_op jit(solution)/shard_map/ppermute | solution.py:306
  21.3 3.7 %collective-permute-start.7 = (bf16[576,256]{1,0:T(8,128)(2,1)S(1)}, bf16[576,256]{1,0:T(8,128)(2,1)S(1)}, u32[]{:S(2)}, u32[]{:S(2)}) collective-permute-start(bf16[576,256]{1,0:T(8,128)(2,1)S(1)} %collective-permute-done.5.refs_4_.refs_7_), channel_id=1, source_target_pairs={{0,4},{1,5},{2,6},{3,7},{4,0},{5,1},{6,2},{7,3},{8,12},{9,13},{10,... | collective-permute-start | bytes 884744 | tf_op jit(solution)/shard_map/ppermute | solution.py:306
  21.3 3.7 %collective-permute-start.6 = (bf16[576,256]{1,0:T(8,128)(2,1)S(1)}, bf16[576,256]{1,0:T(8,128)(2,1)S(1)}, u32[]{:S(2)}, u32[]{:S(2)}) collective-permute-start(bf16[576,256]{1,0:T(8,128)(2,1)S(1)} %collective-permute-done.4.refs_3_.refs_6_), channel_id=1, source_target_pairs={{0,4},{1,5},{2,6},{3,7},{4,0},{5,1},{6,2},{7,3},{8,12},{9,13},{10,... | collective-permute-start | bytes 884744 | tf_op jit(solution)/shard_map/ppermute | solution.py:306
  23.2 6.8 %collective-permute-start.8 = (bf16[576,256]{1,0:T(8,128)(2,1)S(1)}, bf16[576,256]{1,0:T(8,128)(2,1)S(1)}, u32[]{:S(2)}, u32[]{:S(2)}) collective-permute-start(bf16[576,256]{1,0:T(8,128)(2,1)S(1)} %broadcast_select_fusion.1), channel_id=1, source_target_pairs={{0,16},{1,17},{2,18},{3,19},{4,6},{5,7},{6,4},{7,5},{8,24},{9,25},... | collective-permute-start | bytes 884744 | tf_op jit(solution)/shard_map/ppermute | solution.py:306
  30.0 4.2 %collective-permute-start.9 = (bf16[576,256]{1,0:T(8,128)(2,1)S(1)}, bf16[576,256]{1,0:T(8,128)(2,1)S(1)}, u32[]{:S(2)}, u32[]{:S(2)}) collective-permute-start(bf16[576,256]{1,0:T(8,128)(2,1)S(1)} %broadcast_select_fusion), channel_id=1, source_target_pairs={{0,4},{1,5},{2,6},{3,7},{4,0},{5,1},{6,2},{7,3},{8,12},{9,13},{10,... | collective-permute-start | bytes 884744 | tf_op jit(solution)/shard_map/ppermute | solution.py:306
  35.4 10.2 %all-to-all-start = ((f32[32,1,128]{2,1,0:T(1,128)}), f32[32,1,128]{2,1,0:T(1,128)S(1)}, u32[]{:S(2)}, u32[]{:S(2)}) async-start(f32[32,1,128]{2,1,0:T(1,128)} %get-tuple-element.30), calls=%async_computation | async-start | bytes 32768 | tf_op jit(solution)/shard_map/all_to_all | solution.py:398

commit v3 on v2

--- a/solution.py
+++ b/solution.py
@@ -17,7 +17,7 @@
 
 CORE = 4
 FAN = ((1, 2), (8, 1))
-SPREAD = ((8, 16), (16, 2))
+SPREAD = ((16, 8), (2, 16))
 
 
 def nt_dot(left, right):
@@ -110,23 +110,23 @@
     out_ref[...] = jnp.concatenate([rows, ids, spare], axis=0).astype(BF16)
 
 
-def add_tally(count, piece_ref, slots, id_rows):
-    block_rows = slots + -(-id_rows // 16) * 16
+def add_tally(count, ids):
     cand_chunks = count.shape[0]
     lane_rows = iota((LANES, LANES), 0).astype(F32)
     chunk_ids = iota((cand_chunks, LANES), 0).astype(F32)
-    for start in range(slots, piece_ref.shape[0], block_rows):
-        ids = piece_ref[start : start + block_rows - slots, :].astype(F32)
-        high = [(ids[t : t + 1, :LANES] == chunk_ids).astype(F32) for t in range(id_rows)]
-        low = [(ids[t : t + 1, LANES:] == lane_rows).astype(F32) for t in range(id_rows)]
+    ids = ids.astype(F32)
+    for start in range(0, ids.shape[0], 8):
+        rows = [ids[t : t + 1, :] for t in range(start, start + 8)]
+        high = [(row[:, :LANES] == chunk_ids).astype(F32) for row in rows]
+        low = [(row[:, LANES:] == lane_rows).astype(F32) for row in rows]
         high = jnp.concatenate(high, axis=1).astype(BF16)
         low = jnp.concatenate(low, axis=1).astype(BF16)
         count = count + nt_dot(high, low)
     return count
 
 
-def tally_kernel(slots, id_rows, piece_ref, count_ref):
-    count_ref[...] = add_tally(jnp.zeros(count_ref.shape, F32), piece_ref, slots, id_rows)
+def tally_kernel(ids_ref, count_ref):
+    count_ref[...] = add_tally(jnp.zeros(count_ref.shape, F32), ids_ref[...])
 
 
 def holders_in_order(doubling, device_ids):
@@ -143,8 +143,8 @@
     return me ^ mask
 
 
-def slot_kernel(doubling, cap, slots, device_count, point_count, picks_ref, owner_ref, start_ref, place_ref, slot_owner_ref, token_ref):
-    token_ref[...] = start_ref[...]
+def slot_kernel(doubling, cap, slots, device_count, point_count, picks_ref, owner_ref, place_ref, slot_owner_ref, token_ref):
+    token_ref[...] = jnp.zeros(token_ref.shape, F32)
     picks = chunk_rows(picks_ref)
     chunks = picks.shape[0]
     rounds = picks_ref.shape[0]
@@ -188,13 +188,8 @@
     return best
 
 
-def slot_rows(piece_ref, slots, block_rows):
-    return [piece_ref[k : k + slots, :] for k in range(0, piece_ref.shape[0], block_rows)]
-
-
-def scan_table(points_ref, table_ref, best):
+def scan_table(points_ref, table_ref, rows, best):
     points = points_ref[...]
-    rows = table_ref.shape[0]
     step = min(256, rows)
     if rows <= 4096:
         for start in range(0, rows, step):
@@ -207,18 +202,9 @@
     return lax.fori_loop(0, rows // step, visit, best)
 
 
-def scan_pieces(points_ref, piece_refs, best, slots, block_rows):
-    points = points_ref[...]
-    for piece_ref in piece_refs:
-        blocks = slot_rows(piece_ref, slots, block_rows)
-        for k in range(0, len(blocks), 2):
-            best = scan_rows(points, jnp.concatenate(blocks[k : k + 2], axis=0), best)
-    return best
-
-
 def first_scan_kernel(points_ref, centres_ref, best_ref, norm_ref, token_ref):
     token_ref[...] = jnp.zeros(token_ref.shape, F32)
-    best_ref[...] = scan_table(points_ref, centres_ref, jnp.full(best_ref.shape, -jnp.inf, F32))
+    best_ref[...] = scan_table(points_ref, centres_ref, centres_ref.shape[0], jnp.full(best_ref.shape, -jnp.inf, F32))
     wide = points_ref[...].astype(F32)
     square = wide * wide
     top = square.astype(BF16)
@@ -227,36 +213,41 @@
     norm_ref[...] = nt_dot(ones, top) + nt_dot(ones, rest)
 
 
-def next_scan_kernel(slots, block_rows, id_rows, points_ref, best_ref, count_ref, *refs):
+def own_scan_kernel(slot_args, rows, points_ref, best_ref, picks_ref, owner_ref, piece_ref, *refs):
+    next_ref, count_ref, place_ref, slot_owner_ref, token_ref = refs
+    next_ref[...] = scan_table(points_ref, piece_ref, rows, best_ref[...])
+    count_ref[...] = add_tally(jnp.zeros(count_ref.shape, F32), piece_ref[rows:, :])
+    slot_kernel(*slot_args, picks_ref, owner_ref, place_ref, slot_owner_ref, token_ref)
+
+
+def next_scan_kernel(rows, tallied, points_ref, best_ref, count_ref, *refs):
     next_ref, next_count_ref, token_ref = refs[-3:]
     token_ref[...] = jnp.zeros(token_ref.shape, F32)
-    next_ref[...] = scan_pieces(points_ref, refs[:-3], best_ref[...], slots, block_rows)
-    count = count_ref[...]
-    if id_rows:
-        for piece_ref in refs[:-3]:
-            count = add_tally(count, piece_ref, slots, id_rows)
+    best, count = best_ref[...], count_ref[...]
+    for piece_ref in refs[:-3]:
+        best = scan_table(points_ref, piece_ref, rows, best)
+        if tallied:
+            count = add_tally(count, piece_ref[rows:, :])
+    next_ref[...] = best
     next_count_ref[...] = count
 
 
-def last_scan_kernel(slots, block_rows, points_ref, best_ref, norm_ref, piece_ref, near_ref, share_ref):
-    if block_rows:
-        best = scan_pieces(points_ref, [piece_ref], best_ref[...], slots, block_rows)
-    else:
-        best = scan_table(points_ref, piece_ref, best_ref[...])
+def last_scan_kernel(rows, points_ref, best_ref, norm_ref, piece_ref, near_ref, share_ref):
+    best = scan_table(points_ref, piece_ref, rows, best_ref[...])
     near = jnp.maximum(norm_ref[0:1, :] - 2.0 * jnp.max(best, axis=0, keepdims=True), 0.0)
     near_ref[...] = near
     share_ref[...] = jnp.broadcast_to(jnp.sum(near, axis=1, keepdims=True)[None], share_ref.shape)
 
 
-def lloyd_kernel(slots, block_rows, id_rows, count_ref, owner_ref, place_ref, slot_owner_ref, centres_ref, *refs):
+def lloyd_kernel(piece_rows, untold, count_ref, owner_ref, place_ref, slot_owner_ref, centres_ref, *refs):
     piece_refs, out_ref = refs[:-1], refs[-1]
     finals = out_ref.shape[0]
     slot_chunks = slot_owner_ref.shape[0]
     chunks = place_ref.shape[0]
     first_chunks = owner_ref.shape[0] - chunks
     count = count_ref[...]
-    for k in id_rows:
-        count = add_tally(count, piece_refs[k], slots, id_rows[k])
+    for k in untold:
+        count = add_tally(count, piece_refs[k][piece_rows:, :])
     weights = 1.0 + count
     weight_top = weights.astype(BF16).astype(F32)
     weight_rest = (weights - weight_top).astype(BF16).astype(F32)
@@ -286,7 +277,7 @@
     total = jnp.dot(member, centres_ref[...], preferred_element_type=F32)
     start = 0
     for piece_ref in piece_refs:
-        rows = jnp.concatenate(slot_rows(piece_ref, slots, block_rows), axis=0) if block_rows else piece_ref[...]
+        rows = piece_ref[:piece_rows, :]
         stop = start + rows.shape[0] // LANES
         member, mass = members(
             slot_owner_ref[start:stop, :], placed[start:stop], placed[slot_chunks + start : slot_chunks + stop], mass
@@ -339,6 +330,7 @@
     token = shape((1, feature_count), F32)
     id_rows = point_count // LANES
     block_rows = slots + -(-id_rows // 16) * 16
+    piece_rows = slots * (4 if doubling else device_count)
     block = local_call(
         functools.partial(pick_kernel, cap, slots),
         shape((block_rows, feature_count), BF16),
@@ -356,10 +348,12 @@
     count_shape = shape((cand_count // LANES, LANES), F32)
     owner_rows = cand_assign.reshape(-1, LANES)
 
-    def find_slots(start):
-        results = (shape((chunks, LANES), jnp.int32), shape((slot_chunks, LANES), jnp.int32), token)
+    slot_shapes = (shape((chunks, LANES), jnp.int32), shape((slot_chunks, LANES), jnp.int32))
+
+    def find_slots():
+        results = (*slot_shapes, token)
         kernel = functools.partial(slot_kernel, doubling, cap, slots, device_count, point_count)
-        return local_call(kernel, results, (picks, owner_rows, start), "slot_owners", 1.0)
+        return local_call(kernel, results, (picks, owner_rows), "slot_owners", 1.0)
 
     best_shape = shape((8, point_count), F32)
 
@@ -369,47 +363,50 @@
 
     def next_scan(best, counts, tallied, *pieces):
         cost = 0.1 + 0.8e-3 * sum(p.shape[0] for p in pieces)
-        kernel = functools.partial(next_scan_kernel, slots, block_rows, id_rows if tallied else 0)
+        kernel = functools.partial(next_scan_kernel, piece_rows, tallied)
         results = (best_shape, count_shape, token)
         return local_call(kernel, results, (points, best, counts, *pieces), "scan_sampled", cost)
 
-    def last_scan(best, piece, split):
-        cost = 0.5 + 0.8e-3 * piece.shape[0]
-        kernel = functools.partial(last_scan_kernel, slots, block_rows if split else 0)
+    def last_scan(best, piece):
+        cost = 0.5 + 0.8e-3 * piece_rows
+        kernel = functools.partial(last_scan_kernel, piece_rows)
         results = (shape((1, point_count), F32), shape((device_count, 1, LANES), F32))
         return local_call(kernel, results, (points, best, norms, piece), "scan_last", cost)
 
     if doubling:
         swap = (CORE, CORE)
         near = [block, *(permute(block, m) for m in (hop(0), hop(1), both_hops(hop(0), hop(1))))]
-        own = done_after(jnp.concatenate(near, axis=0), scanned)
+        own = [part[:slots] for part in near] + [part[slots : slots + id_rows] for part in near]
+        own = done_after(jnp.concatenate(own, axis=0), scanned)
         first = permute(own, hop(2))
         second = permute(own, hop(3))
         swapped = [permute(own, swap)]
-        places, slot_owners, found = find_slots(scanned)
-        counts = jnp.zeros(count_shape.shape, F32)
-        best, counts, scanned = next_scan(best, counts, True, own, swapped[0])
-        third = permute(done_after(first, scanned, found), hop(3))
+        best, counts, places, slot_owners, scanned = local_call(
+            functools.partial(own_scan_kernel, (doubling, cap, slots, device_count, point_count), piece_rows),
+            (best_shape, count_shape, *slot_shapes, token),
+            (points, best, picks, owner_rows, own),
+            "scan_own",
+            1.5,
+        )
+        third = permute(done_after(first, scanned), hop(3))
         swapped += [permute(first, swap), permute(second, swap)]
-        best, counts, scanned = next_scan(best, counts, True, first, second, swapped[1], swapped[2])
+        best, counts, scanned = next_scan(best, counts, True, first, second, *swapped)
         swapped.append(permute(done_after(third, scanned), swap))
         best, counts, scanned = next_scan(best, counts, False, third)
-        near, share = last_scan(best, swapped[3], True)
+        near, share = last_scan(best, swapped[3])
         shares = lax.all_to_all(share, AXES, 0, 0)
         pieces = (own, first, second, third, *swapped)
-        untold = {3: id_rows, 7: id_rows}
+        untold = (3, 7)
     else:
-        places, slot_owners, found = find_slots(scanned)
-        counts = local_call(
-            functools.partial(tally_kernel, slots, id_rows), count_shape, (block,), "tally", 0.3
-        )
+        places, slot_owners, found = find_slots()
+        counts = local_call(tally_kernel, count_shape, (block[slots : slots + id_rows],), "tally", 0.3)
         counts = lax.psum(counts, AXES)
         pieces = (lax.all_gather(block[:slots], AXES, tiled=True),)
-        near, share = last_scan(best, pieces[0], False)
+        near, share = last_scan(best, pieces[0])
         shares = lax.psum(share[:1], AXES)
-        untold = {}
+        untold = ()
     new_centres = local_call(
-        functools.partial(lloyd_kernel, slots, block_rows if doubling else 0, untold),
+        functools.partial(lloyd_kernel, piece_rows, untold),
         shape((finals, feature_count), F32),
         (counts, owner_rows, places, slot_owners, centres, *pieces),
         "lloyd",

time: 46.5 us -> 42.3 us (0.910)
  starting transfers between devices: 17.3 us -> 13.4 us
  waiting for transfers between devices: 13.6 us -> 12.7 us
  Pallas kernels: 14.4 us -> 15 us
    ppermute x10, starting transfers between devices: 14.3 us -> 9.51 us  [permute(): return lax.ppermute(value, AXES, pairs)]
    ppermute x10, waiting for transfers between devices: 10.1 us -> 9.23 us  [permute(): return lax.ppermute(value, AXES, pairs)]
    all_to_all x1, starting transfers between devices: 3.07 us -> 3.91 us  [shards(): shares = lax.all_to_all(share, AXES, 0, 0)]
    pallas_call x9 -> x8, Pallas kernels: 14.4 us -> 15 us  [local_call(): pl.pallas_call(body, out_shape=out_shape, in_specs=specs, out_specs=jax.t...]
  transfers between devices with their start and end apart: 11 -> 11, of which waited for: 6 -> 8; matrix products, arithmetic and copies ran while one was open for 0% -> 0% of each run, Pallas kernels for 24% -> 27%
where the time goes in v3:
time: 42.3 us; the launch traced here: 42.1 us
  Pallas kernels  15 us (35%)
  starting transfers between devices  13.4 us (32%)
  waiting for transfers between devices  12.7 us (30%)
  between operations  0.79 us (2%)
    pallas_call x8, Pallas kernels, local_call(): pl.pallas_call(body, out_shape=out_shape, in_specs=specs, out_specs=jax.t...  15 us
    ppermute x10, starting transfers between devices, permute(): return lax.ppermute(value, AXES, pairs)  9.51 us
    ppermute x10, waiting for transfers between devices, permute(): return lax.ppermute(value, AXES, pairs)  9.23 us
    all_to_all x1, starting transfers between devices, shards(): shares = lax.all_to_all(share, AXES, 0, 0)  3.91 us
    all_to_all x1, waiting for transfers between devices, shards(): shares = lax.all_to_all(share, AXES, 0, 0)  3.51 us
  transfers between devices with their start and end apart: 11, of which 8 were waited for; matrix products, arithmetic and copies ran while one was open for 0% of the time, Pallas kernels for 27%

profile of v3, /device:TPU:0, one launch (start us, length us, event | category | flops | bytes accessed | tf_op | source)
XLA Modules:
  0.0 42.1 jit_solution(2789555531362929780)
XLA Ops:
  0.6 1.6 %pick_rows.1 = bf16[144,256]{1,0:T(8,128)(2,1)S(1)} custom-call(s32[2,1024]{1,0:T(2,128)} %refs_2_.1, bf16[1024,256]{1,0:T(8,128)(2,1)} %refs_0_.11, s32[8,128]{1,0:T(8,128)} %bitcast.5), custom_call_target="tpu_custom_call" | custom-call | flops 800000000 | tf_op jit(solution)/shard_map/pick_rows/pallas_call | solution.py:50
  2.2 5.1 %collective-permute-start.2 = (bf16[144,256]{1,0:T(8,128)(2,1)S(1)}, bf16[144,256]{1,0:T(8,128)(2,1)S(1)}, u32[]{:S(2)}, u32[]{:S(2)}) collective-permute-start(bf16[144,256]{1,0:T(8,128)(2,1)S(1)} %pick_rows.1), channel_id=1, source_target_pairs={{0,3},{1,2},{2,1},{3,0},{4,13},{5,12},{6,15},{7,14},{8,11},{9,10},... | collective-permute-start | bytes 221192 | tf_op jit(solution)/shard_map/ppermute | solution.py:297
  7.3 0.6 %collective-permute-start = (bf16[144,256]{1,0:T(8,128)(2,1)S(1)}, bf16[144,256]{1,0:T(8,128)(2,1)S(1)}, u32[]{:S(2)}, u32[]{:S(2)}) collective-permute-start(bf16[144,256]{1,0:T(8,128)(2,1)S(1)} %pick_rows.1), channel_id=1, source_target_pairs={{0,1},{1,0},{2,3},{3,2},{4,12},{5,13},{6,14},{7,15},{8,9},{9,8},{1... | collective-permute-start | bytes 221192 | tf_op jit(solution)/shard_map/ppermute | solution.py:297
  8.0 1.7 %scan_centres.1 = (f32[8,1024]{1,0:T(8,128)S(1)}, f32[8,1024]{1,0:T(8,128)S(1)}, f32[1,256]{1,0:T(1,128)S(1)}) custom-call(bf16[1024,256]{1,0:T(8,128)(2,1)S(1)} %copy-done.1, bf16[2048,256]{1,0:T(8,128)(2,1)S(1)} %copy-done), custom_call_target="tpu_custom_call" | custom-call | flops 1600000000 | tf_op jit(solution)/shard_map/scan_centres/pallas_call | solution.py:50
  9.7 1.9 %collective-permute-done = bf16[144,256]{1,0:T(8,128)(2,1)S(1)} collective-permute-done((bf16[144,256]{1,0:T(8,128)(2,1)S(1)}, bf16[144,256]{1,0:T(8,128)(2,1)S(1)}, u32[]{:S(2)}, u32[]{:S(2)}) %collective-permute-start) | collective-permute-done | bytes 73760 | tf_op jit(solution)/shard_map/ppermute | solution.py:297
  11.7 1.1 %collective-permute-done.1 = bf16[144,256]{1,0:T(8,128)(2,1)S(1)} collective-permute-done((bf16[144,256]{1,0:T(8,128)(2,1)S(1)}, bf16[144,256]{1,0:T(8,128)(2,1)S(1)}, u32[]{:S(2)}, u32[]{:S(2)}) %collective-permute-start.1) | collective-permute-done | bytes 73760 | tf_op jit(solution)/shard_map/ppermute | solution.py:297
  13.0 1.3 %collective-permute-start.4 = (bf16[544,256]{1,0:T(8,128)(2,1)S(1)}, bf16[544,256]{1,0:T(8,128)(2,1)S(1)}, u32[]{:S(2)}, u32[]{:S(2)}) collective-permute-start(bf16[544,256]{1,0:T(8,128)(2,1)S(1)} %broadcast_select_fusion.2.refs_4_.refs_5_), channel_id=1, source_target_pairs={{0,8},{1,9},{2,10},{3,11},{4,20},{5,21},{6,22},{7,23},{8,0},{9,1},... | collective-permute-start | bytes 835592 | tf_op jit(solution)/shard_map/ppermute | solution.py:297
  14.3 1.5 %collective-permute-start.3 = (bf16[544,256]{1,0:T(8,128)(2,1)S(1)}, bf16[544,256]{1,0:T(8,128)(2,1)S(1)}, u32[]{:S(2)}, u32[]{:S(2)}) collective-permute-start(bf16[544,256]{1,0:T(8,128)(2,1)S(1)} %broadcast_select_fusion.2.refs_4_.refs_5_), channel_id=1, source_target_pairs={{0,16},{1,17},{2,18},{3,19},{4,6},{5,7},{6,4},{7,5},{8,24},{9,25},... | collective-permute-start | bytes 835592 | tf_op jit(solution)/shard_map/ppermute | solution.py:297
  15.8 2.2 %scan_own.1 = (f32[8,1024]{1,0:T(8,128)S(1)}, f32[32,128]{1,0:T(8,128)S(1)}, s32[16,128]{1,0:T(8,128)S(1)}, s32[32,128]{1,0:T(8,128)S(1)}, f32[1,256]{1,0:T(1,128)S(1)}) custom-call(bf16[1024,256]{1,0:T(8,128)(2,1)S(1)} %copy-done.1, f32[8,1024]{1,0:T(8,128)S(1)} %get-tuple-element.17.refs_1_, s32[2,1024]{1,0:T(2,128)S(1)} %copy-done.3, ...), custom_call_target="tpu_custom_call" | custom-call | flops 1500000000 | tf_op jit(solution)/shard_map/scan_own/pallas_call | solution.py:50
  18.0 1.6 %collective-permute-done.4.refs_4_.refs_7_ = bf16[544,256]{1,0:T(8,128)(2,1)S(1)} collective-permute-done((bf16[544,256]{1,0:T(8,128)(2,1)S(1)}, bf16[544,256]{1,0:T(8,128)(2,1)S(1)}, u32[]{:S(2)}, u32[]{:S(2)}) %collective-permute-start.4) | collective-permute-done | bytes 278560 | tf_op jit(solution)/shard_map/ppermute | solution.py:297
  19.6 1.2 %collective-permute-done.3.refs_3_.refs_6_ = bf16[544,256]{1,0:T(8,128)(2,1)S(1)} collective-permute-done((bf16[544,256]{1,0:T(8,128)(2,1)S(1)}, bf16[544,256]{1,0:T(8,128)(2,1)S(1)}, u32[]{:S(2)}, u32[]{:S(2)}) %collective-permute-start.3) | collective-permute-done | bytes 278560 | tf_op jit(solution)/shard_map/ppermute | solution.py:297
  20.8 0.0 collective-permute-start.6
  20.9 0.8 %collective-permute-start.8 = (bf16[544,256]{1,0:T(8,128)(2,1)S(1)}, bf16[544,256]{1,0:T(8,128)(2,1)S(1)}, u32[]{:S(2)}, u32[]{:S(2)}) collective-permute-start(bf16[544,256]{1,0:T(8,128)(2,1)S(1)} %broadcast_select_fusion.1), channel_id=1, source_target_pairs={{0,8},{1,9},{2,10},{3,11},{4,20},{5,21},{6,22},{7,23},{8,0},{9,1},... | collective-permute-start | bytes 835592 | tf_op jit(solution)/shard_map/ppermute | solution.py:297
  21.7 0.7 %collective-permute-done.6.refs_6_.refs_10_ = bf16[544,256]{1,0:T(8,128)(2,1)S(1)} collective-permute-done((bf16[544,256]{1,0:T(8,128)(2,1)S(1)}, bf16[544,256]{1,0:T(8,128)(2,1)S(1)}, u32[]{:S(2)}, u32[]{:S(2)}) %collective-permute-start.6) | collective-permute-done | bytes 278560 | tf_op jit(solution)/shard_map/ppermute | solution.py:297
  22.4 3.0 %scan_sampled.2 = (f32[8,1024]{1,0:T(8,128)S(1)}, f32[32,128]{1,0:T(8,128)S(1)}, f32[1,256]{1,0:T(1,128)S(1)}) custom-call(bf16[1024,256]{1,0:T(8,128)(2,1)S(1)} %copy-done.1, f32[8,1024]{1,0:T(8,128)S(1)} %get-tuple-element.19.refs_1_, f32[32,128]{1,0:T(8,128)S(1)} %get-tuple-element.20.refs_2_, ...), custom_call_target="tpu_custom_call" | custom-call | flops 2276000000 | tf_op jit(solution)/shard_map/scan_sampled/pallas_call | solution.py:50
  25.4 2.1 %collective-permute-done.8.refs_3_.refs_8_ = bf16[544,256]{1,0:T(8,128)(2,1)S(1)} collective-permute-done((bf16[544,256]{1,0:T(8,128)(2,1)S(1)}, bf16[544,256]{1,0:T(8,128)(2,1)S(1)}, u32[]{:S(2)}, u32[]{:S(2)}) %collective-permute-start.8) | collective-permute-done | bytes 278560 | tf_op jit(solution)/shard_map/ppermute | solution.py:297
  27.5 0.1 collective-permute-start.9
  27.6 1.0 %scan_sampled.3 = (f32[8,1024]{1,0:T(8,128)S(1)}, f32[32,128]{1,0:T(8,128)S(1)}, f32[1,256]{1,0:T(1,128)}) custom-call(bf16[1024,256]{1,0:T(8,128)(2,1)S(1)} %copy-done.1, f32[8,1024]{1,0:T(8,128)S(1)} %get-tuple-element.21.refs_1_, f32[32,128]{1,0:T(8,128)S(1)} %get-tuple-element.22.refs_2_, bf16[544,256]{1,0:T(8,128)(2,1)S(1)} %collective-permute-done.8.refs_3_.refs_8_), custom_call_target="tpu_custom_call" | custom-call | flops 535200000 | tf_op jit(solution)/shard_map/scan_sampled/pallas_call | solution.py:50
  28.6 0.6 %collective-permute-done.9.refs_3_.refs_12_ = bf16[544,256]{1,0:T(8,128)(2,1)S(1)} collective-permute-done((bf16[544,256]{1,0:T(8,128)(2,1)S(1)}, bf16[544,256]{1,0:T(8,128)(2,1)S(1)}, u32[]{:S(2)}, u32[]{:S(2)}) %collective-permute-start.9) | collective-permute-done | bytes 278560 | tf_op jit(solution)/shard_map/ppermute | solution.py:297
  29.1 1.2 %scan_last.1 = (f32[1,1024]{1,0:T(1,128)S(1)}, f32[32,1,128]{2,1,0:T(1,128)}) custom-call(bf16[1024,256]{1,0:T(8,128)(2,1)S(1)} %copy-done.1, f32[8,1024]{1,0:T(8,128)S(1)} %get-tuple-element.24.refs_1_, f32[8,1024]{1,0:T(8,128)S(1)} %get-tuple-element.25.refs_2_, bf16[544,256]{1,0:T(8,128)(2,1)S(1)} %collective-permute-done.9.refs_3_.refs_12_), custom_call_target="tpu_custom_call" | custom-call | flops 909600000 | tf_op jit(solution)/shard_map/scan_last/pallas_call | solution.py:50
  30.3 3.9 %all-to-all-start = ((f32[32,1,128]{2,1,0:T(1,128)}), f32[32,1,128]{2,1,0:T(1,128)S(1)}, u32[]{:S(2)}, u32[]{:S(2)}) async-start(f32[32,1,128]{2,1,0:T(1,128)} %get-tuple-element.28), calls=%async_computation | async-start | bytes 32768 | tf_op jit(solution)/shard_map/all_to_all | solution.py:397
  34.2 3.7 %lloyd.1 = f32[128,256]{1,0:T(8,128)} custom-call(f32[32,128]{1,0:T(8,128)S(1)} %get-tuple-element.29.refs_0_, s32[32,128]{1,0:T(8,128)S(1)} %bitcast.4, s32[16,128]{1,0:T(8,128)S(1)} %get-tuple-element.30.refs_2_, s32[32,128]{1,0:T(8,128)S(1)} %get-tuple-element.31.refs_3_, bf16[2048,256]{1,0:T(8,128)(2,1)S(1)} %copy-done, ...), custom_call_target="tpu_custom_call" | custom-call | flops 2600000000 | tf_op jit(solution)/shard_map/lloyd/pallas_call | solution.py:50
  37.9 3.5 %all-to-all-done.refs_1_ = f32[32,1,128]{2,1,0:T(1,128)S(1)} async-done(((f32[32,1,128]{2,1,0:T(1,128)}), f32[32,1,128]{2,1,0:T(1,128)S(1)}, u32[]{:S(2)}, u32[]{:S(2)}) %all-to-all-start) | async-done | bytes 16416 | tf_op jit(solution)/shard_map/all_to_all | solution.py:397
  41.4 0.7 %finish.1 = f32[1,1024]{1,0:T(1,128)} custom-call(f32[1,1024]{1,0:T(1,128)S(1)} %get-tuple-element.27.refs_0_, f32[32,1,128]{2,1,0:T(1,128)S(1)} %all-to-all-done.refs_1_), custom_call_target="tpu_custom_call" | custom-call | flops 600000000 | tf_op jit(solution)/shard_map/finish/pallas_call | solution.py:50
  (28 shorter events, 0.2 us)
Async XLA Ops:
  0.6 7.4 %copy-start = (bf16[2048,256]{1,0:T(8,128)(2,1)S(1)}, bf16[2048,256]{1,0:T(8,128)(2,1)}, u32[]{:S(2)}) copy-start(bf16[2048,256]{1,0:T(8,128)(2,1)} %refs_4_.1) | copy-start | bytes 3145732
  0.6 7.3 %copy-start.1 = (bf16[1024,256]{1,0:T(8,128)(2,1)S(1)}, bf16[1024,256]{1,0:T(8,128)(2,1)}, u32[]{:S(2)}) copy-start(bf16[1024,256]{1,0:T(8,128)(2,1)} %refs_0_.11) | copy-start | bytes 1572868
  2.2 10.6 %collective-permute-start.2 = (bf16[144,256]{1,0:T(8,128)(2,1)S(1)}, bf16[144,256]{1,0:T(8,128)(2,1)S(1)}, u32[]{:S(2)}, u32[]{:S(2)}) collective-permute-start(bf16[144,256]{1,0:T(8,128)(2,1)S(1)} %pick_rows.1), channel_id=1, source_target_pairs={{0,3},{1,2},{2,1},{3,0},{4,13},{5,12},{6,15},{7,14},{8,11},{9,10},... | collective-permute-start | bytes 221192 | tf_op jit(solution)/shard_map/ppermute | solution.py:297
  7.3 5.5 %collective-permute-start.1 = (bf16[144,256]{1,0:T(8,128)(2,1)S(1)}, bf16[144,256]{1,0:T(8,128)(2,1)S(1)}, u32[]{:S(2)}, u32[]{:S(2)}) collective-permute-start(bf16[144,256]{1,0:T(8,128)(2,1)S(1)} %pick_rows.1), channel_id=1, source_target_pairs={{0,2},{1,3},{2,0},{3,1},{4,5},{5,4},{6,7},{7,6},{8,10},{9,11},{10,... | collective-permute-start | bytes 221192 | tf_op jit(solution)/shard_map/ppermute | solution.py:297
  7.3 4.4 %collective-permute-start = (bf16[144,256]{1,0:T(8,128)(2,1)S(1)}, bf16[144,256]{1,0:T(8,128)(2,1)S(1)}, u32[]{:S(2)}, u32[]{:S(2)}) collective-permute-start(bf16[144,256]{1,0:T(8,128)(2,1)S(1)} %pick_rows.1), channel_id=1, source_target_pairs={{0,1},{1,0},{2,3},{3,2},{4,12},{5,13},{6,14},{7,15},{8,9},{9,8},{1... | collective-permute-start | bytes 221192 | tf_op jit(solution)/shard_map/ppermute | solution.py:297
  12.9 2.9 %copy-start.2 = (s32[4096,1]{0,1:T(1,128)S(1)}, s32[4096,1]{0,1:T(1,128)}, u32[]{:S(2)}) copy-start(s32[4096,1]{0,1:T(1,128)} %param.9) | copy-start | bytes 49156
  12.9 2.9 %copy-start.3 = (s32[2,1024]{1,0:T(2,128)S(1)}, s32[2,1024]{1,0:T(2,128)}, u32[]{:S(2)}) copy-start(s32[2,1024]{1,0:T(2,128)} %refs_2_.1) | copy-start | bytes 24580
  13.0 6.6 %collective-permute-start.4 = (bf16[544,256]{1,0:T(8,128)(2,1)S(1)}, bf16[544,256]{1,0:T(8,128)(2,1)S(1)}, u32[]{:S(2)}, u32[]{:S(2)}) collective-permute-start(bf16[544,256]{1,0:T(8,128)(2,1)S(1)} %broadcast_select_fusion.2.refs_4_.refs_5_), channel_id=1, source_target_pairs={{0,8},{1,9},{2,10},{3,11},{4,20},{5,21},{6,22},{7,23},{8,0},{9,1},... | collective-permute-start | bytes 835592 | tf_op jit(solution)/shard_map/ppermute | solution.py:297
  14.3 6.5 %collective-permute-start.3 = (bf16[544,256]{1,0:T(8,128)(2,1)S(1)}, bf16[544,256]{1,0:T(8,128)(2,1)S(1)}, u32[]{:S(2)}, u32[]{:S(2)}) collective-permute-start(bf16[544,256]{1,0:T(8,128)(2,1)S(1)} %broadcast_select_fusion.2.refs_4_.refs_5_), channel_id=1, source_target_pairs={{0,16},{1,17},{2,18},{3,19},{4,6},{5,7},{6,4},{7,5},{8,24},{9,25},... | collective-permute-start | bytes 835592 | tf_op jit(solution)/shard_map/ppermute | solution.py:297
  15.8 5.9 %collective-permute-start.5 = (bf16[544,256]{1,0:T(8,128)(2,1)S(1)}, bf16[544,256]{1,0:T(8,128)(2,1)S(1)}, u32[]{:S(2)}, u32[]{:S(2)}) collective-permute-start(bf16[544,256]{1,0:T(8,128)(2,1)S(1)} %broadcast_select_fusion.2.refs_4_.refs_5_), channel_id=1, source_target_pairs={{0,4},{1,5},{2,6},{3,7},{4,0},{5,1},{6,2},{7,3},{8,12},{9,13},{10,... | collective-permute-start | bytes 835592 | tf_op jit(solution)/shard_map/ppermute | solution.py:297
  19.6 2.2 %collective-permute-start.7 = (bf16[544,256]{1,0:T(8,128)(2,1)S(1)}, bf16[544,256]{1,0:T(8,128)(2,1)S(1)}, u32[]{:S(2)}, u32[]{:S(2)}) collective-permute-start(bf16[544,256]{1,0:T(8,128)(2,1)S(1)} %collective-permute-done.4.refs_4_.refs_7_), channel_id=1, source_target_pairs={{0,4},{1,5},{2,6},{3,7},{4,0},{5,1},{6,2},{7,3},{8,12},{9,13},{10,... | collective-permute-start | bytes 835592 | tf_op jit(solution)/shard_map/ppermute | solution.py:297
  20.8 1.6 %collective-permute-start.6 = (bf16[544,256]{1,0:T(8,128)(2,1)S(1)}, bf16[544,256]{1,0:T(8,128)(2,1)S(1)}, u32[]{:S(2)}, u32[]{:S(2)}) collective-permute-start(bf16[544,256]{1,0:T(8,128)(2,1)S(1)} %collective-permute-done.3.refs_3_.refs_6_), channel_id=1, source_target_pairs={{0,4},{1,5},{2,6},{3,7},{4,0},{5,1},{6,2},{7,3},{8,12},{9,13},{10,... | collective-permute-start | bytes 835592 | tf_op jit(solution)/shard_map/ppermute | solution.py:297
  20.9 6.6 %collective-permute-start.8 = (bf16[544,256]{1,0:T(8,128)(2,1)S(1)}, bf16[544,256]{1,0:T(8,128)(2,1)S(1)}, u32[]{:S(2)}, u32[]{:S(2)}) collective-permute-start(bf16[544,256]{1,0:T(8,128)(2,1)S(1)} %broadcast_select_fusion.1), channel_id=1, source_target_pairs={{0,8},{1,9},{2,10},{3,11},{4,20},{5,21},{6,22},{7,23},{8,0},{9,1},... | collective-permute-start | bytes 835592 | tf_op jit(solution)/shard_map/ppermute | solution.py:297
  27.5 1.6 %collective-permute-start.9 = (bf16[544,256]{1,0:T(8,128)(2,1)S(1)}, bf16[544,256]{1,0:T(8,128)(2,1)S(1)}, u32[]{:S(2)}, u32[]{:S(2)}) collective-permute-start(bf16[544,256]{1,0:T(8,128)(2,1)S(1)} %broadcast_select_fusion), channel_id=1, source_target_pairs={{0,4},{1,5},{2,6},{3,7},{4,0},{5,1},{6,2},{7,3},{8,12},{9,13},{10,... | collective-permute-start | bytes 835592 | tf_op jit(solution)/shard_map/ppermute | solution.py:297
  30.3 11.1 %all-to-all-start = ((f32[32,1,128]{2,1,0:T(1,128)}), f32[32,1,128]{2,1,0:T(1,128)S(1)}, u32[]{:S(2)}, u32[]{:S(2)}) async-start(f32[32,1,128]{2,1,0:T(1,128)} %get-tuple-element.28), calls=%async_computation | async-start | bytes 32768 | tf_op jit(solution)/shard_map/all_to_all | solution.py:397

commit v4 on v3

v4 whole, which is shorter than its diff:
```python
import functools

import jax
import jax.numpy as jnp
from jax import lax
from jax.experimental import pallas as pl
from jax.experimental.pallas import tpu as pltpu
from jax.sharding import PartitionSpec as P

K_FINAL = 1024
AXES = ("row", "col")
LANES = 128
VMEM_LIMIT = 20 * 1024 * 1024
FLOPS_PER_US = 1.0e9
F32 = jnp.float32
BF16 = jnp.bfloat16

CORE = 4
FAN = ((2, 3), (24, 16))
SPREAD = ((24, 16), (2, 3))


def nt_dot(left, right):
    return lax.dot_general(left, right, (((1,), (1,)), ((), ())), preferred_element_type=F32)


def iota(shape, axis):
    return lax.broadcasted_iota(jnp.int32, shape, axis)


def device_index():
    return lax.axis_index("row") * lax.axis_size("col") + lax.axis_index("col")


def whole_spec():
    return pl.BlockSpec(memory_space=pltpu.VMEM)


def local_call(kernel, out_shape, operands, name, cost, after=(), unread=(), scratch=(), passed=(), vmem=VMEM_LIMIT):
    untouched = pl.BlockSpec(memory_space=pl.ANY)
    specs = [whole_spec()] * len(operands) + [untouched] * (len(after) + len(passed))
    result_specs = jax.tree.map(lambda _: whole_spec(), out_shape)
    aliases = {}
    if passed:
        first = len(operands) + len(after)
        aliases = {first + i: len(out_shape) + i for i in range(len(passed))}
        out_shape = (*out_shape, *(jax.ShapeDtypeStruct(x.shape, x.dtype) for x in passed))
        result_specs = (*result_specs, *[untouched] * len(passed))
    operands = list(operands)
    for place in unread:
        specs[place] = pl.BlockSpec(memory_space=pltpu.HBM)
        operands[place] = pltpu.with_memory_space_constraint(operands[place], pltpu.HBM)
    count = len(operands)

    skipped = len(after) + len(passed)
    results = len(out_shape) if isinstance(out_shape, tuple) else 1

    def body(*refs):
        outs = refs[count + skipped : count + skipped + results - len(passed)]
        kernel(*refs[:count], *outs, *refs[count + skipped + results :])

    return pl.pallas_call(
        body,
        out_shape=out_shape,
        in_specs=specs,
        out_specs=result_specs,
        input_output_aliases=aliases,
        scratch_shapes=list(scratch),
        compiler_params=pltpu.CompilerParams(vmem_limit_bytes=vmem),
        cost_estimate=pl.CostEstimate(flops=int(cost * FLOPS_PER_US), bytes_accessed=0, transcendentals=0),
        name=name,
    )(*operands, *after, *passed)


def chunk_rows(ref):
    rounds, samples = ref.shape
    return jnp.concatenate(
        [ref[r : r + 1, k : k + LANES] for r in range(rounds) for k in range(0, samples, LANES)], axis=0
    )


FAR = 2.0**64


def pick_kernel(cap, slots, picks_hbm, points_hbm, assign_hbm, out_ref, points_ref, picks_ref, assign_ref, sems):
    picks_copy = pltpu.make_async_copy(picks_hbm, picks_ref, sems.at[0])
    assign_copy = pltpu.make_async_copy(assign_hbm, assign_ref, sems.at[1])
    points_copy = pltpu.make_async_copy(points_hbm, points_ref, sems.at[2])
    picks_copy.start()
    assign_copy.start()
    points_copy.start()
    picks_copy.wait()
    rounds = picks_ref.shape[0]
    per_round = picks_ref.shape[1] // LANES
    chunks = rounds * per_round
    point_count = points_ref.shape[0]
    local = chunk_rows(picks_ref) - device_index() * point_count
    owned = (local >= 0) & (local < point_count)
    flags = owned.astype(F32).astype(BF16)
    lower = (iota((LANES, LANES), 0) <= iota((LANES, LANES), 1)).astype(F32).astype(BF16)
    inside = jnp.dot(flags, lower, preferred_element_type=F32)
    sums = jnp.dot(flags, jnp.ones((LANES, LANES), BF16), preferred_element_type=F32)
    first, second = iota((chunks, chunks), 0), iota((chunks, chunks), 1)
    same = lax.div(first, per_round) == lax.div(second, per_round)
    earlier = (same & (second < first)).astype(F32).astype(BF16)
    before = jnp.dot(earlier, sums.astype(BF16), preferred_element_type=F32)
    round_of = lax.div(iota((chunks, LANES), 0), per_round)
    slot = (inside + before).astype(jnp.int32) - 1 + round_of * cap
    slot = jnp.where(owned, slot, -1)
    slot_ids = iota((slots, LANES), 0)
    found = jnp.zeros((slots, LANES), jnp.int32)
    for t in range(chunks):
        found = found + jnp.where(slot[t : t + 1, :] == slot_ids, local[t : t + 1, :] + 1, 0)
    place = jnp.sum(found.astype(F32), axis=1, keepdims=True).astype(jnp.int32)
    chosen = (iota((slots, point_count), 1) + 1 == place).astype(F32).astype(BF16)
    assign_copy.wait()
    count = split_counts(tally(assign_ref[...], out_ref.shape[0] - slots))
    points_copy.wait()
    rows = jnp.dot(chosen, points_ref[...], preferred_element_type=F32)
    rows = jnp.where(place > 0, rows, FAR)
    out_ref[...] = jnp.concatenate([rows, count], axis=0).astype(BF16)


def tally(ids, cand_chunks):
    lane_rows = iota((LANES, LANES), 0)
    chunk_ids = iota((cand_chunks, LANES), 0)
    high = [(lax.div(ids[t : t + 1, :], LANES) == chunk_ids).astype(F32) for t in range(ids.shape[0])]
    low = [(lax.rem(ids[t : t + 1, :], LANES) == lane_rows).astype(F32) for t in range(ids.shape[0])]
    return nt_dot(jnp.concatenate(high, axis=1).astype(BF16), jnp.concatenate(low, axis=1).astype(BF16))


def split_counts(count):
    firsts = jnp.floor(count * (1.0 / 256.0))
    return jnp.concatenate([firsts, count - 256.0 * firsts], axis=1)


def join_counts(parts):
    parts = parts.astype(F32)
    return 256.0 * parts[:, :LANES] + parts[:, LANES:]


def holders_in_order(doubling, device_ids):
    if not doubling:
        return device_ids
    me = device_index()
    core = lax.rem(lax.div(me, CORE), 2)
    other = lax.div(device_ids, 16)
    kind = core ^ other
    mask = other * CORE
    for bit, masks in enumerate((*zip(*FAN), *zip(*SPREAD))):
        present = lax.rem(lax.div(device_ids, 1 << bit), 2)
        mask = mask ^ (present * jnp.where(kind == 0, masks[0], masks[1]))
    return me ^ mask


def slot_kernel(doubling, cap, slots, device_count, point_count, picks_ref, owner_ref, place_ref, slot_owner_ref, token_ref):
    token_ref[...] = jnp.zeros(token_ref.shape, F32)
    picks = chunk_rows(picks_ref)
    chunks = picks.shape[0]
    rounds = picks_ref.shape[0]
    per_round = chunks // rounds
    cand_chunks = owner_ref.shape[0]
    slot_chunks = slot_owner_ref.shape[0]
    lane_rows = iota((LANES, LANES), 0)
    lower = (lane_rows <= iota((LANES, LANES), 1)).astype(F32).astype(BF16)
    ones = jnp.ones((LANES, LANES), BF16)
    device_ids = iota((device_count, LANES), 0)
    first_chunk = cand_chunks - chunks
    holders = holders_in_order(doubling, device_ids)
    owners = jnp.zeros((2 * slot_chunks, LANES), F32)
    for r in range(rounds):
        carry = jnp.zeros((device_count, LANES), F32)
        for u in range(per_round):
            t = r * per_round + u
            holder = lax.div(picks[t : t + 1, :], point_count)
            held = (holder == device_ids).astype(F32)
            running = jnp.dot(held.astype(BF16), lower, preferred_element_type=F32) + carry
            carry = carry + jnp.dot(held.astype(BF16), ones, preferred_element_type=F32)
            rank = jnp.sum(held * running, axis=0, keepdims=True).astype(jnp.int32) - 1
            block = jnp.sum(jnp.where(holders == holder, device_ids, 0), axis=0, keepdims=True)
            place = block * slots + r * cap + rank
            place_ref[t : t + 1, :] = place
            high = lax.div(place, LANES) == iota((slot_chunks, LANES), 0)
            low = (lax.rem(place, LANES) == lane_rows).astype(F32).astype(BF16)
            tag = owner_ref[first_chunk + t : first_chunk + t + 1, :] + 1
            coarse = jnp.where(high, lax.div(tag, 32).astype(F32), 0.0)
            fine = jnp.where(high, lax.rem(tag, 32).astype(F32), 0.0)
            owners = owners + nt_dot(jnp.concatenate([coarse, fine], axis=0).astype(BF16), low)
    slot_owner_ref[...] = (owners[:slot_chunks] * 32.0 + owners[slot_chunks:]).astype(jnp.int32) - 1


def scan_rows(points, piece, best):
    wide = piece.astype(F32)
    half = 0.5 * jnp.sum(wide * wide, axis=1, keepdims=True)
    score = nt_dot(piece, points) - half
    for k in range(0, piece.shape[0], 8):
        best = jnp.maximum(best, score[k : k + 8, :])
    return best


def scan_table(points_ref, table_ref, first, rows, best):
    points = points_ref[...]
    step = min(256, rows)
    if rows <= 4096:
        for start in range(first, first + rows, step):
            best = scan_rows(points, table_ref[start : start + step, :], best)
        return best

    def visit(i, best):
        return scan_rows(points, table_ref[pl.ds(pl.multiple_of(i * step, step), step), :], best)

    return lax.fori_loop(0, rows // step, visit, best)


def first_scan_kernel(points_ref, centres_ref, best_ref, norm_ref, token_ref):
    token_ref[...] = jnp.zeros(token_ref.shape, F32)
    best_ref[...] = scan_table(points_ref, centres_ref, 0, centres_ref.shape[0], jnp.full(best_ref.shape, -jnp.inf, F32))
    wide = points_ref[...].astype(F32)
    square = wide * wide
    top = square.astype(BF16)
    rest = (square - top.astype(F32)).astype(BF16)
    ones = jnp.ones((8, square.shape[1]), BF16)
    norm_ref[...] = nt_dot(ones, top) + nt_dot(ones, rest)


def scan_pieces(points_ref, piece_refs, rows, best):
    for piece_ref in piece_refs:
        best = scan_table(points_ref, piece_ref, 0, rows, best)
    return best


def own_scan_kernel(slot_args, rows, points_ref, beside_ref, best_ref, picks_ref, owner_ref, piece_ref, *refs):
    next_ref, beside_best_ref, place_ref, slot_owner_ref, token_ref = refs
    next_ref[...] = scan_pieces(points_ref, [piece_ref], rows, best_ref[...])
    lowest = jnp.full(beside_best_ref.shape, -jnp.inf, F32)
    beside_best_ref[...] = scan_pieces(beside_ref, [piece_ref], rows, lowest)
    slot_kernel(*slot_args, picks_ref, owner_ref, place_ref, slot_owner_ref, token_ref)


def beside_scan_kernel(rows, beside_ref, best_ref, *refs):
    piece_refs, (message_ref, token_ref) = refs[:-2], refs[-2:]
    token_ref[...] = jnp.zeros(token_ref.shape, F32)
    best = scan_pieces(beside_ref, piece_refs[1:], rows, best_ref[...])
    top = jnp.max(best, axis=0, keepdims=True)
    top = [top[:, k : k + LANES] for k in range(0, top.shape[1], LANES)]
    count = join_counts(piece_refs[0][rows:, :])
    for piece_ref in piece_refs[1:]:
        count = count + join_counts(piece_ref[rows:, :])
    message_ref[...] = jnp.concatenate([*top, count], axis=0)


def next_scan_kernel(rows, points_ref, best_ref, start_ref, *refs):
    refs[-1][...] = jnp.max(scan_pieces(points_ref, refs[:-1], rows, best_ref[...]), axis=0, keepdims=True)


def near_kernel(norm_ref, top_ref, message_ref, near_ref, share_ref):
    top = top_ref[...]
    if message_ref is not None:
        told = message_ref[: top.shape[1] // LANES, :]
        top = jnp.maximum(top, jnp.concatenate([told[k : k + 1, :] for k in range(told.shape[0])], axis=1))
    near = jnp.maximum(norm_ref[0:1, :] - 2.0 * top, 0.0)
    near_ref[...] = near
    share_ref[...] = jnp.broadcast_to(jnp.sum(near, axis=1, keepdims=True)[None], share_ref.shape)


def lloyd_kernel(piece_rows, sides, first_place, count_refs, owner_ref, place_ref, slot_owner_ref, centres_ref, *refs):
    piece_refs, out_refs = refs[:-sides], refs[-sides:]
    finals, features = out_refs[0].shape[0], centres_ref.shape[1]
    slot_chunks = slot_owner_ref.shape[0]
    chunks = place_ref.shape[0]
    first_chunks = owner_ref.shape[0] - chunks
    count = sum(ref[first_place:, :] for ref in count_refs)
    weights = 1.0 + count
    weight_top = weights.astype(BF16).astype(F32)
    weight_rest = (weights - weight_top).astype(BF16).astype(F32)
    lane_rows = iota((LANES, LANES), 0)
    placed = jnp.zeros((2 * slot_chunks, LANES), F32)
    for t in range(chunks):
        place = place_ref[t : t + 1, :]
        high = lax.div(place, LANES) == iota((slot_chunks, LANES), 0)
        low = (lax.rem(place, LANES) == lane_rows).astype(F32).astype(BF16)
        c = first_chunks + t
        both = [jnp.where(high, w[c : c + 1, :], 0.0) for w in (weight_top, weight_rest)]
        placed = placed + nt_dot(jnp.concatenate(both, axis=0).astype(BF16), low)
    row = lax.axis_index("row")
    side = lax.rem(row, sides)
    place = iota((sides * finals, LANES), 0)
    targets = place + row * finals
    if sides == 2:
        targets = jnp.where(place < finals, targets, targets - finals + (1 - 2 * side) * finals)

    def members(owners, tops, rests, mass):
        parts = []
        for b in range(owners.shape[0]):
            mine = owners[b : b + 1, :] == targets
            top = jnp.where(mine, tops[b : b + 1, :], 0.0)
            rest = jnp.where(mine, rests[b : b + 1, :], 0.0)
            mass = mass + (top + rest)
            parts.append(jnp.concatenate([top, rest], axis=0).astype(BF16))
        return jnp.concatenate(parts, axis=1), mass

    def share(values):
        height = first_chunks // sides
        return values[:height] if sides == 1 else jnp.where(side == 0, values[:height], values[height : 2 * height])

    mass = jnp.zeros((sides * finals, LANES), F32)
    member, mass = members(share(owner_ref[...]), share(weight_top), share(weight_rest), mass)
    height = centres_ref.shape[0] // sides
    table = centres_ref[pl.ds(pl.multiple_of(side * height, height), height), :]
    total = jnp.dot(member, table, preferred_element_type=F32)
    start = 0
    for piece_ref in piece_refs:
        stop = start + piece_rows // LANES
        member, mass = members(
            slot_owner_ref[start:stop, :], placed[start:stop], placed[slot_chunks + start : slot_chunks + stop], mass
        )
        total = total + jnp.dot(member, piece_ref[:piece_rows, :], preferred_element_type=F32)
        start = stop
    total = total[: sides * finals] + total[sides * finals :]
    for k, out_ref in enumerate(out_refs):
        out_ref[:, :features] = total[k * finals : (k + 1) * finals]
        out_ref[:, features:] = mass[k * finals : (k + 1) * finals]


def centre_kernel(*refs):
    part_refs, (out_ref, token_ref) = refs[:-2], refs[-2:]
    token_ref[...] = jnp.zeros(token_ref.shape, F32)
    features = out_ref.shape[1]
    total = sum(ref[:, :features] for ref in part_refs)
    out_ref[...] = total / jnp.sum(sum(ref[:, features:] for ref in part_refs), axis=1, keepdims=True)


def finish_kernel(total_points, near_ref, share_ref, token_ref, relative_ref):
    cost = jnp.sum(share_ref[...], axis=0)[0:1, 0:1]
    relative_ref[...] = near_ref[...] * total_points / cost


def permute(value, masks):
    pairs = [(d, d ^ masks[(d // CORE) % 2]) for d in range(lax.axis_size(AXES))]
    return lax.ppermute(value, AXES, pairs)


def hop(index):
    masks = tuple(zip(*FAN)) + tuple(zip(*SPREAD))
    return masks[index]


def done_after(value, *tokens):
    ready = tokens[0] >= 0.0
    for token in tokens[1:]:
        ready = ready & (token >= 0.0)
    return jnp.where(ready[:, : value.shape[1]], value, jnp.zeros_like(value))


def both_hops(first, second):
    return tuple(a ^ b for a, b in zip(first, second))


def shards(points, centres, picks, assign_pts, cand_assign):
    point_count, feature_count = points.shape
    row_count, col_count = lax.axis_size("row"), lax.axis_size("col")
    device_count = row_count * col_count
    doubling = (row_count, col_count) == (8, 4)
    round_count, sample_count = picks.shape
    cand_count = centres.shape[0] + round_count * sample_count
    cap = min(point_count, sample_count, -(-2 * sample_count // device_count))
    slots = -(-round_count * cap // 16) * 16
    slot_chunks = device_count * slots // LANES
    chunks = round_count * sample_count // LANES
    finals = K_FINAL // row_count
    shape = jax.ShapeDtypeStruct

    token = shape((1, feature_count), F32)
    cand_chunks = cand_count // LANES
    piece_rows = slots * (4 if doubling else device_count)
    block, near_points = local_call(
        functools.partial(pick_kernel, cap, slots),
        (shape((slots + cand_chunks, feature_count), BF16), shape(points.shape, BF16)),
        (picks, points, assign_pts.reshape(-1, LANES)),
        "pick_rows",
        0.8,
        unread=(0, 1, 2),
        scratch=(
            pltpu.VMEM(picks.shape, jnp.int32),
            pltpu.VMEM((point_count // LANES, LANES), jnp.int32),
            pltpu.SemaphoreType.DMA((3,)),
        ),
    )
    owner_rows = cand_assign.reshape(-1, LANES)
    best_shape = shape((8, point_count), F32)
    top_shape = shape((1, point_count), F32)
    held_chunks = slot_chunks // 2 if doubling else slot_chunks
    slot_shapes = (shape((chunks, LANES), jnp.int32), shape((held_chunks, LANES), jnp.int32))
    slot_args = (doubling, cap, slots, device_count, point_count)
    beside = permute(near_points, (CORE, CORE)) if doubling else near_points
    best, norms, scanned = local_call(
        first_scan_kernel, (best_shape, best_shape, token), (near_points, centres), "scan_centres", 1.6
    )

    def next_scan(points, best, start, *pieces):
        cost = 0.2 + 0.8e-3 * piece_rows * len(pieces)
        kernel = functools.partial(next_scan_kernel, piece_rows)
        return local_call(kernel, top_shape, (points, best, start, *pieces), "scan_next", cost)

    near_shapes = (top_shape, shape((device_count, 1, LANES), F32))
    sum_shape = shape((finals, feature_count + LANES), F32)

    def centres_of(parts):
        return local_call(
            centre_kernel, (shape((finals, feature_count), F32), token), parts, "new_centres", 0.5
        )

    if doubling:
        swap = (CORE, CORE)
        near = [block, *(permute(block, m) for m in (hop(0), hop(1), both_hops(hop(0), hop(1))))]
        told = split_counts(sum(join_counts(part[slots:]) for part in near)).astype(BF16)
        own = done_after(jnp.concatenate([part[:slots] for part in near] + [told], axis=0), scanned)
        others = [permute(own, m) for m in (hop(2), hop(3), both_hops(hop(2), hop(3)))]
        best, beside_best, places, slot_owners, scanned = local_call(
            functools.partial(own_scan_kernel, slot_args, piece_rows),
            (best_shape, best_shape, *slot_shapes, token),
            (near_points, beside, best, picks, owner_rows, own),
            "scan_own",
            2.0,
        )
        message, scanned = local_call(
            functools.partial(beside_scan_kernel, piece_rows),
            (shape((point_count // LANES + cand_chunks, LANES), F32), token),
            (beside, beside_best, own, *others),
            "scan_beside",
            1.2,
        )
        answer = permute(message, swap)
        top = next_scan(near_points, best, scanned, *others)
        near, share = local_call(near_kernel, near_shapes, (norms, top, answer), "nearest", 0.5)
        shares = lax.all_to_all(share, AXES, 0, 0)

        def both_sides(near_ref, mine_ref, other_ref, *refs):
            lloyd_kernel(piece_rows, 2, point_count // LANES, (mine_ref, other_ref), *refs)

        def sum_up(*operands):
            keep, give = local_call(both_sides, (sum_shape, sum_shape), operands, "lloyd", 1.8)
            return centres_of((keep, permute(give, swap)))

        def nothing(*operands):
            return jnp.zeros((finals, feature_count), F32), jnp.zeros(token.shape, F32)

        operands = (near, message, answer, owner_rows, places, slot_owners, centres, own, *others)
        new_centres, summed = lax.cond(lax.axis_index("row") < K_FINAL, sum_up, nothing, *operands)
    else:
        places, slot_owners, found = local_call(
            functools.partial(slot_kernel, *slot_args), (*slot_shapes, token), (picks, owner_rows), "slot_owners", 1.0
        )
        counts = lax.psum(join_counts(block[slots:]), AXES)
        table = lax.all_gather(block[:slots], AXES, tiled=True)
        top = next_scan(near_points, best, scanned, table)

        def nearest(norm_ref, top_ref, *refs):
            near_kernel(norm_ref, top_ref, None, *refs)

        near, share = local_call(nearest, near_shapes, (norms, top), "nearest", 0.5)
        shares = lax.psum(share[:1], AXES)

        def one_side(count_ref, *refs):
            lloyd_kernel(piece_rows, 1, 0, (count_ref,), *refs)

        operands = (counts, owner_rows, places, slot_owners, centres, table)
        new_centres, summed = centres_of((local_call(one_side, sum_shape, operands, "lloyd", 1.8),))
    relative = local_call(
        functools.partial(finish_kernel, float(point_count * device_count)),
        shape((1, point_count), F32),
        (near, shares, summed),
        "finish",
        0.6,
    )
    return (relative.reshape(-1), new_centres)


def solution(mesh):
    placed = (P(AXES, None), P(), P(), P(AXES), P())
    return jax.shard_map(
        shards,
        mesh=mesh,
        in_specs=placed,
        out_specs=(P(AXES), P("row", None)),
        check_vma=False,
    )
```

time: 42.3 us -> 41.3 us (0.976)
  Pallas kernels: 15 us -> 11.6 us
  starting transfers between devices: 13.4 us -> 15.9 us
    pallas_call x8 -> x9, Pallas kernels: 15 us -> 11.6 us  [local_call(): pl.pallas_call(body, out_shape=out_shape, in_specs=specs, out_specs=resul...]
    all_to_all x1, starting transfers between devices: 3.91 us -> 5.77 us  [shards(): shares = lax.all_to_all(share, AXES, 0, 0)]
    ppermute x10 -> x9, starting transfers between devices: 9.51 us -> 10.1 us  [permute(): return lax.ppermute(value, AXES, pairs)]
    ppermute x10 -> x9, waiting for transfers between devices: 9.23 us -> 9.57 us  [permute(): return lax.ppermute(value, AXES, pairs)]
  transfers between devices with their start and end apart: 11 -> 10, of which waited for: 8 -> 6; matrix products, arithmetic and copies ran while one was open for 0% -> 0% of each run, Pallas kernels for 27% -> 18%
where the time goes in v4:
time: 41.3 us; the launch traced here: 41.1 us
  starting transfers between devices  15.9 us (38%)
  waiting for transfers between devices  12.7 us (31%)
  Pallas kernels  11.6 us (28%)
  between operations  0.81 us (2%)
    pallas_call x9, Pallas kernels, local_call(): pl.pallas_call(body, out_shape=out_shape, in_specs=specs, out_specs=resul...  11.6 us
    ppermute x9, starting transfers between devices, permute(): return lax.ppermute(value, AXES, pairs)  10.1 us
    ppermute x9, waiting for transfers between devices, permute(): return lax.ppermute(value, AXES, pairs)  9.57 us
    all_to_all x1, starting transfers between devices, shards(): shares = lax.all_to_all(share, AXES, 0, 0)  5.77 us
    all_to_all x1, waiting for transfers between devices, shards(): shares = lax.all_to_all(share, AXES, 0, 0)  3.13 us
  transfers between devices with their start and end apart: 10, of which 6 were waited for; matrix products, arithmetic and copies ran while one was open for 0% of the time, Pallas kernels for 18%

profile of v4, /device:TPU:0, one launch (start us, length us, event | category | flops | bytes accessed | tf_op | source)
XLA Modules:
  0.0 41.1 jit_solution(9859343930037123220)
XLA Ops:
  0.6 1.8 %pick_rows.1 = (bf16[160,256]{1,0:T(8,128)(2,1)S(1)}, bf16[1024,256]{1,0:T(8,128)(2,1)S(1)}) custom-call(s32[2,1024]{1,0:T(2,128)} %refs_3_.1, bf16[1024,256]{1,0:T(8,128)(2,1)} %refs_1_.2, s32[8,128]{1,0:T(8,128)} %bitcast.5), custom_call_target="tpu_custom_call" | custom-call | flops 800000000 | tf_op jit(solution)/shard_map/pick_rows/pallas_call | solution.py:62
  2.5 4.1 %collective-permute-start.2 = (bf16[160,256]{1,0:T(8,128)(2,1)S(1)}, bf16[160,256]{1,0:T(8,128)(2,1)S(1)}, u32[]{:S(2)}, u32[]{:S(2)}) collective-permute-start(bf16[160,256]{1,0:T(8,128)(2,1)S(1)} %get-tuple-element.56), channel_id=1, source_target_pairs={{0,2},{1,3},{2,0},{3,1},{4,28},{5,29},{6,30},{7,31},{8,10},{9,11},... | collective-permute-start | bytes 245768 | tf_op jit(solution)/shard_map/ppermute | solution.py:340
  6.6 1.3 %collective-permute-start.3 = (bf16[160,256]{1,0:T(8,128)(2,1)S(1)}, bf16[160,256]{1,0:T(8,128)(2,1)S(1)}, u32[]{:S(2)}, u32[]{:S(2)}) collective-permute-start(bf16[160,256]{1,0:T(8,128)(2,1)S(1)} %get-tuple-element.56), channel_id=1, source_target_pairs={{0,3},{1,2},{2,1},{3,0},{4,20},{5,21},{6,22},{7,23},{8,11},{9,10},... | collective-permute-start | bytes 245768 | tf_op jit(solution)/shard_map/ppermute | solution.py:340
  7.9 0.2 collective-permute-start.4
  8.2 1.7 %scan_centres.1 = (f32[8,1024]{1,0:T(8,128)S(1)}, f32[8,1024]{1,0:T(8,128)S(1)}, f32[1,256]{1,0:T(1,128)S(1)}) custom-call(bf16[1024,256]{1,0:T(8,128)(2,1)S(1)} %get-tuple-element.52.refs_0_, bf16[2048,256]{1,0:T(8,128)(2,1)S(1)} %copy-done.1), custom_call_target="tpu_custom_call" | custom-call | flops 1600000000 | tf_op jit(solution)/shard_map/scan_centres/pallas_call | solution.py:62
  10.0 3.3 %collective-permute-done.4 = bf16[160,256]{1,0:T(8,128)(2,1)S(1)} collective-permute-done((bf16[160,256]{1,0:T(8,128)(2,1)S(1)}, bf16[160,256]{1,0:T(8,128)(2,1)S(1)}, u32[]{:S(2)}, u32[]{:S(2)}) %collective-permute-start.4) | collective-permute-done | bytes 81952 | tf_op jit(solution)/shard_map/ppermute | solution.py:340
  13.4 2.5 %collective-permute-start.5 = (bf16[544,256]{1,0:T(8,128)(2,1)S(1)}, bf16[544,256]{1,0:T(8,128)(2,1)S(1)}, u32[]{:S(2)}, u32[]{:S(2)}) collective-permute-start(bf16[544,256]{1,0:T(8,128)(2,1)S(1)} %broadcast_select_fusion.refs_5_.refs_2_), channel_id=1, source_target_pairs={{0,24},{1,25},{2,26},{3,27},{4,6},{5,7},{6,4},{7,5},{8,16},{9,17},... | collective-permute-start | bytes 835592 | tf_op jit(solution)/shard_map/ppermute | solution.py:340
  16.0 0.5 %collective-permute-start.6 = (bf16[544,256]{1,0:T(8,128)(2,1)S(1)}, bf16[544,256]{1,0:T(8,128)(2,1)S(1)}, u32[]{:S(2)}, u32[]{:S(2)}) collective-permute-start(bf16[544,256]{1,0:T(8,128)(2,1)S(1)} %broadcast_select_fusion.refs_5_.refs_2_), channel_id=1, source_target_pairs={{0,16},{1,17},{2,18},{3,19},{4,7},{5,6},{6,5},{7,4},{8,24},{9,25},... | collective-permute-start | bytes 835592 | tf_op jit(solution)/shard_map/ppermute | solution.py:340
  16.5 0.5 %collective-permute-start.7 = (bf16[544,256]{1,0:T(8,128)(2,1)S(1)}, bf16[544,256]{1,0:T(8,128)(2,1)S(1)}, u32[]{:S(2)}, u32[]{:S(2)}) collective-permute-start(bf16[544,256]{1,0:T(8,128)(2,1)S(1)} %broadcast_select_fusion.refs_5_.refs_2_), channel_id=1, source_target_pairs={{0,8},{1,9},{2,10},{3,11},{4,5},{5,4},{6,7},{7,6},{8,0},{9,1},{10,... | collective-permute-start | bytes 835592 | tf_op jit(solution)/shard_map/ppermute | solution.py:340
  17.0 1.9 %scan_own.1 = (f32[8,1024]{1,0:T(8,128)S(1)}, f32[8,1024]{1,0:T(8,128)S(1)}, s32[16,128]{1,0:T(8,128)S(1)}, s32[16,128]{1,0:T(8,128)S(1)}, f32[1,256]{1,0:T(1,128)}) custom-call(bf16[1024,256]{1,0:T(8,128)(2,1)S(1)} %get-tuple-element.52.refs_0_, bf16[1024,256]{1,0:T(8,128)(2,1)S(1)} %collective-permute-done.1.refs_1_.refs_0_, ...), custom_call_target="tpu_custom_call" | custom-call | flops 2000000000 | tf_op jit(solution)/shard_map/scan_own/pallas_call | solution.py:62
  18.9 2.1 %collective-permute-done.5.refs_3_ = bf16[544,256]{1,0:T(8,128)(2,1)S(1)} collective-permute-done((bf16[544,256]{1,0:T(8,128)(2,1)S(1)}, bf16[544,256]{1,0:T(8,128)(2,1)S(1)}, u32[]{:S(2)}, u32[]{:S(2)}) %collective-permute-start.5) | collective-permute-done | bytes 278560 | tf_op jit(solution)/shard_map/ppermute | solution.py:340
  21.1 2.9 %collective-permute-done.6.refs_4_ = bf16[544,256]{1,0:T(8,128)(2,1)S(1)} collective-permute-done((bf16[544,256]{1,0:T(8,128)(2,1)S(1)}, bf16[544,256]{1,0:T(8,128)(2,1)S(1)}, u32[]{:S(2)}, u32[]{:S(2)}) %collective-permute-start.6) | collective-permute-done | bytes 278560 | tf_op jit(solution)/shard_map/ppermute | solution.py:340
  24.0 1.1 %scan_beside.1 = (f32[40,128]{1,0:T(8,128)S(1)}, f32[1,256]{1,0:T(1,128)S(1)}) custom-call(bf16[1024,256]{1,0:T(8,128)(2,1)S(1)} %collective-permute-done.1.refs_1_.refs_0_, f32[8,1024]{1,0:T(8,128)S(1)} %get-tuple-element.58.refs_1_, bf16[544,256]{1,0:T(8,128)(2,1)S(1)} %broadcast_select_fusion.refs_5_.refs_2_, ...), custom_call_target="tpu_custom_call" | custom-call | flops 1200000000 | tf_op jit(solution)/shard_map/scan_beside/pallas_call | solution.py:62
  25.1 0.6 %collective-permute-start.8 = (f32[40,128]{1,0:T(8,128)S(1)}, f32[40,128]{1,0:T(8,128)S(1)}, u32[]{:S(2)}, u32[]{:S(2)}) collective-permute-start(f32[40,128]{1,0:T(8,128)S(1)} %get-tuple-element.60), channel_id=1, source_target_pairs={{0,4},{1,5},{2,6},{3,7},{4,0},{5,1},{6,2},{7,3},{8,12},{9,13},{10,... | collective-permute-start | bytes 61448 | tf_op jit(solution)/shard_map/ppermute | solution.py:340
  25.7 1.1 %scan_next.1.refs_1_ = f32[1,1024]{1,0:T(1,128)S(1)} custom-call(bf16[1024,256]{1,0:T(8,128)(2,1)S(1)} %get-tuple-element.52.refs_0_, f32[8,1024]{1,0:T(8,128)S(1)} %get-tuple-element.57.refs_1_, f32[1,256]{1,0:T(1,128)S(1)} %get-tuple-element.59.refs_2_, bf16[544,256]{1,0:T(8,128)(2,1)S(1)} %collective-permute-done.5.refs_3_, ...), custom_call_target="tpu_custom_call" | custom-call | flops 1428800000 | tf_op jit(solution)/shard_map/scan_next/pallas_call | solution.py:62
  26.8 0.7 %nearest.1 = (f32[1,1024]{1,0:T(1,128)S(1)}, f32[32,1,128]{2,1,0:T(1,128)}) custom-call(f32[8,1024]{1,0:T(8,128)S(1)} %get-tuple-element.53.refs_0_, f32[1,1024]{1,0:T(1,128)S(1)} %scan_next.1.refs_1_, f32[40,128]{1,0:T(8,128)S(1)} %collective-permute-done.8.refs_2_), custom_call_target="tpu_custom_call" | custom-call | flops 500000000 | tf_op jit(solution)/shard_map/nearest/pallas_call | solution.py:62
  27.5 5.8 %all-to-all-start = ((f32[32,1,128]{2,1,0:T(1,128)}), f32[32,1,128]{2,1,0:T(1,128)S(1)}, u32[]{:S(2)}, u32[]{:S(2)}) async-start(f32[32,1,128]{2,1,0:T(1,128)} %get-tuple-element.62), calls=%async_computation | async-start | bytes 32768 | tf_op jit(solution)/shard_map/all_to_all | solution.py:436
  33.3 4.0 %conditional.1 = ((f32[128,256]{1,0:T(8,128)}, f32[1,256]{1,0:T(1,128)S(1)})) conditional(s32[]{:T(128)} %convert_element_type.20, () %tuple.15, (f32[1,1024]{1,0:T(1,128)S(1)}, f32[40,128]{1,0:T(8,128)S(1)}, f32[40,128]{1,0:T(8,128)S(1)}, s32[32,128]{1,0:T(8,128)S(1)}, s32[16,128]{1,0:T(8,128)S(1)}, /*index=5*/s32[16,128]{1,0:T(8,128)S(1)}, ...), branch_computations={%region_0.1_spmd, %region_1.2_spmd} | conditional | flops 2300000000 | bytes 786480 | solution.py:449
  33.3 1.8 %lloyd.1 = (f32[128,384]{1,0:T(8,128)S(1)}, f32[128,384]{1,0:T(8,128)S(1)}) custom-call(f32[1,1024]{1,0:T(1,128)S(1)} %get-tuple-element.22.refs_0_, f32[40,128]{1,0:T(8,128)S(1)} %get-tuple-element.23.refs_1_, f32[40,128]{1,0:T(8,128)S(1)} %get-tuple-element.24.refs_2_, s32[32,128]{1,0:T(8,128)S(1)} %get-tuple-element.25.refs_3_, ...), custom_call_target="tpu_custom_call" | custom-call | flops 1800000000 | tf_op jit(solution)/shard_map/cond/branch_1_fun/lloyd/pallas_call | solution.py:62
  35.1 0.3 collective-permute-start
  35.4 1.2 %collective-permute-done.refs_1_ = f32[128,384]{1,0:T(8,128)S(1)} collective-permute-done((f32[128,384]{1,0:T(8,128)S(1)}, f32[128,384]{1,0:T(8,128)S(1)}, u32[]{:S(2)}, u32[]{:S(2)}) %collective-permute-start) | collective-permute-done | bytes 196640 | tf_op jit(solution)/shard_map/cond/branch_1_fun/ppermute | solution.py:340
  36.6 0.8 %new_centres.1 = (f32[128,256]{1,0:T(8,128)}, f32[1,256]{1,0:T(1,128)S(1)}) custom-call(f32[128,384]{1,0:T(8,128)S(1)} %get-tuple-element.33.refs_0_, f32[128,384]{1,0:T(8,128)S(1)} %collective-permute-done.refs_1_), custom_call_target="tpu_custom_call" | custom-call | flops 500000000 | tf_op jit(solution)/shard_map/cond/branch_1_fun/new_centres/pallas_call | solution.py:62
  37.3 3.1 %all-to-all-done.refs_1_ = f32[32,1,128]{2,1,0:T(1,128)S(1)} async-done(((f32[32,1,128]{2,1,0:T(1,128)}), f32[32,1,128]{2,1,0:T(1,128)S(1)}, u32[]{:S(2)}, u32[]{:S(2)}) %all-to-all-start) | async-done | bytes 16416 | tf_op jit(solution)/shard_map/all_to_all | solution.py:436
  40.4 0.7 %finish.1 = f32[1,1024]{1,0:T(1,128)} custom-call(f32[1,1024]{1,0:T(1,128)S(1)} %get-tuple-element.61.refs_0_, f32[32,1,128]{2,1,0:T(1,128)S(1)} %all-to-all-done.refs_1_, f32[1,256]{1,0:T(1,128)S(1)} %get-tuple-element.65.refs_2_), custom_call_target="tpu_custom_call" | custom-call | flops 600000000 | tf_op jit(solution)/shard_map/finish/pallas_call | solution.py:62
  (25 shorter events, 0.3 us)
Async XLA Ops:
  0.6 7.5 %copy-start.1 = (bf16[2048,256]{1,0:T(8,128)(2,1)S(1)}, bf16[2048,256]{1,0:T(8,128)(2,1)}, u32[]{:S(2)}) copy-start(bf16[2048,256]{1,0:T(8,128)(2,1)} %refs_1_.3) | copy-start | bytes 3145732
  2.5 10.8 %collective-permute-start.2 = (bf16[160,256]{1,0:T(8,128)(2,1)S(1)}, bf16[160,256]{1,0:T(8,128)(2,1)S(1)}, u32[]{:S(2)}, u32[]{:S(2)}) collective-permute-start(bf16[160,256]{1,0:T(8,128)(2,1)S(1)} %get-tuple-element.56), channel_id=1, source_target_pairs={{0,2},{1,3},{2,0},{3,1},{4,28},{5,29},{6,30},{7,31},{8,10},{9,11},... | collective-permute-start | bytes 245768 | tf_op jit(solution)/shard_map/ppermute | solution.py:340
  6.6 6.7 %collective-permute-start.3 = (bf16[160,256]{1,0:T(8,128)(2,1)S(1)}, bf16[160,256]{1,0:T(8,128)(2,1)S(1)}, u32[]{:S(2)}, u32[]{:S(2)}) collective-permute-start(bf16[160,256]{1,0:T(8,128)(2,1)S(1)} %get-tuple-element.56), channel_id=1, source_target_pairs={{0,3},{1,2},{2,1},{3,0},{4,20},{5,21},{6,22},{7,23},{8,11},{9,10},... | collective-permute-start | bytes 245768 | tf_op jit(solution)/shard_map/ppermute | solution.py:340
  7.9 5.3 %collective-permute-start.4 = (bf16[160,256]{1,0:T(8,128)(2,1)S(1)}, bf16[160,256]{1,0:T(8,128)(2,1)S(1)}, u32[]{:S(2)}, u32[]{:S(2)}) collective-permute-start(bf16[160,256]{1,0:T(8,128)(2,1)S(1)} %get-tuple-element.56), channel_id=1, source_target_pairs={{0,1},{1,0},{2,3},{3,2},{4,12},{5,13},{6,14},{7,15},{8,9},{9,8},{1... | collective-permute-start | bytes 245768 | tf_op jit(solution)/shard_map/ppermute | solution.py:340
  8.1 8.8 %collective-permute-start.1 = (bf16[1024,256]{1,0:T(8,128)(2,1)S(1)}, bf16[1024,256]{1,0:T(8,128)(2,1)S(1)}, u32[]{:S(2)}, u32[]{:S(2)}) collective-permute-start(bf16[1024,256]{1,0:T(8,128)(2,1)S(1)} %get-tuple-element.52.refs_0_), channel_id=1, source_target_pairs={{0,4},{1,5},{2,6},{3,7},{4,0},{5,1},{6,2},{7,3},{8,12},{9,13},{10,... | collective-permute-start | bytes 1572872 | tf_op jit(solution)/shard_map/ppermute | solution.py:340
  13.4 3.6 %copy-start = (s32[2,1024]{1,0:T(2,128)S(1)}, s32[2,1024]{1,0:T(2,128)}, u32[]{:S(2)}) copy-start(s32[2,1024]{1,0:T(2,128)} %refs_3_.1) | copy-start | bytes 24580
  13.4 3.6 %copy-start.2 = (s32[4096,1]{0,1:T(1,128)S(1)}, s32[4096,1]{0,1:T(1,128)}, u32[]{:S(2)}) copy-start(s32[4096,1]{0,1:T(1,128)} %param.11) | copy-start | bytes 49156
  13.4 7.6 %collective-permute-start.5 = (bf16[544,256]{1,0:T(8,128)(2,1)S(1)}, bf16[544,256]{1,0:T(8,128)(2,1)S(1)}, u32[]{:S(2)}, u32[]{:S(2)}) collective-permute-start(bf16[544,256]{1,0:T(8,128)(2,1)S(1)} %broadcast_select_fusion.refs_5_.refs_2_), channel_id=1, source_target_pairs={{0,24},{1,25},{2,26},{3,27},{4,6},{5,7},{6,4},{7,5},{8,16},{9,17},... | collective-permute-start | bytes 835592 | tf_op jit(solution)/shard_map/ppermute | solution.py:340
  16.0 8.0 %collective-permute-start.6 = (bf16[544,256]{1,0:T(8,128)(2,1)S(1)}, bf16[544,256]{1,0:T(8,128)(2,1)S(1)}, u32[]{:S(2)}, u32[]{:S(2)}) collective-permute-start(bf16[544,256]{1,0:T(8,128)(2,1)S(1)} %broadcast_select_fusion.refs_5_.refs_2_), channel_id=1, source_target_pairs={{0,16},{1,17},{2,18},{3,19},{4,7},{5,6},{6,5},{7,4},{8,24},{9,25},... | collective-permute-start | bytes 835592 | tf_op jit(solution)/shard_map/ppermute | solution.py:340
  16.5 7.6 %collective-permute-start.7 = (bf16[544,256]{1,0:T(8,128)(2,1)S(1)}, bf16[544,256]{1,0:T(8,128)(2,1)S(1)}, u32[]{:S(2)}, u32[]{:S(2)}) collective-permute-start(bf16[544,256]{1,0:T(8,128)(2,1)S(1)} %broadcast_select_fusion.refs_5_.refs_2_), channel_id=1, source_target_pairs={{0,8},{1,9},{2,10},{3,11},{4,5},{5,4},{6,7},{7,6},{8,0},{9,1},{10,... | collective-permute-start | bytes 835592 | tf_op jit(solution)/shard_map/ppermute | solution.py:340
  25.1 1.7 %collective-permute-start.8 = (f32[40,128]{1,0:T(8,128)S(1)}, f32[40,128]{1,0:T(8,128)S(1)}, u32[]{:S(2)}, u32[]{:S(2)}) collective-permute-start(f32[40,128]{1,0:T(8,128)S(1)} %get-tuple-element.60), channel_id=1, source_target_pairs={{0,4},{1,5},{2,6},{3,7},{4,0},{5,1},{6,2},{7,3},{8,12},{9,13},{10,... | collective-permute-start | bytes 61448 | tf_op jit(solution)/shard_map/ppermute | solution.py:340
  27.5 12.9 %all-to-all-start = ((f32[32,1,128]{2,1,0:T(1,128)}), f32[32,1,128]{2,1,0:T(1,128)S(1)}, u32[]{:S(2)}, u32[]{:S(2)}) async-start(f32[32,1,128]{2,1,0:T(1,128)} %get-tuple-element.62), calls=%async_computation | async-start | bytes 32768 | tf_op jit(solution)/shard_map/all_to_all | solution.py:436
  35.1 1.5 %collective-permute-start = (f32[128,384]{1,0:T(8,128)S(1)}, f32[128,384]{1,0:T(8,128)S(1)}, u32[]{:S(2)}, u32[]{:S(2)}) collective-permute-start(f32[128,384]{1,0:T(8,128)S(1)} %get-tuple-element.34), channel_id=1, source_target_pairs={{0,4},{1,5},{2,6},{3,7},{4,0},{5,1},{6,2},{7,3},{8,12},{9,13},{10,... | collective-permute-start | bytes 589832 | tf_op jit(solution)/shard_map/cond/branch_1_fun/ppermute | solution.py:340

commit v5 on v4

--- a/solution.py
+++ b/solution.py
@@ -16,7 +16,7 @@
 BF16 = jnp.bfloat16
 
 CORE = 4
-FAN = ((2, 3), (24, 16))
+FAN = ((1, 2), (8, 16))
 SPREAD = ((24, 16), (2, 3))
 
 
@@ -212,8 +212,7 @@
     return lax.fori_loop(0, rows // step, visit, best)
 
 
-def first_scan_kernel(points_ref, centres_ref, best_ref, norm_ref, token_ref):
-    token_ref[...] = jnp.zeros(token_ref.shape, F32)
+def first_scan_kernel(points_ref, centres_ref, best_ref, norm_ref):
     best_ref[...] = scan_table(points_ref, centres_ref, 0, centres_ref.shape[0], jnp.full(best_ref.shape, -jnp.inf, F32))
     wide = points_ref[...].astype(F32)
     square = wide * wide
@@ -229,12 +228,15 @@
     return best
 
 
-def own_scan_kernel(slot_args, rows, points_ref, beside_ref, best_ref, picks_ref, owner_ref, piece_ref, *refs):
-    next_ref, beside_best_ref, place_ref, slot_owner_ref, token_ref = refs
-    next_ref[...] = scan_pieces(points_ref, [piece_ref], rows, best_ref[...])
-    lowest = jnp.full(beside_best_ref.shape, -jnp.inf, F32)
-    beside_best_ref[...] = scan_pieces(beside_ref, [piece_ref], rows, lowest)
+def own_scan_kernel(slot_args, rows, points_ref, centres_ref, picks_ref, owner_ref, piece_ref, *refs):
+    best_ref, norm_ref, place_ref, slot_owner_ref, token_ref = refs
+    first_scan_kernel(points_ref, centres_ref, best_ref, norm_ref)
+    best_ref[...] = scan_pieces(points_ref, [piece_ref], rows, best_ref[...])
     slot_kernel(*slot_args, picks_ref, owner_ref, place_ref, slot_owner_ref, token_ref)
+
+
+def start_scan_kernel(rows, beside_ref, piece_ref, best_ref):
+    best_ref[...] = scan_pieces(beside_ref, [piece_ref], rows, jnp.full(best_ref.shape, -jnp.inf, F32))
 
 
 def beside_scan_kernel(rows, beside_ref, best_ref, *refs):
@@ -392,11 +394,6 @@
     held_chunks = slot_chunks // 2 if doubling else slot_chunks
     slot_shapes = (shape((chunks, LANES), jnp.int32), shape((held_chunks, LANES), jnp.int32))
     slot_args = (doubling, cap, slots, device_count, point_count)
-    beside = permute(near_points, (CORE, CORE)) if doubling else near_points
-    best, norms, scanned = local_call(
-        first_scan_kernel, (best_shape, best_shape, token), (near_points, centres), "scan_centres", 1.6
-    )
-
     def next_scan(points, best, start, *pieces):
         cost = 0.2 + 0.8e-3 * piece_rows * len(pieces)
         kernel = functools.partial(next_scan_kernel, piece_rows)
@@ -414,14 +411,18 @@
         swap = (CORE, CORE)
         near = [block, *(permute(block, m) for m in (hop(0), hop(1), both_hops(hop(0), hop(1))))]
         told = split_counts(sum(join_counts(part[slots:]) for part in near)).astype(BF16)
-        own = done_after(jnp.concatenate([part[:slots] for part in near] + [told], axis=0), scanned)
+        own = jnp.concatenate([part[:slots] for part in near] + [told], axis=0)
         others = [permute(own, m) for m in (hop(2), hop(3), both_hops(hop(2), hop(3)))]
-        best, beside_best, places, slot_owners, scanned = local_call(
+        best, norms, places, slot_owners, scanned = local_call(
             functools.partial(own_scan_kernel, slot_args, piece_rows),
             (best_shape, best_shape, *slot_shapes, token),
-            (near_points, beside, best, picks, owner_rows, own),
+            (near_points, centres, picks, owner_rows, own),
             "scan_own",
-            2.0,
+            3.0,
+        )
+        beside = permute(near_points, swap)
+        beside_best = local_call(
+            functools.partial(start_scan_kernel, piece_rows), best_shape, (beside, own), "scan_start", 0.5
         )
         message, scanned = local_call(
             functools.partial(beside_scan_kernel, piece_rows),
@@ -448,12 +449,15 @@
         operands = (near, message, answer, owner_rows, places, slot_owners, centres, own, *others)
         new_centres, summed = lax.cond(lax.axis_index("row") < K_FINAL, sum_up, nothing, *operands)
     else:
+        best, norms = local_call(
+            first_scan_kernel, (best_shape, best_shape), (near_points, centres), "scan_centres", 1.6
+        )
         places, slot_owners, found = local_call(
             functools.partial(slot_kernel, *slot_args), (*slot_shapes, token), (picks, owner_rows), "slot_owners", 1.0
         )
         counts = lax.psum(join_counts(block[slots:]), AXES)
         table = lax.all_gather(block[:slots], AXES, tiled=True)
-        top = next_scan(near_points, best, scanned, table)
+        top = next_scan(near_points, best, found, table)
 
         def nearest(norm_ref, top_ref, *refs):
             near_kernel(norm_ref, top_ref, None, *refs)

time: 41.3 us -> 39.9 us (0.966)
  starting transfers between devices: 15.9 us -> 14.9 us
    all_to_all x1, starting transfers between devices: 5.77 us -> 5.12 us  [shards(): shares = lax.all_to_all(share, AXES, 0, 0)]
  transfers between devices with their start and end apart: 10 -> 10, of which waited for: 6 -> 7; matrix products, arithmetic and copies ran while one was open for 0% -> 0% of each run, Pallas kernels for 18% -> 18%
where the time goes in v5:
time: 39.9 us; the launch traced here: 39.7 us
  starting transfers between devices  14.9 us (37%)
  waiting for transfers between devices  12.3 us (31%)
  Pallas kernels  11.6 us (29%)
  between operations  0.78 us (2%)
    pallas_call x9, Pallas kernels, local_call(): pl.pallas_call(body, out_shape=out_shape, in_specs=specs, out_specs=resul...  11.6 us
    ppermute x9, starting transfers between devices, permute(): return lax.ppermute(value, AXES, pairs)  9.81 us
    ppermute x9, waiting for transfers between devices, permute(): return lax.ppermute(value, AXES, pairs)  9.16 us
    all_to_all x1, starting transfers between devices, shards(): shares = lax.all_to_all(share, AXES, 0, 0)  5.12 us
    all_to_all x1, waiting for transfers between devices, shards(): shares = lax.all_to_all(share, AXES, 0, 0)  3.12 us
  transfers between devices with their start and end apart: 10, of which 7 were waited for; matrix products, arithmetic and copies ran while one was open for 0% of the time, Pallas kernels for 18%

profile of v5, /device:TPU:0, one launch (start us, length us, event | category | flops | bytes accessed | tf_op | source)
XLA Modules:
  0.0 39.7 jit_solution(5389204591427995686)
XLA Ops:
  0.6 1.8 %pick_rows.1 = (bf16[160,256]{1,0:T(8,128)(2,1)S(1)}, bf16[1024,256]{1,0:T(8,128)(2,1)S(1)}) custom-call(s32[2,1024]{1,0:T(2,128)} %refs_2_.1, bf16[1024,256]{1,0:T(8,128)(2,1)} %refs_1_.2, s32[8,128]{1,0:T(8,128)} %bitcast.5), custom_call_target="tpu_custom_call" | custom-call | flops 800000000 | tf_op jit(solution)/shard_map/pick_rows/pallas_call | solution.py:62
  2.5 5.1 %collective-permute-start.3 = (bf16[160,256]{1,0:T(8,128)(2,1)S(1)}, bf16[160,256]{1,0:T(8,128)(2,1)S(1)}, u32[]{:S(2)}, u32[]{:S(2)}) collective-permute-start(bf16[160,256]{1,0:T(8,128)(2,1)S(1)} %get-tuple-element.50), channel_id=1, source_target_pairs={{0,3},{1,2},{2,1},{3,0},{4,28},{5,29},{6,30},{7,31},{8,11},{9,10},... | collective-permute-start | bytes 245768 | tf_op jit(solution)/shard_map/ppermute | solution.py:342
  7.6 0.6 %collective-permute-start.1 = (bf16[160,256]{1,0:T(8,128)(2,1)S(1)}, bf16[160,256]{1,0:T(8,128)(2,1)S(1)}, u32[]{:S(2)}, u32[]{:S(2)}) collective-permute-start(bf16[160,256]{1,0:T(8,128)(2,1)S(1)} %get-tuple-element.50), channel_id=1, source_target_pairs={{0,1},{1,0},{2,3},{3,2},{4,12},{5,13},{6,14},{7,15},{8,9},{9,8},{1... | collective-permute-start | bytes 245768 | tf_op jit(solution)/shard_map/ppermute | solution.py:342
  8.2 1.9 %collective-permute-done.3 = bf16[160,256]{1,0:T(8,128)(2,1)S(1)} collective-permute-done((bf16[160,256]{1,0:T(8,128)(2,1)S(1)}, bf16[160,256]{1,0:T(8,128)(2,1)S(1)}, u32[]{:S(2)}, u32[]{:S(2)}) %collective-permute-start.3) | collective-permute-done | bytes 81952 | tf_op jit(solution)/shard_map/ppermute | solution.py:342
  10.1 2.8 %collective-permute-done.2 = bf16[160,256]{1,0:T(8,128)(2,1)S(1)} collective-permute-done((bf16[160,256]{1,0:T(8,128)(2,1)S(1)}, bf16[160,256]{1,0:T(8,128)(2,1)S(1)}, u32[]{:S(2)}, u32[]{:S(2)}) %collective-permute-start.2) | collective-permute-done | bytes 81952 | tf_op jit(solution)/shard_map/ppermute | solution.py:342
  13.1 2.8 %collective-permute-start.5 = (bf16[544,256]{1,0:T(8,128)(2,1)S(1)}, bf16[544,256]{1,0:T(8,128)(2,1)S(1)}, u32[]{:S(2)}, u32[]{:S(2)}) collective-permute-start(bf16[544,256]{1,0:T(8,128)(2,1)S(1)} %maximum_dynamic-update-slice_fusion.refs_4_.refs_1_.refs_2_), channel_id=1, source_target_pairs={{0,24},{1,25},{2,26},{3,27},{4,6},{5,7},{6,4},{7,5},{8,16},{9,17},... | collective-permute-start | bytes 835592 | tf_op jit(solution)/shard_map/ppermute | solution.py:342
  15.9 0.5 %collective-permute-start.6 = (bf16[544,256]{1,0:T(8,128)(2,1)S(1)}, bf16[544,256]{1,0:T(8,128)(2,1)S(1)}, u32[]{:S(2)}, u32[]{:S(2)}) collective-permute-start(bf16[544,256]{1,0:T(8,128)(2,1)S(1)} %maximum_dynamic-update-slice_fusion.refs_4_.refs_1_.refs_2_), channel_id=1, source_target_pairs={{0,16},{1,17},{2,18},{3,19},{4,7},{5,6},{6,5},{7,4},{8,24},{9,25},... | collective-permute-start | bytes 835592 | tf_op jit(solution)/shard_map/ppermute | solution.py:342
  16.4 0.2 collective-permute-start.7
  16.6 3.2 %scan_own.1 = (f32[8,1024]{1,0:T(8,128)S(1)}, f32[8,1024]{1,0:T(8,128)S(1)}, s32[16,128]{1,0:T(8,128)S(1)}, s32[16,128]{1,0:T(8,128)S(1)}, f32[1,256]{1,0:T(1,128)}) custom-call(bf16[1024,256]{1,0:T(8,128)(2,1)S(1)} %get-tuple-element.49.refs_0_, bf16[2048,256]{1,0:T(8,128)(2,1)S(1)} %copy-done.1, s32[2,1024]{1,0:T(2,128)S(1)} %copy-done, ...), custom_call_target="tpu_custom_call" | custom-call | flops 3000000000 | tf_op jit(solution)/shard_map/scan_own/pallas_call | solution.py:62
  19.9 0.5 %scan_start.1.refs_1_ = f32[8,1024]{1,0:T(8,128)S(1)} custom-call(bf16[1024,256]{1,0:T(8,128)(2,1)S(1)} %collective-permute-done.4.refs_0_, bf16[544,256]{1,0:T(8,128)(2,1)S(1)} %maximum_dynamic-update-slice_fusion.refs_4_.refs_1_.refs_2_), custom_call_target="tpu_custom_call" | custom-call | flops 500000000 | tf_op jit(solution)/shard_map/scan_start/pallas_call | solution.py:62
  20.4 0.3 collective-permute-done.5.refs_3_
  20.7 2.9 %collective-permute-done.6.refs_4_ = bf16[544,256]{1,0:T(8,128)(2,1)S(1)} collective-permute-done((bf16[544,256]{1,0:T(8,128)(2,1)S(1)}, bf16[544,256]{1,0:T(8,128)(2,1)S(1)}, u32[]{:S(2)}, u32[]{:S(2)}) %collective-permute-start.6) | collective-permute-done | bytes 278560 | tf_op jit(solution)/shard_map/ppermute | solution.py:342
  23.7 1.1 %scan_beside.1 = (f32[40,128]{1,0:T(8,128)S(1)}, f32[1,256]{1,0:T(1,128)S(1)}) custom-call(bf16[1024,256]{1,0:T(8,128)(2,1)S(1)} %collective-permute-done.4.refs_0_, f32[8,1024]{1,0:T(8,128)S(1)} %scan_start.1.refs_1_, bf16[544,256]{1,0:T(8,128)(2,1)S(1)} %maximum_dynamic-update-slice_fusion.refs_4_.refs_1_.refs_2_, ...), custom_call_target="tpu_custom_call" | custom-call | flops 1200000000 | tf_op jit(solution)/shard_map/scan_beside/pallas_call | solution.py:62
  24.7 0.2 collective-permute-start.8
  24.9 1.1 %scan_next.1.refs_1_ = f32[1,1024]{1,0:T(1,128)S(1)} custom-call(bf16[1024,256]{1,0:T(8,128)(2,1)S(1)} %get-tuple-element.49.refs_0_, f32[8,1024]{1,0:T(8,128)S(1)} %get-tuple-element.52.refs_1_, f32[1,256]{1,0:T(1,128)S(1)} %get-tuple-element.53.refs_2_, bf16[544,256]{1,0:T(8,128)(2,1)S(1)} %collective-permute-done.5.refs_3_, ...), custom_call_target="tpu_custom_call" | custom-call | flops 1428800000 | tf_op jit(solution)/shard_map/scan_next/pallas_call | solution.py:62
  26.0 0.7 %nearest.1 = (f32[1,1024]{1,0:T(1,128)S(1)}, f32[32,1,128]{2,1,0:T(1,128)}) custom-call(f32[8,1024]{1,0:T(8,128)S(1)} %get-tuple-element.51.refs_0_, f32[1,1024]{1,0:T(1,128)S(1)} %scan_next.1.refs_1_, f32[40,128]{1,0:T(8,128)S(1)} %collective-permute-done.8.refs_2_), custom_call_target="tpu_custom_call" | custom-call | flops 500000000 | tf_op jit(solution)/shard_map/nearest/pallas_call | solution.py:62
  26.7 5.1 %all-to-all-start = ((f32[32,1,128]{2,1,0:T(1,128)}), f32[32,1,128]{2,1,0:T(1,128)S(1)}, u32[]{:S(2)}, u32[]{:S(2)}) async-start(f32[32,1,128]{2,1,0:T(1,128)} %get-tuple-element.56), calls=%async_computation | async-start | bytes 32768 | tf_op jit(solution)/shard_map/all_to_all | solution.py:437
  31.8 4.0 %conditional.1 = ((f32[128,256]{1,0:T(8,128)}, f32[1,256]{1,0:T(1,128)S(1)})) conditional(s32[]{:T(128)} %convert_element_type.20, () %tuple.15, (f32[1,1024]{1,0:T(1,128)S(1)}, f32[40,128]{1,0:T(8,128)S(1)}, f32[40,128]{1,0:T(8,128)S(1)}, s32[32,128]{1,0:T(8,128)S(1)}, s32[16,128]{1,0:T(8,128)S(1)}, /*index=5*/s32[16,128]{1,0:T(8,128)S(1)}, ...), branch_computations={%region_0.0_spmd, %region_1.0_spmd} | conditional | flops 2300000000 | bytes 786480 | solution.py:450
  31.9 1.8 %lloyd.1 = (f32[128,384]{1,0:T(8,128)S(1)}, f32[128,384]{1,0:T(8,128)S(1)}) custom-call(f32[1,1024]{1,0:T(1,128)S(1)} %get-tuple-element.22.refs_0_, f32[40,128]{1,0:T(8,128)S(1)} %get-tuple-element.23.refs_1_, f32[40,128]{1,0:T(8,128)S(1)} %get-tuple-element.24.refs_2_, s32[32,128]{1,0:T(8,128)S(1)} %get-tuple-element.25.refs_3_, ...), custom_call_target="tpu_custom_call" | custom-call | flops 1800000000 | tf_op jit(solution)/shard_map/cond/branch_1_fun/lloyd/pallas_call | solution.py:62
  33.6 0.3 collective-permute-start
  33.9 1.2 %collective-permute-done.refs_1_ = f32[128,384]{1,0:T(8,128)S(1)} collective-permute-done((f32[128,384]{1,0:T(8,128)S(1)}, f32[128,384]{1,0:T(8,128)S(1)}, u32[]{:S(2)}, u32[]{:S(2)}) %collective-permute-start) | collective-permute-done | bytes 196640 | tf_op jit(solution)/shard_map/cond/branch_1_fun/ppermute | solution.py:342
  35.1 0.8 %new_centres.1 = (f32[128,256]{1,0:T(8,128)}, f32[1,256]{1,0:T(1,128)S(1)}) custom-call(f32[128,384]{1,0:T(8,128)S(1)} %get-tuple-element.33.refs_0_, f32[128,384]{1,0:T(8,128)S(1)} %collective-permute-done.refs_1_), custom_call_target="tpu_custom_call" | custom-call | flops 500000000 | tf_op jit(solution)/shard_map/cond/branch_1_fun/new_centres/pallas_call | solution.py:62
  35.9 3.1 %all-to-all-done.refs_1_ = f32[32,1,128]{2,1,0:T(1,128)S(1)} async-done(((f32[32,1,128]{2,1,0:T(1,128)}), f32[32,1,128]{2,1,0:T(1,128)S(1)}, u32[]{:S(2)}, u32[]{:S(2)}) %all-to-all-start) | async-done | bytes 16416 | tf_op jit(solution)/shard_map/all_to_all | solution.py:437
  39.0 0.7 %finish.1 = f32[1,1024]{1,0:T(1,128)} custom-call(f32[1,1024]{1,0:T(1,128)S(1)} %get-tuple-element.55.refs_0_, f32[32,1,128]{2,1,0:T(1,128)S(1)} %all-to-all-done.refs_1_, f32[1,256]{1,0:T(1,128)S(1)} %get-tuple-element.59.refs_2_), custom_call_target="tpu_custom_call" | custom-call | flops 600000000 | tf_op jit(solution)/shard_map/finish/pallas_call | solution.py:62
  (23 shorter events, 0.2 us)
Async XLA Ops:
  0.6 16.0 %copy-start.1 = (bf16[2048,256]{1,0:T(8,128)(2,1)S(1)}, bf16[2048,256]{1,0:T(8,128)(2,1)}, u32[]{:S(2)}) copy-start(bf16[2048,256]{1,0:T(8,128)(2,1)} %refs_1_.3) | copy-start | bytes 3145732
  2.5 7.6 %collective-permute-start.3 = (bf16[160,256]{1,0:T(8,128)(2,1)S(1)}, bf16[160,256]{1,0:T(8,128)(2,1)S(1)}, u32[]{:S(2)}, u32[]{:S(2)}) collective-permute-start(bf16[160,256]{1,0:T(8,128)(2,1)S(1)} %get-tuple-element.50), channel_id=1, source_target_pairs={{0,3},{1,2},{2,1},{3,0},{4,28},{5,29},{6,30},{7,31},{8,11},{9,10},... | collective-permute-start | bytes 245768 | tf_op jit(solution)/shard_map/ppermute | solution.py:342
  7.6 5.3 %collective-permute-start.2 = (bf16[160,256]{1,0:T(8,128)(2,1)S(1)}, bf16[160,256]{1,0:T(8,128)(2,1)S(1)}, u32[]{:S(2)}, u32[]{:S(2)}) collective-permute-start(bf16[160,256]{1,0:T(8,128)(2,1)S(1)} %get-tuple-element.50), channel_id=1, source_target_pairs={{0,2},{1,3},{2,0},{3,1},{4,20},{5,21},{6,22},{7,23},{8,10},{9,11},... | collective-permute-start | bytes 245768 | tf_op jit(solution)/shard_map/ppermute | solution.py:342
  7.6 5.3 %collective-permute-start.1 = (bf16[160,256]{1,0:T(8,128)(2,1)S(1)}, bf16[160,256]{1,0:T(8,128)(2,1)S(1)}, u32[]{:S(2)}, u32[]{:S(2)}) collective-permute-start(bf16[160,256]{1,0:T(8,128)(2,1)S(1)} %get-tuple-element.50), channel_id=1, source_target_pairs={{0,1},{1,0},{2,3},{3,2},{4,12},{5,13},{6,14},{7,15},{8,9},{9,8},{1... | collective-permute-start | bytes 245768 | tf_op jit(solution)/shard_map/ppermute | solution.py:342
  8.2 11.7 %collective-permute-start.4 = (bf16[1024,256]{1,0:T(8,128)(2,1)S(1)}, bf16[1024,256]{1,0:T(8,128)(2,1)S(1)}, u32[]{:S(2)}, u32[]{:S(2)}) collective-permute-start(bf16[1024,256]{1,0:T(8,128)(2,1)S(1)} %get-tuple-element.49.refs_0_), channel_id=1, source_target_pairs={{0,4},{1,5},{2,6},{3,7},{4,0},{5,1},{6,2},{7,3},{8,12},{9,13},{10,... | collective-permute-start | bytes 1572872 | tf_op jit(solution)/shard_map/ppermute | solution.py:342
  13.0 3.6 %copy-start = (s32[2,1024]{1,0:T(2,128)S(1)}, s32[2,1024]{1,0:T(2,128)}, u32[]{:S(2)}) copy-start(s32[2,1024]{1,0:T(2,128)} %refs_2_.1) | copy-start | bytes 24580
  13.0 3.6 %copy-start.2 = (s32[4096,1]{0,1:T(1,128)S(1)}, s32[4096,1]{0,1:T(1,128)}, u32[]{:S(2)}) copy-start(s32[4096,1]{0,1:T(1,128)} %param.11) | copy-start | bytes 49156
  13.1 7.6 %collective-permute-start.5 = (bf16[544,256]{1,0:T(8,128)(2,1)S(1)}, bf16[544,256]{1,0:T(8,128)(2,1)S(1)}, u32[]{:S(2)}, u32[]{:S(2)}) collective-permute-start(bf16[544,256]{1,0:T(8,128)(2,1)S(1)} %maximum_dynamic-update-slice_fusion.refs_4_.refs_1_.refs_2_), channel_id=1, source_target_pairs={{0,24},{1,25},{2,26},{3,27},{4,6},{5,7},{6,4},{7,5},{8,16},{9,17},... | collective-permute-start | bytes 835592 | tf_op jit(solution)/shard_map/ppermute | solution.py:342
  15.9 7.7 %collective-permute-start.6 = (bf16[544,256]{1,0:T(8,128)(2,1)S(1)}, bf16[544,256]{1,0:T(8,128)(2,1)S(1)}, u32[]{:S(2)}, u32[]{:S(2)}) collective-permute-start(bf16[544,256]{1,0:T(8,128)(2,1)S(1)} %maximum_dynamic-update-slice_fusion.refs_4_.refs_1_.refs_2_), channel_id=1, source_target_pairs={{0,16},{1,17},{2,18},{3,19},{4,7},{5,6},{6,5},{7,4},{8,24},{9,25},... | collective-permute-start | bytes 835592 | tf_op jit(solution)/shard_map/ppermute | solution.py:342
  16.4 7.2 %collective-permute-start.7 = (bf16[544,256]{1,0:T(8,128)(2,1)S(1)}, bf16[544,256]{1,0:T(8,128)(2,1)S(1)}, u32[]{:S(2)}, u32[]{:S(2)}) collective-permute-start(bf16[544,256]{1,0:T(8,128)(2,1)S(1)} %maximum_dynamic-update-slice_fusion.refs_4_.refs_1_.refs_2_), channel_id=1, source_target_pairs={{0,8},{1,9},{2,10},{3,11},{4,5},{5,4},{6,7},{7,6},{8,0},{9,1},{10,... | collective-permute-start | bytes 835592 | tf_op jit(solution)/shard_map/ppermute | solution.py:342
  24.7 1.3 %collective-permute-start.8 = (f32[40,128]{1,0:T(8,128)S(1)}, f32[40,128]{1,0:T(8,128)S(1)}, u32[]{:S(2)}, u32[]{:S(2)}) collective-permute-start(f32[40,128]{1,0:T(8,128)S(1)} %get-tuple-element.54), channel_id=1, source_target_pairs={{0,4},{1,5},{2,6},{3,7},{4,0},{5,1},{6,2},{7,3},{8,12},{9,13},{10,... | collective-permute-start | bytes 61448 | tf_op jit(solution)/shard_map/ppermute | solution.py:342
  26.7 12.3 %all-to-all-start = ((f32[32,1,128]{2,1,0:T(1,128)}), f32[32,1,128]{2,1,0:T(1,128)S(1)}, u32[]{:S(2)}, u32[]{:S(2)}) async-start(f32[32,1,128]{2,1,0:T(1,128)} %get-tuple-element.56), calls=%async_computation | async-start | bytes 32768 | tf_op jit(solution)/shard_map/all_to_all | solution.py:437
  33.6 1.5 %collective-permute-start = (f32[128,384]{1,0:T(8,128)S(1)}, f32[128,384]{1,0:T(8,128)S(1)}, u32[]{:S(2)}, u32[]{:S(2)}) collective-permute-start(f32[128,384]{1,0:T(8,128)S(1)} %get-tuple-element.34), channel_id=1, source_target_pairs={{0,4},{1,5},{2,6},{3,7},{4,0},{5,1},{6,2},{7,3},{8,12},{9,13},{10,... | collective-permute-start | bytes 589832 | tf_op jit(solution)/shard_map/cond/branch_1_fun/ppermute | solution.py:342

commit v6 on v5

--- a/solution.py
+++ b/solution.py
@@ -16,7 +16,7 @@
 BF16 = jnp.bfloat16
 
 CORE = 4
-FAN = ((1, 2), (8, 16))
+FAN = ((3, 2), (24, 16))
 SPREAD = ((24, 16), (2, 3))
 
 
@@ -235,14 +235,16 @@
     slot_kernel(*slot_args, picks_ref, owner_ref, place_ref, slot_owner_ref, token_ref)
 
 
-def start_scan_kernel(rows, beside_ref, piece_ref, best_ref):
-    best_ref[...] = scan_pieces(beside_ref, [piece_ref], rows, jnp.full(best_ref.shape, -jnp.inf, F32))
+def both_scan_kernel(rows, points_ref, beside_ref, best_ref, own_ref, piece_ref, next_ref, beside_best_ref):
+    next_ref[...] = scan_pieces(points_ref, [piece_ref], rows, best_ref[...])
+    lowest = jnp.full(beside_best_ref.shape, -jnp.inf, F32)
+    beside_best_ref[...] = scan_pieces(beside_ref, [own_ref, piece_ref], rows, lowest)
 
 
 def beside_scan_kernel(rows, beside_ref, best_ref, *refs):
     piece_refs, (message_ref, token_ref) = refs[:-2], refs[-2:]
     token_ref[...] = jnp.zeros(token_ref.shape, F32)
-    best = scan_pieces(beside_ref, piece_refs[1:], rows, best_ref[...])
+    best = scan_pieces(beside_ref, piece_refs[2:], rows, best_ref[...])
     top = jnp.max(best, axis=0, keepdims=True)
     top = [top[:, k : k + LANES] for k in range(0, top.shape[1], LANES)]
     count = join_counts(piece_refs[0][rows:, :])
@@ -421,8 +423,12 @@
             3.0,
         )
         beside = permute(near_points, swap)
-        beside_best = local_call(
-            functools.partial(start_scan_kernel, piece_rows), best_shape, (beside, own), "scan_start", 0.5
+        best, beside_best = local_call(
+            functools.partial(both_scan_kernel, piece_rows),
+            (best_shape, best_shape),
+            (near_points, beside, best, own, others[0]),
+            "scan_both",
+            1.3,
         )
         message, scanned = local_call(
             functools.partial(beside_scan_kernel, piece_rows),
@@ -432,7 +438,7 @@
             1.2,
         )
         answer = permute(message, swap)
-        top = next_scan(near_points, best, scanned, *others)
+        top = next_scan(near_points, best, scanned, *others[1:])
         near, share = local_call(near_kernel, near_shapes, (norms, top, answer), "nearest", 0.5)
         shares = lax.all_to_all(share, AXES, 0, 0)
 

time: 39.9 us -> 39.4 us (0.987)
  transfers between devices with their start and end apart: 10 -> 10, of which waited for: 7 -> 8; matrix products, arithmetic and copies ran while one was open for 0% -> 0% of each run, Pallas kernels for 18% -> 19%
where the time goes in v6:
time: 39.4 us; the launch traced here: 39.2 us
  starting transfers between devices  14.7 us (37%)
  waiting for transfers between devices  12.1 us (31%)
  Pallas kernels  11.4 us (29%)
  between operations  0.77 us (2%)
    pallas_call x9, Pallas kernels, local_call(): pl.pallas_call(body, out_shape=out_shape, in_specs=specs, out_specs=resul...  11.4 us
    ppermute x9, starting transfers between devices, permute(): return lax.ppermute(value, AXES, pairs)  9.81 us
    ppermute x9, waiting for transfers between devices, permute(): return lax.ppermute(value, AXES, pairs)  9.02 us
    all_to_all x1, starting transfers between devices, shards(): shares = lax.all_to_all(share, AXES, 0, 0)  4.93 us
    all_to_all x1, waiting for transfers between devices, shards(): shares = lax.all_to_all(share, AXES, 0, 0)  3.12 us
  transfers between devices with their start and end apart: 10, of which 8 were waited for; matrix products, arithmetic and copies ran while one was open for 0% of the time, Pallas kernels for 19%

profile of v6, /device:TPU:0, one launch (start us, length us, event | category | flops | bytes accessed | tf_op | source)
XLA Modules:
  0.0 39.2 jit_solution(2343376787067884852)
XLA Ops:
  0.6 1.8 %pick_rows.1 = (bf16[160,256]{1,0:T(8,128)(2,1)S(1)}, bf16[1024,256]{1,0:T(8,128)(2,1)S(1)}) custom-call(s32[2,1024]{1,0:T(2,128)} %refs_2_.1, bf16[1024,256]{1,0:T(8,128)(2,1)} %refs_1_.2, s32[8,128]{1,0:T(8,128)} %bitcast.5), custom_call_target="tpu_custom_call" | custom-call | flops 800000000 | tf_op jit(solution)/shard_map/pick_rows/pallas_call | solution.py:62
  2.5 5.1 %collective-permute-start.1 = (bf16[160,256]{1,0:T(8,128)(2,1)S(1)}, bf16[160,256]{1,0:T(8,128)(2,1)S(1)}, u32[]{:S(2)}, u32[]{:S(2)}) collective-permute-start(bf16[160,256]{1,0:T(8,128)(2,1)S(1)} %get-tuple-element.52), channel_id=1, source_target_pairs={{0,3},{1,2},{2,1},{3,0},{4,28},{5,29},{6,30},{7,31},{8,11},{9,10},... | collective-permute-start | bytes 245768 | tf_op jit(solution)/shard_map/ppermute | solution.py:344
  7.6 0.6 %collective-permute-start.3 = (bf16[160,256]{1,0:T(8,128)(2,1)S(1)}, bf16[160,256]{1,0:T(8,128)(2,1)S(1)}, u32[]{:S(2)}, u32[]{:S(2)}) collective-permute-start(bf16[160,256]{1,0:T(8,128)(2,1)S(1)} %get-tuple-element.52), channel_id=1, source_target_pairs={{0,1},{1,0},{2,3},{3,2},{4,12},{5,13},{6,14},{7,15},{8,9},{9,8},{1... | collective-permute-start | bytes 245768 | tf_op jit(solution)/shard_map/ppermute | solution.py:344
  8.2 3.8 %collective-permute-done.3 = bf16[160,256]{1,0:T(8,128)(2,1)S(1)} collective-permute-done((bf16[160,256]{1,0:T(8,128)(2,1)S(1)}, bf16[160,256]{1,0:T(8,128)(2,1)S(1)}, u32[]{:S(2)}, u32[]{:S(2)}) %collective-permute-start.3) | collective-permute-done | bytes 81952 | tf_op jit(solution)/shard_map/ppermute | solution.py:344
  12.0 0.9 %collective-permute-done.2 = bf16[160,256]{1,0:T(8,128)(2,1)S(1)} collective-permute-done((bf16[160,256]{1,0:T(8,128)(2,1)S(1)}, bf16[160,256]{1,0:T(8,128)(2,1)S(1)}, u32[]{:S(2)}, u32[]{:S(2)}) %collective-permute-start.2) | collective-permute-done | bytes 81952 | tf_op jit(solution)/shard_map/ppermute | solution.py:344
  13.1 2.8 %collective-permute-start.5 = (bf16[544,256]{1,0:T(8,128)(2,1)S(1)}, bf16[544,256]{1,0:T(8,128)(2,1)S(1)}, u32[]{:S(2)}, u32[]{:S(2)}) collective-permute-start(bf16[544,256]{1,0:T(8,128)(2,1)S(1)} %maximum_dynamic-update-slice_fusion.refs_4_.refs_3_.refs_2_), channel_id=1, source_target_pairs={{0,24},{1,25},{2,26},{3,27},{4,6},{5,7},{6,4},{7,5},{8,16},{9,17},... | collective-permute-start | bytes 835592 | tf_op jit(solution)/shard_map/ppermute | solution.py:344
  15.9 0.5 %collective-permute-start.6 = (bf16[544,256]{1,0:T(8,128)(2,1)S(1)}, bf16[544,256]{1,0:T(8,128)(2,1)S(1)}, u32[]{:S(2)}, u32[]{:S(2)}) collective-permute-start(bf16[544,256]{1,0:T(8,128)(2,1)S(1)} %maximum_dynamic-update-slice_fusion.refs_4_.refs_3_.refs_2_), channel_id=1, source_target_pairs={{0,16},{1,17},{2,18},{3,19},{4,7},{5,6},{6,5},{7,4},{8,24},{9,25},... | collective-permute-start | bytes 835592 | tf_op jit(solution)/shard_map/ppermute | solution.py:344
  16.4 0.2 collective-permute-start.7
  16.6 3.1 %scan_own.1 = (f32[8,1024]{1,0:T(8,128)S(1)}, f32[8,1024]{1,0:T(8,128)S(1)}, s32[16,128]{1,0:T(8,128)S(1)}, s32[16,128]{1,0:T(8,128)S(1)}, f32[1,256]{1,0:T(1,128)}) custom-call(bf16[1024,256]{1,0:T(8,128)(2,1)S(1)} %get-tuple-element.51.refs_0_, bf16[2048,256]{1,0:T(8,128)(2,1)S(1)} %copy-done.1, s32[2,1024]{1,0:T(2,128)S(1)} %copy-done, ...), custom_call_target="tpu_custom_call" | custom-call | flops 3000000000 | tf_op jit(solution)/shard_map/scan_own/pallas_call | solution.py:62
  19.8 0.9 %collective-permute-done.5.refs_4_.refs_3_ = bf16[544,256]{1,0:T(8,128)(2,1)S(1)} collective-permute-done((bf16[544,256]{1,0:T(8,128)(2,1)S(1)}, bf16[544,256]{1,0:T(8,128)(2,1)S(1)}, u32[]{:S(2)}, u32[]{:S(2)}) %collective-permute-start.5) | collective-permute-done | bytes 278560 | tf_op jit(solution)/shard_map/ppermute | solution.py:344
  20.7 1.0 %scan_both.1 = (f32[8,1024]{1,0:T(8,128)S(1)}, f32[8,1024]{1,0:T(8,128)S(1)}) custom-call(bf16[1024,256]{1,0:T(8,128)(2,1)S(1)} %get-tuple-element.51.refs_0_, bf16[1024,256]{1,0:T(8,128)(2,1)S(1)} %collective-permute-done.4.refs_1_.refs_0_, f32[8,1024]{1,0:T(8,128)S(1)} %get-tuple-element.54.refs_2_, ...), custom_call_target="tpu_custom_call" | custom-call | flops 1300000000 | tf_op jit(solution)/shard_map/scan_both/pallas_call | solution.py:62
  21.7 1.8 %collective-permute-done.6.refs_4_.refs_3_ = bf16[544,256]{1,0:T(8,128)(2,1)S(1)} collective-permute-done((bf16[544,256]{1,0:T(8,128)(2,1)S(1)}, bf16[544,256]{1,0:T(8,128)(2,1)S(1)}, u32[]{:S(2)}, u32[]{:S(2)}) %collective-permute-start.6) | collective-permute-done | bytes 278560 | tf_op jit(solution)/shard_map/ppermute | solution.py:344
  23.7 0.8 %scan_beside.1 = (f32[40,128]{1,0:T(8,128)S(1)}, f32[1,256]{1,0:T(1,128)S(1)}) custom-call(bf16[1024,256]{1,0:T(8,128)(2,1)S(1)} %collective-permute-done.4.refs_1_.refs_0_, f32[8,1024]{1,0:T(8,128)S(1)} %get-tuple-element.56.refs_1_, bf16[544,256]{1,0:T(8,128)(2,1)S(1)} %maximum_dynamic-update-slice_fusion.refs_4_.refs_3_.refs_2_, ...), custom_call_target="tpu_custom_call" | custom-call | flops 1200000000 | tf_op jit(solution)/shard_map/scan_beside/pallas_call | solution.py:62
  24.6 0.8 %scan_next.1.refs_1_ = f32[1,1024]{1,0:T(1,128)S(1)} custom-call(bf16[1024,256]{1,0:T(8,128)(2,1)S(1)} %get-tuple-element.51.refs_0_, f32[8,1024]{1,0:T(8,128)S(1)} %get-tuple-element.55.refs_1_, f32[1,256]{1,0:T(1,128)S(1)} %get-tuple-element.57.refs_2_, bf16[544,256]{1,0:T(8,128)(2,1)S(1)} %collective-permute-done.6.refs_4_.refs_3_, ...), custom_call_target="tpu_custom_call" | custom-call | flops 1019200000 | tf_op jit(solution)/shard_map/scan_next/pallas_call | solution.py:62
  25.4 0.3 collective-permute-done.8.refs_2_
  25.7 0.7 %nearest.1 = (f32[1,1024]{1,0:T(1,128)S(1)}, f32[32,1,128]{2,1,0:T(1,128)}) custom-call(f32[8,1024]{1,0:T(8,128)S(1)} %get-tuple-element.53.refs_0_, f32[1,1024]{1,0:T(1,128)S(1)} %scan_next.1.refs_1_, f32[40,128]{1,0:T(8,128)S(1)} %collective-permute-done.8.refs_2_), custom_call_target="tpu_custom_call" | custom-call | flops 500000000 | tf_op jit(solution)/shard_map/nearest/pallas_call | solution.py:62
  26.4 4.9 %all-to-all-start = ((f32[32,1,128]{2,1,0:T(1,128)}), f32[32,1,128]{2,1,0:T(1,128)S(1)}, u32[]{:S(2)}, u32[]{:S(2)}) async-start(f32[32,1,128]{2,1,0:T(1,128)} %get-tuple-element.60), calls=%async_computation | async-start | bytes 32768 | tf_op jit(solution)/shard_map/all_to_all | solution.py:443
  31.3 4.0 %conditional.1 = ((f32[128,256]{1,0:T(8,128)}, f32[1,256]{1,0:T(1,128)S(1)})) conditional(s32[]{:T(128)} %convert_element_type.20, () %tuple.15, (f32[1,1024]{1,0:T(1,128)S(1)}, f32[40,128]{1,0:T(8,128)S(1)}, f32[40,128]{1,0:T(8,128)S(1)}, s32[32,128]{1,0:T(8,128)S(1)}, s32[16,128]{1,0:T(8,128)S(1)}, /*index=5*/s32[16,128]{1,0:T(8,128)S(1)}, ...), branch_computations={%region_0.0_spmd, %region_1.0_spmd} | conditional | flops 2300000000 | bytes 786480 | solution.py:456
  31.4 1.8 %lloyd.1 = (f32[128,384]{1,0:T(8,128)S(1)}, f32[128,384]{1,0:T(8,128)S(1)}) custom-call(f32[1,1024]{1,0:T(1,128)S(1)} %get-tuple-element.22.refs_0_, f32[40,128]{1,0:T(8,128)S(1)} %get-tuple-element.23.refs_1_, f32[40,128]{1,0:T(8,128)S(1)} %get-tuple-element.24.refs_2_, s32[32,128]{1,0:T(8,128)S(1)} %get-tuple-element.25.refs_3_, ...), custom_call_target="tpu_custom_call" | custom-call | flops 1800000000 | tf_op jit(solution)/shard_map/cond/branch_1_fun/lloyd/pallas_call | solution.py:62
  33.1 0.3 collective-permute-start
  33.4 1.2 %collective-permute-done.refs_1_ = f32[128,384]{1,0:T(8,128)S(1)} collective-permute-done((f32[128,384]{1,0:T(8,128)S(1)}, f32[128,384]{1,0:T(8,128)S(1)}, u32[]{:S(2)}, u32[]{:S(2)}) %collective-permute-start) | collective-permute-done | bytes 196640 | tf_op jit(solution)/shard_map/cond/branch_1_fun/ppermute | solution.py:344
  34.6 0.8 %new_centres.1 = (f32[128,256]{1,0:T(8,128)}, f32[1,256]{1,0:T(1,128)S(1)}) custom-call(f32[128,384]{1,0:T(8,128)S(1)} %get-tuple-element.33.refs_0_, f32[128,384]{1,0:T(8,128)S(1)} %collective-permute-done.refs_1_), custom_call_target="tpu_custom_call" | custom-call | flops 500000000 | tf_op jit(solution)/shard_map/cond/branch_1_fun/new_centres/pallas_call | solution.py:62
  35.4 3.1 %all-to-all-done.refs_1_ = f32[32,1,128]{2,1,0:T(1,128)S(1)} async-done(((f32[32,1,128]{2,1,0:T(1,128)}), f32[32,1,128]{2,1,0:T(1,128)S(1)}, u32[]{:S(2)}, u32[]{:S(2)}) %all-to-all-start) | async-done | bytes 16416 | tf_op jit(solution)/shard_map/all_to_all | solution.py:443
  38.5 0.7 %finish.1 = f32[1,1024]{1,0:T(1,128)} custom-call(f32[1,1024]{1,0:T(1,128)S(1)} %get-tuple-element.59.refs_0_, f32[32,1,128]{2,1,0:T(1,128)S(1)} %all-to-all-done.refs_1_, f32[1,256]{1,0:T(1,128)S(1)} %get-tuple-element.63.refs_2_), custom_call_target="tpu_custom_call" | custom-call | flops 600000000 | tf_op jit(solution)/shard_map/finish/pallas_call | solution.py:62
  (23 shorter events, 0.4 us)
Async XLA Ops:
  0.6 16.0 %copy-start.1 = (bf16[2048,256]{1,0:T(8,128)(2,1)S(1)}, bf16[2048,256]{1,0:T(8,128)(2,1)}, u32[]{:S(2)}) copy-start(bf16[2048,256]{1,0:T(8,128)(2,1)} %refs_1_.3) | copy-start | bytes 3145732
  2.5 10.5 %collective-permute-start.1 = (bf16[160,256]{1,0:T(8,128)(2,1)S(1)}, bf16[160,256]{1,0:T(8,128)(2,1)S(1)}, u32[]{:S(2)}, u32[]{:S(2)}) collective-permute-start(bf16[160,256]{1,0:T(8,128)(2,1)S(1)} %get-tuple-element.52), channel_id=1, source_target_pairs={{0,3},{1,2},{2,1},{3,0},{4,28},{5,29},{6,30},{7,31},{8,11},{9,10},... | collective-permute-start | bytes 245768 | tf_op jit(solution)/shard_map/ppermute | solution.py:344
  7.6 5.3 %collective-permute-start.2 = (bf16[160,256]{1,0:T(8,128)(2,1)S(1)}, bf16[160,256]{1,0:T(8,128)(2,1)S(1)}, u32[]{:S(2)}, u32[]{:S(2)}) collective-permute-start(bf16[160,256]{1,0:T(8,128)(2,1)S(1)} %get-tuple-element.52), channel_id=1, source_target_pairs={{0,2},{1,3},{2,0},{3,1},{4,20},{5,21},{6,22},{7,23},{8,10},{9,11},... | collective-permute-start | bytes 245768 | tf_op jit(solution)/shard_map/ppermute | solution.py:344
  7.6 4.4 %collective-permute-start.3 = (bf16[160,256]{1,0:T(8,128)(2,1)S(1)}, bf16[160,256]{1,0:T(8,128)(2,1)S(1)}, u32[]{:S(2)}, u32[]{:S(2)}) collective-permute-start(bf16[160,256]{1,0:T(8,128)(2,1)S(1)} %get-tuple-element.52), channel_id=1, source_target_pairs={{0,1},{1,0},{2,3},{3,2},{4,12},{5,13},{6,14},{7,15},{8,9},{9,8},{1... | collective-permute-start | bytes 245768 | tf_op jit(solution)/shard_map/ppermute | solution.py:344
  8.2 12.5 %collective-permute-start.4 = (bf16[1024,256]{1,0:T(8,128)(2,1)S(1)}, bf16[1024,256]{1,0:T(8,128)(2,1)S(1)}, u32[]{:S(2)}, u32[]{:S(2)}) collective-permute-start(bf16[1024,256]{1,0:T(8,128)(2,1)S(1)} %get-tuple-element.51.refs_0_), channel_id=1, source_target_pairs={{0,4},{1,5},{2,6},{3,7},{4,0},{5,1},{6,2},{7,3},{8,12},{9,13},{10,... | collective-permute-start | bytes 1572872 | tf_op jit(solution)/shard_map/ppermute | solution.py:344
  13.0 3.6 %copy-start = (s32[2,1024]{1,0:T(2,128)S(1)}, s32[2,1024]{1,0:T(2,128)}, u32[]{:S(2)}) copy-start(s32[2,1024]{1,0:T(2,128)} %refs_2_.1) | copy-start | bytes 24580
  13.0 3.6 %copy-start.2 = (s32[4096,1]{0,1:T(1,128)S(1)}, s32[4096,1]{0,1:T(1,128)}, u32[]{:S(2)}) copy-start(s32[4096,1]{0,1:T(1,128)} %param.11) | copy-start | bytes 49156
  13.1 7.6 %collective-permute-start.5 = (bf16[544,256]{1,0:T(8,128)(2,1)S(1)}, bf16[544,256]{1,0:T(8,128)(2,1)S(1)}, u32[]{:S(2)}, u32[]{:S(2)}) collective-permute-start(bf16[544,256]{1,0:T(8,128)(2,1)S(1)} %maximum_dynamic-update-slice_fusion.refs_4_.refs_3_.refs_2_), channel_id=1, source_target_pairs={{0,24},{1,25},{2,26},{3,27},{4,6},{5,7},{6,4},{7,5},{8,16},{9,17},... | collective-permute-start | bytes 835592 | tf_op jit(solution)/shard_map/ppermute | solution.py:344
  15.9 7.7 %collective-permute-start.6 = (bf16[544,256]{1,0:T(8,128)(2,1)S(1)}, bf16[544,256]{1,0:T(8,128)(2,1)S(1)}, u32[]{:S(2)}, u32[]{:S(2)}) collective-permute-start(bf16[544,256]{1,0:T(8,128)(2,1)S(1)} %maximum_dynamic-update-slice_fusion.refs_4_.refs_3_.refs_2_), channel_id=1, source_target_pairs={{0,16},{1,17},{2,18},{3,19},{4,7},{5,6},{6,5},{7,4},{8,24},{9,25},... | collective-permute-start | bytes 835592 | tf_op jit(solution)/shard_map/ppermute | solution.py:344
  16.4 7.3 %collective-permute-start.7 = (bf16[544,256]{1,0:T(8,128)(2,1)S(1)}, bf16[544,256]{1,0:T(8,128)(2,1)S(1)}, u32[]{:S(2)}, u32[]{:S(2)}) collective-permute-start(bf16[544,256]{1,0:T(8,128)(2,1)S(1)} %maximum_dynamic-update-slice_fusion.refs_4_.refs_3_.refs_2_), channel_id=1, source_target_pairs={{0,8},{1,9},{2,10},{3,11},{4,5},{5,4},{6,7},{7,6},{8,0},{9,1},{10,... | collective-permute-start | bytes 835592 | tf_op jit(solution)/shard_map/ppermute | solution.py:344
  24.4 1.3 %collective-permute-start.8 = (f32[40,128]{1,0:T(8,128)S(1)}, f32[40,128]{1,0:T(8,128)S(1)}, u32[]{:S(2)}, u32[]{:S(2)}) collective-permute-start(f32[40,128]{1,0:T(8,128)S(1)} %get-tuple-element.58), channel_id=1, source_target_pairs={{0,4},{1,5},{2,6},{3,7},{4,0},{5,1},{6,2},{7,3},{8,12},{9,13},{10,... | collective-permute-start | bytes 61448 | tf_op jit(solution)/shard_map/ppermute | solution.py:344
  26.4 12.1 %all-to-all-start = ((f32[32,1,128]{2,1,0:T(1,128)}), f32[32,1,128]{2,1,0:T(1,128)S(1)}, u32[]{:S(2)}, u32[]{:S(2)}) async-start(f32[32,1,128]{2,1,0:T(1,128)} %get-tuple-element.60), calls=%async_computation | async-start | bytes 32768 | tf_op jit(solution)/shard_map/all_to_all | solution.py:443
  33.1 1.5 %collective-permute-start = (f32[128,384]{1,0:T(8,128)S(1)}, f32[128,384]{1,0:T(8,128)S(1)}, u32[]{:S(2)}, u32[]{:S(2)}) collective-permute-start(f32[128,384]{1,0:T(8,128)S(1)} %get-tuple-element.34), channel_id=1, source_target_pairs={{0,4},{1,5},{2,6},{3,7},{4,0},{5,1},{6,2},{7,3},{8,12},{9,13},{10,... | collective-permute-start | bytes 589832 | tf_op jit(solution)/shard_map/cond/branch_1_fun/ppermute | solution.py:344

commit v7 on v6

--- a/solution.py
+++ b/solution.py
@@ -114,29 +114,33 @@
     place = jnp.sum(found.astype(F32), axis=1, keepdims=True).astype(jnp.int32)
     chosen = (iota((slots, point_count), 1) + 1 == place).astype(F32).astype(BF16)
     assign_copy.wait()
-    count = split_counts(tally(assign_ref[...], out_ref.shape[0] - slots))
+    ids = assign_ref[...]
+    ids = jnp.concatenate([lax.div(ids, LANES), lax.rem(ids, LANES)], axis=1).astype(F32)
     points_copy.wait()
     rows = jnp.dot(chosen, points_ref[...], preferred_element_type=F32)
     rows = jnp.where(place > 0, rows, FAR)
-    out_ref[...] = jnp.concatenate([rows, count], axis=0).astype(BF16)
-
-
-def tally(ids, cand_chunks):
-    lane_rows = iota((LANES, LANES), 0)
-    chunk_ids = iota((cand_chunks, LANES), 0)
-    high = [(lax.div(ids[t : t + 1, :], LANES) == chunk_ids).astype(F32) for t in range(ids.shape[0])]
-    low = [(lax.rem(ids[t : t + 1, :], LANES) == lane_rows).astype(F32) for t in range(ids.shape[0])]
-    return nt_dot(jnp.concatenate(high, axis=1).astype(BF16), jnp.concatenate(low, axis=1).astype(BF16))
-
-
-def split_counts(count):
-    firsts = jnp.floor(count * (1.0 / 256.0))
-    return jnp.concatenate([firsts, count - 256.0 * firsts], axis=1)
-
-
-def join_counts(parts):
-    parts = parts.astype(F32)
-    return 256.0 * parts[:, :LANES] + parts[:, LANES:]
+    out_ref[...] = jnp.concatenate([rows, ids], axis=0).astype(BF16)
+
+
+def add_tally(count, ids):
+    lane_rows = iota((LANES, LANES), 0).astype(F32)
+    chunk_ids = iota(count.shape, 0).astype(F32)
+    ids = ids.astype(F32)
+    for start in range(0, ids.shape[0], 8):
+        rows = [ids[t : t + 1, :] for t in range(start, start + 8)]
+        high = [(row[:, :LANES] == chunk_ids).astype(F32) for row in rows]
+        low = [(row[:, LANES:] == lane_rows).astype(F32) for row in rows]
+        high = jnp.concatenate(high, axis=1).astype(BF16)
+        low = jnp.concatenate(low, axis=1).astype(BF16)
+        count = count + nt_dot(high, low)
+    return count
+
+
+def tally_kernel(first, count_ref, *refs):
+    count = count_ref[...]
+    for ref in refs[:-1]:
+        count = add_tally(count, ref[first:, :])
+    refs[-1][...] = count
 
 
 def holders_in_order(doubling, device_ids):
@@ -235,45 +239,38 @@
     slot_kernel(*slot_args, picks_ref, owner_ref, place_ref, slot_owner_ref, token_ref)
 
 
-def both_scan_kernel(rows, points_ref, beside_ref, best_ref, own_ref, piece_ref, next_ref, beside_best_ref):
+def both_scan_kernel(rows, points_ref, beside_ref, best_ref, own_ref, piece_ref, *refs):
+    next_ref, next_count_ref, beside_best_ref = refs
     next_ref[...] = scan_pieces(points_ref, [piece_ref], rows, best_ref[...])
+    next_count_ref[...] = add_tally(jnp.zeros(next_count_ref.shape, F32), piece_ref[rows:, :])
     lowest = jnp.full(beside_best_ref.shape, -jnp.inf, F32)
     beside_best_ref[...] = scan_pieces(beside_ref, [own_ref, piece_ref], rows, lowest)
 
 
 def beside_scan_kernel(rows, beside_ref, best_ref, *refs):
-    piece_refs, (message_ref, token_ref) = refs[:-2], refs[-2:]
+    top_ref, token_ref = refs[-2:]
     token_ref[...] = jnp.zeros(token_ref.shape, F32)
-    best = scan_pieces(beside_ref, piece_refs[2:], rows, best_ref[...])
-    top = jnp.max(best, axis=0, keepdims=True)
-    top = [top[:, k : k + LANES] for k in range(0, top.shape[1], LANES)]
-    count = join_counts(piece_refs[0][rows:, :])
-    for piece_ref in piece_refs[1:]:
-        count = count + join_counts(piece_ref[rows:, :])
-    message_ref[...] = jnp.concatenate([*top, count], axis=0)
+    top_ref[...] = jnp.max(scan_pieces(beside_ref, refs[:-2], rows, best_ref[...]), axis=0, keepdims=True)
 
 
 def next_scan_kernel(rows, points_ref, best_ref, start_ref, *refs):
     refs[-1][...] = jnp.max(scan_pieces(points_ref, refs[:-1], rows, best_ref[...]), axis=0, keepdims=True)
 
 
-def near_kernel(norm_ref, top_ref, message_ref, near_ref, share_ref):
-    top = top_ref[...]
-    if message_ref is not None:
-        told = message_ref[: top.shape[1] // LANES, :]
-        top = jnp.maximum(top, jnp.concatenate([told[k : k + 1, :] for k in range(told.shape[0])], axis=1))
+def near_kernel(norm_ref, top_ref, beside_ref, near_ref, share_ref):
+    top = jnp.maximum(top_ref[...], beside_ref[...])
     near = jnp.maximum(norm_ref[0:1, :] - 2.0 * top, 0.0)
     near_ref[...] = near
     share_ref[...] = jnp.broadcast_to(jnp.sum(near, axis=1, keepdims=True)[None], share_ref.shape)
 
 
-def lloyd_kernel(piece_rows, sides, first_place, count_refs, owner_ref, place_ref, slot_owner_ref, centres_ref, *refs):
+def lloyd_kernel(piece_rows, sides, count_refs, owner_ref, place_ref, slot_owner_ref, centres_ref, *refs):
     piece_refs, out_refs = refs[:-sides], refs[-sides:]
     finals, features = out_refs[0].shape[0], centres_ref.shape[1]
     slot_chunks = slot_owner_ref.shape[0]
     chunks = place_ref.shape[0]
     first_chunks = owner_ref.shape[0] - chunks
-    count = sum(ref[first_place:, :] for ref in count_refs)
+    count = sum(ref[...] for ref in count_refs)
     weights = 1.0 + count
     weight_top = weights.astype(BF16).astype(F32)
     weight_rest = (weights - weight_top).astype(BF16).astype(F32)
@@ -375,18 +372,19 @@
     shape = jax.ShapeDtypeStruct
 
     token = shape((1, feature_count), F32)
-    cand_chunks = cand_count // LANES
+    count_shape = shape((cand_count // LANES, LANES), F32)
+    id_rows = point_count // LANES
     piece_rows = slots * (4 if doubling else device_count)
     block, near_points = local_call(
         functools.partial(pick_kernel, cap, slots),
-        (shape((slots + cand_chunks, feature_count), BF16), shape(points.shape, BF16)),
-        (picks, points, assign_pts.reshape(-1, LANES)),
+        (shape((slots + id_rows, feature_count), BF16), shape(points.shape, BF16)),
+        (picks, points, assign_pts.reshape(id_rows, LANES)),
         "pick_rows",
         0.8,
         unread=(0, 1, 2),
         scratch=(
             pltpu.VMEM(picks.shape, jnp.int32),
-            pltpu.VMEM((point_count // LANES, LANES), jnp.int32),
+            pltpu.VMEM((id_rows, LANES), jnp.int32),
             pltpu.SemaphoreType.DMA((3,)),
         ),
     )
@@ -412,8 +410,8 @@
     if doubling:
         swap = (CORE, CORE)
         near = [block, *(permute(block, m) for m in (hop(0), hop(1), both_hops(hop(0), hop(1))))]
-        told = split_counts(sum(join_counts(part[slots:]) for part in near)).astype(BF16)
-        own = jnp.concatenate([part[:slots] for part in near] + [told], axis=0)
+        own = [part[:slots] for part in near] + [part[slots:] for part in near]
+        own = jnp.concatenate(own, axis=0)
         others = [permute(own, m) for m in (hop(2), hop(3), both_hops(hop(2), hop(3)))]
         best, norms, places, slot_owners, scanned = local_call(
             functools.partial(own_scan_kernel, slot_args, piece_rows),
@@ -423,36 +421,42 @@
             3.0,
         )
         beside = permute(near_points, swap)
-        best, beside_best = local_call(
+        best, counts, beside_best = local_call(
             functools.partial(both_scan_kernel, piece_rows),
-            (best_shape, best_shape),
+            (best_shape, count_shape, best_shape),
             (near_points, beside, best, own, others[0]),
             "scan_both",
             1.3,
         )
         message, scanned = local_call(
             functools.partial(beside_scan_kernel, piece_rows),
-            (shape((point_count // LANES + cand_chunks, LANES), F32), token),
-            (beside, beside_best, own, *others),
+            (top_shape, token),
+            (beside, beside_best, *others[1:]),
             "scan_beside",
-            1.2,
+            0.9,
         )
         answer = permute(message, swap)
         top = next_scan(near_points, best, scanned, *others[1:])
         near, share = local_call(near_kernel, near_shapes, (norms, top, answer), "nearest", 0.5)
         shares = lax.all_to_all(share, AXES, 0, 0)
 
-        def both_sides(near_ref, mine_ref, other_ref, *refs):
-            lloyd_kernel(piece_rows, 2, point_count // LANES, (mine_ref, other_ref), *refs)
-
-        def sum_up(*operands):
+        def both_sides(mine_ref, other_ref, *refs):
+            lloyd_kernel(piece_rows, 2, (mine_ref, other_ref), *refs)
+
+        def rest_of_tally(near_ref, *refs):
+            tally_kernel(piece_rows, *refs)
+
+        def sum_up(near, counts, *operands):
+            own, *others = operands[-4:]
+            counts = local_call(rest_of_tally, count_shape, (near, counts, own, *others[1:]), "tally", 1.2)
+            operands = (counts, permute(counts, swap), *operands)
             keep, give = local_call(both_sides, (sum_shape, sum_shape), operands, "lloyd", 1.8)
             return centres_of((keep, permute(give, swap)))
 
         def nothing(*operands):
             return jnp.zeros((finals, feature_count), F32), jnp.zeros(token.shape, F32)
 
-        operands = (near, message, answer, owner_rows, places, slot_owners, centres, own, *others)
+        operands = (near, counts, owner_rows, places, slot_owners, centres, own, *others)
         new_centres, summed = lax.cond(lax.axis_index("row") < K_FINAL, sum_up, nothing, *operands)
     else:
         best, norms = local_call(
@@ -461,18 +465,17 @@
         places, slot_owners, found = local_call(
             functools.partial(slot_kernel, *slot_args), (*slot_shapes, token), (picks, owner_rows), "slot_owners", 1.0
         )
-        counts = lax.psum(join_counts(block[slots:]), AXES)
+        counts = jnp.zeros(count_shape.shape, F32)
+        counts = local_call(functools.partial(tally_kernel, 0), count_shape, (counts, block[slots:]), "tally", 0.3)
+        counts = lax.psum(counts, AXES)
         table = lax.all_gather(block[:slots], AXES, tiled=True)
         top = next_scan(near_points, best, found, table)
 
-        def nearest(norm_ref, top_ref, *refs):
-            near_kernel(norm_ref, top_ref, None, *refs)
-
-        near, share = local_call(nearest, near_shapes, (norms, top), "nearest", 0.5)
+        near, share = local_call(near_kernel, near_shapes, (norms, top, top), "nearest", 0.5)
         shares = lax.psum(share[:1], AXES)
 
         def one_side(count_ref, *refs):
-            lloyd_kernel(piece_rows, 1, 0, (count_ref,), *refs)
+            lloyd_kernel(piece_rows, 1, (count_ref,), *refs)
 
         operands = (counts, owner_rows, places, slot_owners, centres, table)
         new_centres, summed = centres_of((local_call(one_side, sum_shape, operands, "lloyd", 1.8),))

time: 39.4 us -> 38.9 us (0.987)
  waiting for transfers between devices: 12.1 us -> 10.3 us
  Pallas kernels: 11.4 us -> 12.6 us
    all_to_all x1, waiting for transfers between devices: 3.12 us -> 0.81 us  [shards(): shares = lax.all_to_all(share, AXES, 0, 0)]
    pallas_call x9 -> x10, Pallas kernels: 11.4 us -> 12.6 us  [local_call(): pl.pallas_call(body, out_shape=out_shape, in_specs=specs, out_specs=resul...]
    ppermute x9 -> x10, waiting for transfers between devices: 9.02 us -> 9.51 us  [permute(): return lax.ppermute(value, AXES, pairs)]
    ppermute x9 -> x10, starting transfers between devices: 9.81 us -> 10.1 us  [permute(): return lax.ppermute(value, AXES, pairs)]
  transfers between devices with their start and end apart: 10 -> 11, of which waited for: 8 -> 9; matrix products, arithmetic and copies ran while one was open for 0% -> 0% of each run, Pallas kernels for 19% -> 23%
where the time goes in v7:
time: 38.9 us; the launch traced here: 38.7 us
  starting transfers between devices  15 us (39%)
  Pallas kernels  12.6 us (32%)
  waiting for transfers between devices  10.3 us (26%)
  between operations  0.75 us (2%)
    pallas_call x10, Pallas kernels, local_call(): pl.pallas_call(body, out_shape=out_shape, in_specs=specs, out_specs=resul...  12.6 us
    ppermute x10, starting transfers between devices, permute(): return lax.ppermute(value, AXES, pairs)  10.1 us
    ppermute x10, waiting for transfers between devices, permute(): return lax.ppermute(value, AXES, pairs)  9.51 us
    all_to_all x1, starting transfers between devices, shards(): shares = lax.all_to_all(share, AXES, 0, 0)  4.95 us
    all_to_all x1, waiting for transfers between devices, shards(): shares = lax.all_to_all(share, AXES, 0, 0)  0.81 us
  transfers between devices with their start and end apart: 11, of which 9 were waited for; matrix products, arithmetic and copies ran while one was open for 0% of the time, Pallas kernels for 23%

profile of v7, /device:TPU:0, one launch (start us, length us, event | category | flops | bytes accessed | tf_op | source)
XLA Modules:
  0.0 38.7 jit_solution(12187333722976902872)
XLA Ops:
  0.6 1.5 %pick_rows.1 = (bf16[136,256]{1,0:T(8,128)(2,1)S(1)}, bf16[1024,256]{1,0:T(8,128)(2,1)S(1)}) custom-call(s32[2,1024]{1,0:T(2,128)} %refs_2_.1, bf16[1024,256]{1,0:T(8,128)(2,1)} %refs_1_.2, s32[8,128]{1,0:T(8,128)} %bitcast.5), custom_call_target="tpu_custom_call" | custom-call | flops 800000000 | tf_op jit(solution)/shard_map/pick_rows/pallas_call | solution.py:62
  2.2 5.1 %collective-permute-start.2 = (bf16[136,256]{1,0:T(8,128)(2,1)S(1)}, bf16[136,256]{1,0:T(8,128)(2,1)S(1)}, u32[]{:S(2)}, u32[]{:S(2)}) collective-permute-start(bf16[136,256]{1,0:T(8,128)(2,1)S(1)} %get-tuple-element.50), channel_id=1, source_target_pairs={{0,3},{1,2},{2,1},{3,0},{4,28},{5,29},{6,30},{7,31},{8,11},{9,10},... | collective-permute-start | bytes 208904 | tf_op jit(solution)/shard_map/ppermute | solution.py:341
  7.3 0.6 %collective-permute-start.4 = (bf16[136,256]{1,0:T(8,128)(2,1)S(1)}, bf16[136,256]{1,0:T(8,128)(2,1)S(1)}, u32[]{:S(2)}, u32[]{:S(2)}) collective-permute-start(bf16[136,256]{1,0:T(8,128)(2,1)S(1)} %get-tuple-element.50), channel_id=1, source_target_pairs={{0,1},{1,0},{2,3},{3,2},{4,12},{5,13},{6,14},{7,15},{8,9},{9,8},{1... | collective-permute-start | bytes 208904 | tf_op jit(solution)/shard_map/ppermute | solution.py:341
  7.9 1.7 %collective-permute-done.2 = bf16[136,256]{1,0:T(8,128)(2,1)S(1)} collective-permute-done((bf16[136,256]{1,0:T(8,128)(2,1)S(1)}, bf16[136,256]{1,0:T(8,128)(2,1)S(1)}, u32[]{:S(2)}, u32[]{:S(2)}) %collective-permute-start.2) | collective-permute-done | bytes 69664 | tf_op jit(solution)/shard_map/ppermute | solution.py:341
  9.7 2.8 %collective-permute-done.3 = bf16[136,256]{1,0:T(8,128)(2,1)S(1)} collective-permute-done((bf16[136,256]{1,0:T(8,128)(2,1)S(1)}, bf16[136,256]{1,0:T(8,128)(2,1)S(1)}, u32[]{:S(2)}, u32[]{:S(2)}) %collective-permute-start.3) | collective-permute-done | bytes 69664 | tf_op jit(solution)/shard_map/ppermute | solution.py:341
  12.6 2.8 %collective-permute-start.6 = (bf16[544,256]{1,0:T(8,128)(2,1)S(1)}, bf16[544,256]{1,0:T(8,128)(2,1)S(1)}, u32[]{:S(2)}, u32[]{:S(2)}) collective-permute-start(bf16[544,256]{1,0:T(8,128)(2,1)S(1)} %constant_dynamic-update-slice_fusion.refs_4_.refs_3_), channel_id=1, source_target_pairs={{0,24},{1,25},{2,26},{3,27},{4,6},{5,7},{6,4},{7,5},{8,16},{9,17},... | collective-permute-start | bytes 835592 | tf_op jit(solution)/shard_map/ppermute | solution.py:341
  15.4 0.5 %collective-permute-start.7 = (bf16[544,256]{1,0:T(8,128)(2,1)S(1)}, bf16[544,256]{1,0:T(8,128)(2,1)S(1)}, u32[]{:S(2)}, u32[]{:S(2)}) collective-permute-start(bf16[544,256]{1,0:T(8,128)(2,1)S(1)} %constant_dynamic-update-slice_fusion.refs_4_.refs_3_), channel_id=1, source_target_pairs={{0,16},{1,17},{2,18},{3,19},{4,7},{5,6},{6,5},{7,4},{8,24},{9,25},... | collective-permute-start | bytes 835592 | tf_op jit(solution)/shard_map/ppermute | solution.py:341
  16.2 3.1 %scan_own.1 = (f32[8,1024]{1,0:T(8,128)S(1)}, f32[8,1024]{1,0:T(8,128)S(1)}, s32[16,128]{1,0:T(8,128)S(1)}, s32[16,128]{1,0:T(8,128)S(1)}, f32[1,256]{1,0:T(1,128)}) custom-call(bf16[1024,256]{1,0:T(8,128)(2,1)S(1)} %get-tuple-element.49.refs_0_, bf16[2048,256]{1,0:T(8,128)(2,1)S(1)} %copy-done.1, s32[2,1024]{1,0:T(2,128)S(1)} %copy-done, ...), custom_call_target="tpu_custom_call" | custom-call | flops 3000000000 | tf_op jit(solution)/shard_map/scan_own/pallas_call | solution.py:62
  19.3 0.9 %collective-permute-done.6.refs_4_ = bf16[544,256]{1,0:T(8,128)(2,1)S(1)} collective-permute-done((bf16[544,256]{1,0:T(8,128)(2,1)S(1)}, bf16[544,256]{1,0:T(8,128)(2,1)S(1)}, u32[]{:S(2)}, u32[]{:S(2)}) %collective-permute-start.6) | collective-permute-done | bytes 278560 | tf_op jit(solution)/shard_map/ppermute | solution.py:341
  20.2 1.3 %scan_both.1 = (f32[8,1024]{1,0:T(8,128)S(1)}, f32[32,128]{1,0:T(8,128)S(1)}, f32[8,1024]{1,0:T(8,128)S(1)}) custom-call(bf16[1024,256]{1,0:T(8,128)(2,1)S(1)} %get-tuple-element.49.refs_0_, bf16[1024,256]{1,0:T(8,128)(2,1)S(1)} %collective-permute-done.5.refs_1_.refs_0_, f32[8,1024]{1,0:T(8,128)S(1)} %get-tuple-element.52.refs_2_, ...), custom_call_target="tpu_custom_call" | custom-call | flops 1300000000 | tf_op jit(solution)/shard_map/scan_both/pallas_call | solution.py:62
  21.6 1.5 %collective-permute-done.7.refs_2_.refs_3_ = bf16[544,256]{1,0:T(8,128)(2,1)S(1)} collective-permute-done((bf16[544,256]{1,0:T(8,128)(2,1)S(1)}, bf16[544,256]{1,0:T(8,128)(2,1)S(1)}, u32[]{:S(2)}, u32[]{:S(2)}) %collective-permute-start.7) | collective-permute-done | bytes 278560 | tf_op jit(solution)/shard_map/ppermute | solution.py:341
  23.2 0.8 %scan_beside.1 = (f32[1,1024]{1,0:T(1,128)S(1)}, f32[1,256]{1,0:T(1,128)S(1)}) custom-call(bf16[1024,256]{1,0:T(8,128)(2,1)S(1)} %collective-permute-done.5.refs_1_.refs_0_, f32[8,1024]{1,0:T(8,128)S(1)} %get-tuple-element.54.refs_1_, bf16[544,256]{1,0:T(8,128)(2,1)S(1)} %collective-permute-done.7.refs_2_.refs_3_, ...), custom_call_target="tpu_custom_call" | custom-call | flops 900000000 | tf_op jit(solution)/shard_map/scan_beside/pallas_call | solution.py:62
  24.1 0.8 %scan_next.1.refs_1_ = f32[1,1024]{1,0:T(1,128)S(1)} custom-call(bf16[1024,256]{1,0:T(8,128)(2,1)S(1)} %get-tuple-element.49.refs_0_, f32[8,1024]{1,0:T(8,128)S(1)} %get-tuple-element.53.refs_1_, f32[1,256]{1,0:T(1,128)S(1)} %get-tuple-element.55.refs_2_, bf16[544,256]{1,0:T(8,128)(2,1)S(1)} %collective-permute-done.7.refs_2_.refs_3_, ...), custom_call_target="tpu_custom_call" | custom-call | flops 1019200000 | tf_op jit(solution)/shard_map/scan_next/pallas_call | solution.py:62
  25.2 0.7 %nearest.1 = (f32[1,1024]{1,0:T(1,128)S(1)}, f32[32,1,128]{2,1,0:T(1,128)}) custom-call(f32[8,1024]{1,0:T(8,128)S(1)} %get-tuple-element.51.refs_0_, f32[1,1024]{1,0:T(1,128)S(1)} %scan_next.1.refs_1_, f32[1,1024]{1,0:T(1,128)S(1)} %collective-permute-done.9.refs_2_), custom_call_target="tpu_custom_call" | custom-call | flops 500000000 | tf_op jit(solution)/shard_map/nearest/pallas_call | solution.py:62
  25.9 5.0 %all-to-all-start = ((f32[32,1,128]{2,1,0:T(1,128)}), f32[32,1,128]{2,1,0:T(1,128)S(1)}, u32[]{:S(2)}, u32[]{:S(2)}) async-start(f32[32,1,128]{2,1,0:T(1,128)} %get-tuple-element.58), calls=%async_computation | async-start | bytes 32768 | tf_op jit(solution)/shard_map/all_to_all | solution.py:441
  30.9 6.4 %conditional.1 = ((f32[128,256]{1,0:T(8,128)}, f32[1,256]{1,0:T(1,128)S(1)})) conditional(s32[]{:T(128)} %convert_element_type.3, () %tuple.15, (f32[1,1024]{1,0:T(1,128)S(1)}, f32[32,128]{1,0:T(8,128)S(1)}, bf16[544,256]{1,0:T(8,128)(2,1)S(1)}, bf16[544,256]{1,0:T(8,128)(2,1)S(1)}, bf16[544,256]{1,0:T(8,128)(2,1)S(1)}, ...), branch_computations={%region_0.0_spmd, %region_1.0_spmd} | conditional | flops 3500000000 | bytes 852056 | solution.py:460
  30.9 1.1 %tally.1.refs_0_ = f32[32,128]{1,0:T(8,128)S(1)} custom-call(f32[1,1024]{1,0:T(1,128)S(1)} %get-tuple-element.20.refs_0_, f32[32,128]{1,0:T(8,128)S(1)} %get-tuple-element.21.refs_1_, bf16[544,256]{1,0:T(8,128)(2,1)S(1)} %get-tuple-element.22.refs_2_.refs_6_, bf16[544,256]{1,0:T(8,128)(2,1)S(1)} %get-tuple-element.23.refs_3_.refs_8_, ...), custom_call_target="tpu_custom_call" | custom-call | flops 1200000000 | tf_op jit(solution)/shard_map/cond/branch_1_fun/tally/pallas_call | solution.py:62
  32.2 0.9 %collective-permute-done.refs_1_ = f32[32,128]{1,0:T(8,128)S(1)} collective-permute-done((f32[32,128]{1,0:T(8,128)S(1)}, f32[32,128]{1,0:T(8,128)S(1)}, u32[]{:S(2)}, u32[]{:S(2)}) %collective-permute-start) | collective-permute-done | bytes 16416 | tf_op jit(solution)/shard_map/cond/branch_1_fun/ppermute | solution.py:341
  33.2 1.8 %lloyd.1 = (f32[128,384]{1,0:T(8,128)S(1)}, f32[128,384]{1,0:T(8,128)S(1)}) custom-call(f32[32,128]{1,0:T(8,128)S(1)} %tally.1.refs_0_, f32[32,128]{1,0:T(8,128)S(1)} %collective-permute-done.refs_1_, s32[32,128]{1,0:T(8,128)S(1)} %get-tuple-element.25.refs_2_, s32[16,128]{1,0:T(8,128)S(1)} %get-tuple-element.26.refs_3_, ...), custom_call_target="tpu_custom_call" | custom-call | flops 1800000000 | tf_op jit(solution)/shard_map/cond/branch_1_fun/lloyd/pallas_call | solution.py:62
  35.0 0.3 collective-permute-start.1
  35.3 1.2 %collective-permute-done.1.refs_1_ = f32[128,384]{1,0:T(8,128)S(1)} collective-permute-done((f32[128,384]{1,0:T(8,128)S(1)}, f32[128,384]{1,0:T(8,128)S(1)}, u32[]{:S(2)}, u32[]{:S(2)}) %collective-permute-start.1) | collective-permute-done | bytes 196640 | tf_op jit(solution)/shard_map/cond/branch_1_fun/ppermute | solution.py:341
  36.5 0.8 %new_centres.1 = (f32[128,256]{1,0:T(8,128)}, f32[1,256]{1,0:T(1,128)S(1)}) custom-call(f32[128,384]{1,0:T(8,128)S(1)} %get-tuple-element.30.refs_0_, f32[128,384]{1,0:T(8,128)S(1)} %collective-permute-done.1.refs_1_), custom_call_target="tpu_custom_call" | custom-call | flops 500000000 | tf_op jit(solution)/shard_map/cond/branch_1_fun/new_centres/pallas_call | solution.py:62
  37.2 0.8 %all-to-all-done.refs_1_ = f32[32,1,128]{2,1,0:T(1,128)S(1)} async-done(((f32[32,1,128]{2,1,0:T(1,128)}), f32[32,1,128]{2,1,0:T(1,128)S(1)}, u32[]{:S(2)}, u32[]{:S(2)}) %all-to-all-start) | async-done | bytes 16416 | tf_op jit(solution)/shard_map/all_to_all | solution.py:441
  38.0 0.7 %finish.1 = f32[1,1024]{1,0:T(1,128)} custom-call(f32[1,1024]{1,0:T(1,128)S(1)} %get-tuple-element.57.refs_0_, f32[32,1,128]{2,1,0:T(1,128)S(1)} %all-to-all-done.refs_1_, f32[1,256]{1,0:T(1,128)S(1)} %get-tuple-element.62.refs_2_), custom_call_target="tpu_custom_call" | custom-call | flops 600000000 | tf_op jit(solution)/shard_map/finish/pallas_call | solution.py:62
  (23 shorter events, 1.1 us)
Async XLA Ops:
  0.6 15.5 %copy-start.1 = (bf16[2048,256]{1,0:T(8,128)(2,1)S(1)}, bf16[2048,256]{1,0:T(8,128)(2,1)}, u32[]{:S(2)}) copy-start(bf16[2048,256]{1,0:T(8,128)(2,1)} %refs_1_.3) | copy-start | bytes 3145732
  2.2 7.5 %collective-permute-start.2 = (bf16[136,256]{1,0:T(8,128)(2,1)S(1)}, bf16[136,256]{1,0:T(8,128)(2,1)S(1)}, u32[]{:S(2)}, u32[]{:S(2)}) collective-permute-start(bf16[136,256]{1,0:T(8,128)(2,1)S(1)} %get-tuple-element.50), channel_id=1, source_target_pairs={{0,3},{1,2},{2,1},{3,0},{4,28},{5,29},{6,30},{7,31},{8,11},{9,10},... | collective-permute-start | bytes 208904 | tf_op jit(solution)/shard_map/ppermute | solution.py:341
  7.3 5.2 %collective-permute-start.3 = (bf16[136,256]{1,0:T(8,128)(2,1)S(1)}, bf16[136,256]{1,0:T(8,128)(2,1)S(1)}, u32[]{:S(2)}, u32[]{:S(2)}) collective-permute-start(bf16[136,256]{1,0:T(8,128)(2,1)S(1)} %get-tuple-element.50), channel_id=1, source_target_pairs={{0,2},{1,3},{2,0},{3,1},{4,20},{5,21},{6,22},{7,23},{8,10},{9,11},... | collective-permute-start | bytes 208904 | tf_op jit(solution)/shard_map/ppermute | solution.py:341
  7.3 5.2 %collective-permute-start.4 = (bf16[136,256]{1,0:T(8,128)(2,1)S(1)}, bf16[136,256]{1,0:T(8,128)(2,1)S(1)}, u32[]{:S(2)}, u32[]{:S(2)}) collective-permute-start(bf16[136,256]{1,0:T(8,128)(2,1)S(1)} %get-tuple-element.50), channel_id=1, source_target_pairs={{0,1},{1,0},{2,3},{3,2},{4,12},{5,13},{6,14},{7,15},{8,9},{9,8},{1... | collective-permute-start | bytes 208904 | tf_op jit(solution)/shard_map/ppermute | solution.py:341
  7.9 12.3 %collective-permute-start.5 = (bf16[1024,256]{1,0:T(8,128)(2,1)S(1)}, bf16[1024,256]{1,0:T(8,128)(2,1)S(1)}, u32[]{:S(2)}, u32[]{:S(2)}) collective-permute-start(bf16[1024,256]{1,0:T(8,128)(2,1)S(1)} %get-tuple-element.49.refs_0_), channel_id=1, source_target_pairs={{0,4},{1,5},{2,6},{3,7},{4,0},{5,1},{6,2},{7,3},{8,12},{9,13},{10,... | collective-permute-start | bytes 1572872 | tf_op jit(solution)/shard_map/ppermute | solution.py:341
  12.5 3.6 %copy-start.2 = (s32[4096,1]{0,1:T(1,128)S(1)}, s32[4096,1]{0,1:T(1,128)}, u32[]{:S(2)}) copy-start(s32[4096,1]{0,1:T(1,128)} %param.11) | copy-start | bytes 49156
  12.6 3.6 %copy-start = (s32[2,1024]{1,0:T(2,128)S(1)}, s32[2,1024]{1,0:T(2,128)}, u32[]{:S(2)}) copy-start(s32[2,1024]{1,0:T(2,128)} %refs_2_.1) | copy-start | bytes 24580
  12.6 7.6 %collective-permute-start.6 = (bf16[544,256]{1,0:T(8,128)(2,1)S(1)}, bf16[544,256]{1,0:T(8,128)(2,1)S(1)}, u32[]{:S(2)}, u32[]{:S(2)}) collective-permute-start(bf16[544,256]{1,0:T(8,128)(2,1)S(1)} %constant_dynamic-update-slice_fusion.refs_4_.refs_3_), channel_id=1, source_target_pairs={{0,24},{1,25},{2,26},{3,27},{4,6},{5,7},{6,4},{7,5},{8,16},{9,17},... | collective-permute-start | bytes 835592 | tf_op jit(solution)/shard_map/ppermute | solution.py:341
  15.4 7.7 %collective-permute-start.7 = (bf16[544,256]{1,0:T(8,128)(2,1)S(1)}, bf16[544,256]{1,0:T(8,128)(2,1)S(1)}, u32[]{:S(2)}, u32[]{:S(2)}) collective-permute-start(bf16[544,256]{1,0:T(8,128)(2,1)S(1)} %constant_dynamic-update-slice_fusion.refs_4_.refs_3_), channel_id=1, source_target_pairs={{0,16},{1,17},{2,18},{3,19},{4,7},{5,6},{6,5},{7,4},{8,24},{9,25},... | collective-permute-start | bytes 835592 | tf_op jit(solution)/shard_map/ppermute | solution.py:341
  15.9 7.3 %collective-permute-start.8 = (bf16[544,256]{1,0:T(8,128)(2,1)S(1)}, bf16[544,256]{1,0:T(8,128)(2,1)S(1)}, u32[]{:S(2)}, u32[]{:S(2)}) collective-permute-start(bf16[544,256]{1,0:T(8,128)(2,1)S(1)} %constant_dynamic-update-slice_fusion.refs_4_.refs_3_), channel_id=1, source_target_pairs={{0,8},{1,9},{2,10},{3,11},{4,5},{5,4},{6,7},{7,6},{8,0},{9,1},{10,... | collective-permute-start | bytes 835592 | tf_op jit(solution)/shard_map/ppermute | solution.py:341
  24.0 1.2 %collective-permute-start.9 = (f32[1,1024]{1,0:T(1,128)S(1)}, f32[1,1024]{1,0:T(1,128)S(1)}, u32[]{:S(2)}, u32[]{:S(2)}) collective-permute-start(f32[1,1024]{1,0:T(1,128)S(1)} %get-tuple-element.56), channel_id=1, source_target_pairs={{0,4},{1,5},{2,6},{3,7},{4,0},{5,1},{6,2},{7,3},{8,12},{9,13},{10,... | collective-permute-start | bytes 12296 | tf_op jit(solution)/shard_map/ppermute | solution.py:341
  25.9 12.1 %all-to-all-start = ((f32[32,1,128]{2,1,0:T(1,128)}), f32[32,1,128]{2,1,0:T(1,128)S(1)}, u32[]{:S(2)}, u32[]{:S(2)}) async-start(f32[32,1,128]{2,1,0:T(1,128)} %get-tuple-element.58), calls=%async_computation | async-start | bytes 32768 | tf_op jit(solution)/shard_map/all_to_all | solution.py:441
  32.0 1.2 %collective-permute-start = (f32[32,128]{1,0:T(8,128)S(1)}, f32[32,128]{1,0:T(8,128)S(1)}, u32[]{:S(2)}, u32[]{:S(2)}) collective-permute-start(f32[32,128]{1,0:T(8,128)S(1)} %tally.1.refs_0_), channel_id=1, source_target_pairs={{0,4},{1,5},{2,6},{3,7},{4,0},{5,1},{6,2},{7,3},{8,12},{9,13},{10,... | collective-permute-start | bytes 49160 | tf_op jit(solution)/shard_map/cond/branch_1_fun/ppermute | solution.py:341
  35.0 1.5 %collective-permute-start.1 = (f32[128,384]{1,0:T(8,128)S(1)}, f32[128,384]{1,0:T(8,128)S(1)}, u32[]{:S(2)}, u32[]{:S(2)}) collective-permute-start(f32[128,384]{1,0:T(8,128)S(1)} %get-tuple-element.31), channel_id=1, source_target_pairs={{0,4},{1,5},{2,6},{3,7},{4,0},{5,1},{6,2},{7,3},{8,12},{9,13},{10,... | collective-permute-start | bytes 589832 | tf_op jit(solution)/shard_map/cond/branch_1_fun/ppermute | solution.py:341

commit v8 on v7

--- a/solution.py
+++ b/solution.py
@@ -17,7 +17,7 @@
 
 CORE = 4
 FAN = ((3, 2), (24, 16))
-SPREAD = ((24, 16), (2, 3))
+SPREAD = ((24, 16), (3, 2))
 
 
 def nt_dot(left, right):
@@ -232,19 +232,20 @@
     return best
 
 
-def own_scan_kernel(slot_args, rows, points_ref, centres_ref, picks_ref, owner_ref, piece_ref, *refs):
-    best_ref, norm_ref, place_ref, slot_owner_ref, token_ref = refs
+def own_scan_kernel(slot_args, rows, points_ref, beside_ref, centres_ref, picks_ref, owner_ref, piece_ref, *refs):
+    best_ref, beside_best_ref, norm_ref, place_ref, slot_owner_ref, token_ref = refs
     first_scan_kernel(points_ref, centres_ref, best_ref, norm_ref)
     best_ref[...] = scan_pieces(points_ref, [piece_ref], rows, best_ref[...])
+    lowest = jnp.full(best_ref.shape, -jnp.inf, F32)
+    beside_best_ref[...] = scan_pieces(beside_ref, [piece_ref], rows, lowest)
     slot_kernel(*slot_args, picks_ref, owner_ref, place_ref, slot_owner_ref, token_ref)
 
 
-def both_scan_kernel(rows, points_ref, beside_ref, best_ref, own_ref, piece_ref, *refs):
-    next_ref, next_count_ref, beside_best_ref = refs
+def both_scan_kernel(rows, points_ref, beside_ref, best_ref, beside_best_ref, piece_ref, *refs):
+    next_ref, next_beside_ref, count_ref = refs
     next_ref[...] = scan_pieces(points_ref, [piece_ref], rows, best_ref[...])
-    next_count_ref[...] = add_tally(jnp.zeros(next_count_ref.shape, F32), piece_ref[rows:, :])
-    lowest = jnp.full(beside_best_ref.shape, -jnp.inf, F32)
-    beside_best_ref[...] = scan_pieces(beside_ref, [own_ref, piece_ref], rows, lowest)
+    next_beside_ref[...] = scan_pieces(beside_ref, [piece_ref], rows, beside_best_ref[...])
+    count_ref[...] = add_tally(jnp.zeros(count_ref.shape, F32), piece_ref[rows:, :])
 
 
 def beside_scan_kernel(rows, beside_ref, best_ref, *refs):
@@ -413,18 +414,18 @@
         own = [part[:slots] for part in near] + [part[slots:] for part in near]
         own = jnp.concatenate(own, axis=0)
         others = [permute(own, m) for m in (hop(2), hop(3), both_hops(hop(2), hop(3)))]
-        best, norms, places, slot_owners, scanned = local_call(
+        beside = permute(near_points, swap)
+        best, beside_best, norms, places, slot_owners, scanned = local_call(
             functools.partial(own_scan_kernel, slot_args, piece_rows),
-            (best_shape, best_shape, *slot_shapes, token),
-            (near_points, centres, picks, owner_rows, own),
+            (best_shape, best_shape, best_shape, *slot_shapes, token),
+            (near_points, beside, centres, picks, owner_rows, own),
             "scan_own",
             3.0,
         )
-        beside = permute(near_points, swap)
-        best, counts, beside_best = local_call(
+        best, beside_best, counts = local_call(
             functools.partial(both_scan_kernel, piece_rows),
-            (best_shape, count_shape, best_shape),
-            (near_points, beside, best, own, others[0]),
+            (best_shape, best_shape, count_shape),
+            (near_points, beside, best, beside_best, others[0]),
             "scan_both",
             1.3,
         )

time: 38.9 us -> 38.9 us (level)
    ppermute x10, starting transfers between devices: 10.1 us -> 11.4 us  [permute(): return lax.ppermute(value, AXES, pairs)]
    all_to_all x1, starting transfers between devices: 4.95 us -> 3.86 us  [shards(): shares = lax.all_to_all(share, AXES, 0, 0)]
  transfers between devices with their start and end apart: 11 -> 11, of which waited for: 9 -> 8; matrix products, arithmetic and copies ran while one was open for 0% -> 0% of each run, Pallas kernels for 23% -> 23%
where the time goes in v8:
time: 38.9 us; the launch traced here: 38.7 us
  starting transfers between devices  15.2 us (39%)
  Pallas kernels  12.6 us (32%)
  waiting for transfers between devices  10 us (26%)
  between operations  0.75 us (2%)
    pallas_call x10, Pallas kernels, local_call(): pl.pallas_call(body, out_shape=out_shape, in_specs=specs, out_specs=resul...  12.6 us
    ppermute x10, starting transfers between devices, permute(): return lax.ppermute(value, AXES, pairs)  11.4 us
    ppermute x10, waiting for transfers between devices, permute(): return lax.ppermute(value, AXES, pairs)  9.23 us
    all_to_all x1, starting transfers between devices, shards(): shares = lax.all_to_all(share, AXES, 0, 0)  3.86 us
    all_to_all x1, waiting for transfers between devices, shards(): shares = lax.all_to_all(share, AXES, 0, 0)  0.8 us
  transfers between devices with their start and end apart: 11, of which 8 were waited for; matrix products, arithmetic and copies ran while one was open for 0% of the time, Pallas kernels for 23%

profile of v8, /device:TPU:0, one launch (start us, length us, event | category | flops | bytes accessed | tf_op | source)
XLA Modules:
  0.0 38.7 jit_solution(4572552772783718071)
XLA Ops:
  0.6 1.5 %pick_rows.1 = (bf16[136,256]{1,0:T(8,128)(2,1)S(1)}, bf16[1024,256]{1,0:T(8,128)(2,1)S(1)}) custom-call(s32[2,1024]{1,0:T(2,128)} %refs_3_.1, bf16[1024,256]{1,0:T(8,128)(2,1)} %refs_1_.1, s32[8,128]{1,0:T(8,128)} %bitcast.5), custom_call_target="tpu_custom_call" | custom-call | flops 800000000 | tf_op jit(solution)/shard_map/pick_rows/pallas_call | solution.py:62
  2.2 5.1 %collective-permute-start.3 = (bf16[136,256]{1,0:T(8,128)(2,1)S(1)}, bf16[136,256]{1,0:T(8,128)(2,1)S(1)}, u32[]{:S(2)}, u32[]{:S(2)}) collective-permute-start(bf16[136,256]{1,0:T(8,128)(2,1)S(1)} %get-tuple-element.51), channel_id=1, source_target_pairs={{0,3},{1,2},{2,1},{3,0},{4,28},{5,29},{6,30},{7,31},{8,11},{9,10},... | collective-permute-start | bytes 208904 | tf_op jit(solution)/shard_map/ppermute | solution.py:342
  7.3 0.6 %collective-permute-start.5 = (bf16[136,256]{1,0:T(8,128)(2,1)S(1)}, bf16[136,256]{1,0:T(8,128)(2,1)S(1)}, u32[]{:S(2)}, u32[]{:S(2)}) collective-permute-start(bf16[136,256]{1,0:T(8,128)(2,1)S(1)} %get-tuple-element.51), channel_id=1, source_target_pairs={{0,1},{1,0},{2,3},{3,2},{4,12},{5,13},{6,14},{7,15},{8,9},{9,8},{1... | collective-permute-start | bytes 208904 | tf_op jit(solution)/shard_map/ppermute | solution.py:342
  7.9 1.7 %collective-permute-done.3 = bf16[136,256]{1,0:T(8,128)(2,1)S(1)} collective-permute-done((bf16[136,256]{1,0:T(8,128)(2,1)S(1)}, bf16[136,256]{1,0:T(8,128)(2,1)S(1)}, u32[]{:S(2)}, u32[]{:S(2)}) %collective-permute-start.3) | collective-permute-done | bytes 69664 | tf_op jit(solution)/shard_map/ppermute | solution.py:342
  9.7 2.8 %collective-permute-done.4 = bf16[136,256]{1,0:T(8,128)(2,1)S(1)} collective-permute-done((bf16[136,256]{1,0:T(8,128)(2,1)S(1)}, bf16[136,256]{1,0:T(8,128)(2,1)S(1)}, u32[]{:S(2)}, u32[]{:S(2)}) %collective-permute-start.4) | collective-permute-done | bytes 69664 | tf_op jit(solution)/shard_map/ppermute | solution.py:342
  12.6 2.9 %collective-permute-start.6 = (bf16[544,256]{1,0:T(8,128)(2,1)S(1)}, bf16[544,256]{1,0:T(8,128)(2,1)S(1)}, u32[]{:S(2)}, u32[]{:S(2)}) collective-permute-start(bf16[544,256]{1,0:T(8,128)(2,1)S(1)} %constant_dynamic-update-slice_fusion.refs_5_), channel_id=1, source_target_pairs={{0,24},{1,25},{2,26},{3,27},{4,7},{5,6},{6,5},{7,4},{8,16},{9,17},... | collective-permute-start | bytes 835592 | tf_op jit(solution)/shard_map/ppermute | solution.py:342
  15.5 0.5 %collective-permute-start.7 = (bf16[544,256]{1,0:T(8,128)(2,1)S(1)}, bf16[544,256]{1,0:T(8,128)(2,1)S(1)}, u32[]{:S(2)}, u32[]{:S(2)}) collective-permute-start(bf16[544,256]{1,0:T(8,128)(2,1)S(1)} %constant_dynamic-update-slice_fusion.refs_5_), channel_id=1, source_target_pairs={{0,16},{1,17},{2,18},{3,19},{4,6},{5,7},{6,4},{7,5},{8,24},{9,25},... | collective-permute-start | bytes 835592 | tf_op jit(solution)/shard_map/ppermute | solution.py:342
  16.2 3.4 %scan_own.1 = (f32[8,1024]{1,0:T(8,128)S(1)}, f32[8,1024]{1,0:T(8,128)S(1)}, f32[8,1024]{1,0:T(8,128)S(1)}, s32[16,128]{1,0:T(8,128)S(1)}, s32[16,128]{1,0:T(8,128)S(1)}, /*index=5*/f32[1,256]{1,0:T(1,128)}) custom-call(bf16[1024,256]{1,0:T(8,128)(2,1)S(1)} %get-tuple-element.50.refs_0_, bf16[1024,256]{1,0:T(8,128)(2,1)S(1)} %collective-permute-done.2.refs_1_.refs_0_, ...), custom_call_target="tpu_custom_call" | custom-call | flops 3000000000 | tf_op jit(solution)/shard_map/scan_own/pallas_call | solution.py:62
  19.6 0.6 %collective-permute-done.6.refs_4_ = bf16[544,256]{1,0:T(8,128)(2,1)S(1)} collective-permute-done((bf16[544,256]{1,0:T(8,128)(2,1)S(1)}, bf16[544,256]{1,0:T(8,128)(2,1)S(1)}, u32[]{:S(2)}, u32[]{:S(2)}) %collective-permute-start.6) | collective-permute-done | bytes 278560 | tf_op jit(solution)/shard_map/ppermute | solution.py:342
  20.2 1.0 %scan_both.1 = (f32[8,1024]{1,0:T(8,128)S(1)}, f32[8,1024]{1,0:T(8,128)S(1)}, f32[32,128]{1,0:T(8,128)S(1)}) custom-call(bf16[1024,256]{1,0:T(8,128)(2,1)S(1)} %get-tuple-element.50.refs_0_, bf16[1024,256]{1,0:T(8,128)(2,1)S(1)} %collective-permute-done.2.refs_1_.refs_0_, f32[8,1024]{1,0:T(8,128)S(1)} %get-tuple-element.53.refs_2_, ...), custom_call_target="tpu_custom_call" | custom-call | flops 1300000000 | tf_op jit(solution)/shard_map/scan_both/pallas_call | solution.py:62
  21.3 1.8 %collective-permute-done.7.refs_2_.refs_3_ = bf16[544,256]{1,0:T(8,128)(2,1)S(1)} collective-permute-done((bf16[544,256]{1,0:T(8,128)(2,1)S(1)}, bf16[544,256]{1,0:T(8,128)(2,1)S(1)}, u32[]{:S(2)}, u32[]{:S(2)}) %collective-permute-start.7) | collective-permute-done | bytes 278560 | tf_op jit(solution)/shard_map/ppermute | solution.py:342
  23.2 0.8 %scan_beside.1 = (f32[1,1024]{1,0:T(1,128)S(1)}, f32[1,256]{1,0:T(1,128)S(1)}) custom-call(bf16[1024,256]{1,0:T(8,128)(2,1)S(1)} %collective-permute-done.2.refs_1_.refs_0_, f32[8,1024]{1,0:T(8,128)S(1)} %get-tuple-element.56.refs_1_, bf16[544,256]{1,0:T(8,128)(2,1)S(1)} %collective-permute-done.7.refs_2_.refs_3_, ...), custom_call_target="tpu_custom_call" | custom-call | flops 900000000 | tf_op jit(solution)/shard_map/scan_beside/pallas_call | solution.py:62
  24.0 1.5 %collective-permute-start.9 = (f32[1,1024]{1,0:T(1,128)S(1)}, f32[1,1024]{1,0:T(1,128)S(1)}, u32[]{:S(2)}, u32[]{:S(2)}) collective-permute-start(f32[1,1024]{1,0:T(1,128)S(1)} %get-tuple-element.58), channel_id=1, source_target_pairs={{0,4},{1,5},{2,6},{3,7},{4,0},{5,1},{6,2},{7,3},{8,12},{9,13},{10,... | collective-permute-start | bytes 12296 | tf_op jit(solution)/shard_map/ppermute | solution.py:342
  25.4 0.8 %scan_next.1.refs_1_ = f32[1,1024]{1,0:T(1,128)S(1)} custom-call(bf16[1024,256]{1,0:T(8,128)(2,1)S(1)} %get-tuple-element.50.refs_0_, f32[8,1024]{1,0:T(8,128)S(1)} %get-tuple-element.55.refs_1_, f32[1,256]{1,0:T(1,128)S(1)} %get-tuple-element.57.refs_2_, bf16[544,256]{1,0:T(8,128)(2,1)S(1)} %collective-permute-done.7.refs_2_.refs_3_, ...), custom_call_target="tpu_custom_call" | custom-call | flops 1019200000 | tf_op jit(solution)/shard_map/scan_next/pallas_call | solution.py:62
  26.2 0.7 %nearest.1 = (f32[1,1024]{1,0:T(1,128)S(1)}, f32[32,1,128]{2,1,0:T(1,128)}) custom-call(f32[8,1024]{1,0:T(8,128)S(1)} %get-tuple-element.52.refs_0_, f32[1,1024]{1,0:T(1,128)S(1)} %scan_next.1.refs_1_, f32[1,1024]{1,0:T(1,128)S(1)} %collective-permute-done.9.refs_2_), custom_call_target="tpu_custom_call" | custom-call | flops 500000000 | tf_op jit(solution)/shard_map/nearest/pallas_call | solution.py:62
  26.9 3.9 %all-to-all-start = ((f32[32,1,128]{2,1,0:T(1,128)}), f32[32,1,128]{2,1,0:T(1,128)S(1)}, u32[]{:S(2)}, u32[]{:S(2)}) async-start(f32[32,1,128]{2,1,0:T(1,128)} %get-tuple-element.60), calls=%async_computation | async-start | bytes 32768 | tf_op jit(solution)/shard_map/all_to_all | solution.py:442
  30.8 6.4 %conditional.1 = ((f32[128,256]{1,0:T(8,128)}, f32[1,256]{1,0:T(1,128)S(1)})) conditional(s32[]{:T(128)} %convert_element_type.3, () %tuple.15, (f32[1,1024]{1,0:T(1,128)S(1)}, f32[32,128]{1,0:T(8,128)S(1)}, bf16[544,256]{1,0:T(8,128)(2,1)S(1)}, bf16[544,256]{1,0:T(8,128)(2,1)S(1)}, bf16[544,256]{1,0:T(8,128)(2,1)S(1)}, ...), branch_computations={%region_0.0_spmd, %region_1.0_spmd} | conditional | flops 3500000000 | bytes 852056 | solution.py:461
  30.8 1.1 %tally.1.refs_0_ = f32[32,128]{1,0:T(8,128)S(1)} custom-call(f32[1,1024]{1,0:T(1,128)S(1)} %get-tuple-element.20.refs_0_, f32[32,128]{1,0:T(8,128)S(1)} %get-tuple-element.21.refs_1_, bf16[544,256]{1,0:T(8,128)(2,1)S(1)} %get-tuple-element.22.refs_2_.refs_6_, bf16[544,256]{1,0:T(8,128)(2,1)S(1)} %get-tuple-element.23.refs_3_.refs_8_, ...), custom_call_target="tpu_custom_call" | custom-call | flops 1200000000 | tf_op jit(solution)/shard_map/cond/branch_1_fun/tally/pallas_call | solution.py:62
  32.2 0.9 %collective-permute-done.refs_1_ = f32[32,128]{1,0:T(8,128)S(1)} collective-permute-done((f32[32,128]{1,0:T(8,128)S(1)}, f32[32,128]{1,0:T(8,128)S(1)}, u32[]{:S(2)}, u32[]{:S(2)}) %collective-permute-start) | collective-permute-done | bytes 16416 | tf_op jit(solution)/shard_map/cond/branch_1_fun/ppermute | solution.py:342
  33.1 1.8 %lloyd.1 = (f32[128,384]{1,0:T(8,128)S(1)}, f32[128,384]{1,0:T(8,128)S(1)}) custom-call(f32[32,128]{1,0:T(8,128)S(1)} %tally.1.refs_0_, f32[32,128]{1,0:T(8,128)S(1)} %collective-permute-done.refs_1_, s32[32,128]{1,0:T(8,128)S(1)} %get-tuple-element.25.refs_2_, s32[16,128]{1,0:T(8,128)S(1)} %get-tuple-element.26.refs_3_, ...), custom_call_target="tpu_custom_call" | custom-call | flops 1800000000 | tf_op jit(solution)/shard_map/cond/branch_1_fun/lloyd/pallas_call | solution.py:62
  35.2 1.2 %collective-permute-done.1.refs_1_ = f32[128,384]{1,0:T(8,128)S(1)} collective-permute-done((f32[128,384]{1,0:T(8,128)S(1)}, f32[128,384]{1,0:T(8,128)S(1)}, u32[]{:S(2)}, u32[]{:S(2)}) %collective-permute-start.1) | collective-permute-done | bytes 196640 | tf_op jit(solution)/shard_map/cond/branch_1_fun/ppermute | solution.py:342
  36.4 0.8 %new_centres.1 = (f32[128,256]{1,0:T(8,128)}, f32[1,256]{1,0:T(1,128)S(1)}) custom-call(f32[128,384]{1,0:T(8,128)S(1)} %get-tuple-element.30.refs_0_, f32[128,384]{1,0:T(8,128)S(1)} %collective-permute-done.1.refs_1_), custom_call_target="tpu_custom_call" | custom-call | flops 500000000 | tf_op jit(solution)/shard_map/cond/branch_1_fun/new_centres/pallas_call | solution.py:62
  37.2 0.8 %all-to-all-done.refs_1_ = f32[32,1,128]{2,1,0:T(1,128)S(1)} async-done(((f32[32,1,128]{2,1,0:T(1,128)}), f32[32,1,128]{2,1,0:T(1,128)S(1)}, u32[]{:S(2)}, u32[]{:S(2)}) %all-to-all-start) | async-done | bytes 16416 | tf_op jit(solution)/shard_map/all_to_all | solution.py:442
  38.0 0.7 %finish.1 = f32[1,1024]{1,0:T(1,128)} custom-call(f32[1,1024]{1,0:T(1,128)S(1)} %get-tuple-element.59.refs_0_, f32[32,1,128]{2,1,0:T(1,128)S(1)} %all-to-all-done.refs_1_, f32[1,256]{1,0:T(1,128)S(1)} %get-tuple-element.64.refs_2_), custom_call_target="tpu_custom_call" | custom-call | flops 600000000 | tf_op jit(solution)/shard_map/finish/pallas_call | solution.py:62
  (23 shorter events, 0.9 us)
Async XLA Ops:
  0.6 15.6 %copy-start.1 = (bf16[2048,256]{1,0:T(8,128)(2,1)S(1)}, bf16[2048,256]{1,0:T(8,128)(2,1)}, u32[]{:S(2)}) copy-start(bf16[2048,256]{1,0:T(8,128)(2,1)} %refs_2_.1) | copy-start | bytes 3145732
  2.2 7.5 %collective-permute-start.3 = (bf16[136,256]{1,0:T(8,128)(2,1)S(1)}, bf16[136,256]{1,0:T(8,128)(2,1)S(1)}, u32[]{:S(2)}, u32[]{:S(2)}) collective-permute-start(bf16[136,256]{1,0:T(8,128)(2,1)S(1)} %get-tuple-element.51), channel_id=1, source_target_pairs={{0,3},{1,2},{2,1},{3,0},{4,28},{5,29},{6,30},{7,31},{8,11},{9,10},... | collective-permute-start | bytes 208904 | tf_op jit(solution)/shard_map/ppermute | solution.py:342
  7.3 5.2 %collective-permute-start.4 = (bf16[136,256]{1,0:T(8,128)(2,1)S(1)}, bf16[136,256]{1,0:T(8,128)(2,1)S(1)}, u32[]{:S(2)}, u32[]{:S(2)}) collective-permute-start(bf16[136,256]{1,0:T(8,128)(2,1)S(1)} %get-tuple-element.51), channel_id=1, source_target_pairs={{0,2},{1,3},{2,0},{3,1},{4,20},{5,21},{6,22},{7,23},{8,10},{9,11},... | collective-permute-start | bytes 208904 | tf_op jit(solution)/shard_map/ppermute | solution.py:342
  7.3 5.2 %collective-permute-start.5 = (bf16[136,256]{1,0:T(8,128)(2,1)S(1)}, bf16[136,256]{1,0:T(8,128)(2,1)S(1)}, u32[]{:S(2)}, u32[]{:S(2)}) collective-permute-start(bf16[136,256]{1,0:T(8,128)(2,1)S(1)} %get-tuple-element.51), channel_id=1, source_target_pairs={{0,1},{1,0},{2,3},{3,2},{4,12},{5,13},{6,14},{7,15},{8,9},{9,8},{1... | collective-permute-start | bytes 208904 | tf_op jit(solution)/shard_map/ppermute | solution.py:342
  7.9 8.2 %collective-permute-start.2 = (bf16[1024,256]{1,0:T(8,128)(2,1)S(1)}, bf16[1024,256]{1,0:T(8,128)(2,1)S(1)}, u32[]{:S(2)}, u32[]{:S(2)}) collective-permute-start(bf16[1024,256]{1,0:T(8,128)(2,1)S(1)} %get-tuple-element.50.refs_0_), channel_id=1, source_target_pairs={{0,4},{1,5},{2,6},{3,7},{4,0},{5,1},{6,2},{7,3},{8,12},{9,13},{10,... | collective-permute-start | bytes 1572872 | tf_op jit(solution)/shard_map/ppermute | solution.py:342
  12.5 3.7 %copy-start.2 = (s32[4096,1]{0,1:T(1,128)S(1)}, s32[4096,1]{0,1:T(1,128)}, u32[]{:S(2)}) copy-start(s32[4096,1]{0,1:T(1,128)} %param.11) | copy-start | bytes 49156
  12.6 3.6 %copy-start = (s32[2,1024]{1,0:T(2,128)S(1)}, s32[2,1024]{1,0:T(2,128)}, u32[]{:S(2)}) copy-start(s32[2,1024]{1,0:T(2,128)} %refs_3_.1) | copy-start | bytes 24580
  12.6 7.6 %collective-permute-start.6 = (bf16[544,256]{1,0:T(8,128)(2,1)S(1)}, bf16[544,256]{1,0:T(8,128)(2,1)S(1)}, u32[]{:S(2)}, u32[]{:S(2)}) collective-permute-start(bf16[544,256]{1,0:T(8,128)(2,1)S(1)} %constant_dynamic-update-slice_fusion.refs_5_), channel_id=1, source_target_pairs={{0,24},{1,25},{2,26},{3,27},{4,7},{5,6},{6,5},{7,4},{8,16},{9,17},... | collective-permute-start | bytes 835592 | tf_op jit(solution)/shard_map/ppermute | solution.py:342
  15.5 7.6 %collective-permute-start.7 = (bf16[544,256]{1,0:T(8,128)(2,1)S(1)}, bf16[544,256]{1,0:T(8,128)(2,1)S(1)}, u32[]{:S(2)}, u32[]{:S(2)}) collective-permute-start(bf16[544,256]{1,0:T(8,128)(2,1)S(1)} %constant_dynamic-update-slice_fusion.refs_5_), channel_id=1, source_target_pairs={{0,16},{1,17},{2,18},{3,19},{4,6},{5,7},{6,4},{7,5},{8,24},{9,25},... | collective-permute-start | bytes 835592 | tf_op jit(solution)/shard_map/ppermute | solution.py:342
  16.1 7.1 %collective-permute-start.8 = (bf16[544,256]{1,0:T(8,128)(2,1)S(1)}, bf16[544,256]{1,0:T(8,128)(2,1)S(1)}, u32[]{:S(2)}, u32[]{:S(2)}) collective-permute-start(bf16[544,256]{1,0:T(8,128)(2,1)S(1)} %constant_dynamic-update-slice_fusion.refs_5_), channel_id=1, source_target_pairs={{0,8},{1,9},{2,10},{3,11},{4,5},{5,4},{6,7},{7,6},{8,0},{9,1},{10,... | collective-permute-start | bytes 835592 | tf_op jit(solution)/shard_map/ppermute | solution.py:342
  24.0 2.3 %collective-permute-start.9 = (f32[1,1024]{1,0:T(1,128)S(1)}, f32[1,1024]{1,0:T(1,128)S(1)}, u32[]{:S(2)}, u32[]{:S(2)}) collective-permute-start(f32[1,1024]{1,0:T(1,128)S(1)} %get-tuple-element.58), channel_id=1, source_target_pairs={{0,4},{1,5},{2,6},{3,7},{4,0},{5,1},{6,2},{7,3},{8,12},{9,13},{10,... | collective-permute-start | bytes 12296 | tf_op jit(solution)/shard_map/ppermute | solution.py:342
  26.9 11.0 %all-to-all-start = ((f32[32,1,128]{2,1,0:T(1,128)}), f32[32,1,128]{2,1,0:T(1,128)S(1)}, u32[]{:S(2)}, u32[]{:S(2)}) async-start(f32[32,1,128]{2,1,0:T(1,128)} %get-tuple-element.60), calls=%async_computation | async-start | bytes 32768 | tf_op jit(solution)/shard_map/all_to_all | solution.py:442
  31.9 1.2 %collective-permute-start = (f32[32,128]{1,0:T(8,128)S(1)}, f32[32,128]{1,0:T(8,128)S(1)}, u32[]{:S(2)}, u32[]{:S(2)}) collective-permute-start(f32[32,128]{1,0:T(8,128)S(1)} %tally.1.refs_0_), channel_id=1, source_target_pairs={{0,4},{1,5},{2,6},{3,7},{4,0},{5,1},{6,2},{7,3},{8,12},{9,13},{10,... | collective-permute-start | bytes 49160 | tf_op jit(solution)/shard_map/cond/branch_1_fun/ppermute | solution.py:342
  34.9 1.5 %collective-permute-start.1 = (f32[128,384]{1,0:T(8,128)S(1)}, f32[128,384]{1,0:T(8,128)S(1)}, u32[]{:S(2)}, u32[]{:S(2)}) collective-permute-start(f32[128,384]{1,0:T(8,128)S(1)} %get-tuple-element.31), channel_id=1, source_target_pairs={{0,4},{1,5},{2,6},{3,7},{4,0},{5,1},{6,2},{7,3},{8,12},{9,13},{10,... | collective-permute-start | bytes 589832 | tf_op jit(solution)/shard_map/cond/branch_1_fun/ppermute | solution.py:342

commit v9 on v7

--- a/solution.py
+++ b/solution.py
@@ -261,7 +261,7 @@
     top = jnp.maximum(top_ref[...], beside_ref[...])
     near = jnp.maximum(norm_ref[0:1, :] - 2.0 * top, 0.0)
     near_ref[...] = near
-    share_ref[...] = jnp.broadcast_to(jnp.sum(near, axis=1, keepdims=True)[None], share_ref.shape)
+    share_ref[...] = jnp.broadcast_to(jnp.sum(near, axis=1, keepdims=True), share_ref.shape)
 
 
 def lloyd_kernel(piece_rows, sides, count_refs, owner_ref, place_ref, slot_owner_ref, centres_ref, *refs):
@@ -332,7 +332,7 @@
 
 
 def finish_kernel(total_points, near_ref, share_ref, token_ref, relative_ref):
-    cost = jnp.sum(share_ref[...], axis=0)[0:1, 0:1]
+    cost = jnp.sum(share_ref[...], axis=0, keepdims=True)[:, 0:1]
     relative_ref[...] = near_ref[...] * total_points / cost
 
 
@@ -399,7 +399,7 @@
         kernel = functools.partial(next_scan_kernel, piece_rows)
         return local_call(kernel, top_shape, (points, best, start, *pieces), "scan_next", cost)
 
-    near_shapes = (top_shape, shape((device_count, 1, LANES), F32))
+    near_shapes = (top_shape, shape((device_count, LANES), F32))
     sum_shape = shape((finals, feature_count + LANES), F32)
 
     def centres_of(parts):

time: 38.9 us -> 38.9 us (level)
  no operation moved by 1% of the time
where the time goes in v9:
time: 38.9 us; the launch traced here: 38.7 us
  starting transfers between devices  15 us (39%)
  Pallas kernels  12.5 us (32%)
  waiting for transfers between devices  10.3 us (26%)
  between operations  0.75 us (2%)
    pallas_call x10, Pallas kernels, local_call(): pl.pallas_call(body, out_shape=out_shape, in_specs=specs, out_specs=resul...  12.5 us
    ppermute x10, starting transfers between devices, permute(): return lax.ppermute(value, AXES, pairs)  10.1 us
    ppermute x10, waiting for transfers between devices, permute(): return lax.ppermute(value, AXES, pairs)  9.49 us
    all_to_all x1, starting transfers between devices, shards(): shares = lax.all_to_all(share, AXES, 0, 0)  4.95 us
    all_to_all x1, waiting for transfers between devices, shards(): shares = lax.all_to_all(share, AXES, 0, 0)  0.81 us
  transfers between devices with their start and end apart: 11, of which 9 were waited for; matrix products, arithmetic and copies ran while one was open for 0% of the time, Pallas kernels for 23%

profile of v9, /device:TPU:0, one launch (start us, length us, event | category | flops | bytes accessed | tf_op | source)
XLA Modules:
  0.0 38.7 jit_solution(17088019462887662323)
XLA Ops:
  0.6 1.5 %pick_rows.1 = (bf16[136,256]{1,0:T(8,128)(2,1)S(1)}, bf16[1024,256]{1,0:T(8,128)(2,1)S(1)}) custom-call(s32[2,1024]{1,0:T(2,128)} %refs_2_.1, bf16[1024,256]{1,0:T(8,128)(2,1)} %refs_1_.2, s32[8,128]{1,0:T(8,128)} %bitcast.10), custom_call_target="tpu_custom_call" | custom-call | flops 800000000 | tf_op jit(solution)/shard_map/pick_rows/pallas_call | solution.py:62
  2.2 5.1 %collective-permute-start.2 = (bf16[136,256]{1,0:T(8,128)(2,1)S(1)}, bf16[136,256]{1,0:T(8,128)(2,1)S(1)}, u32[]{:S(2)}, u32[]{:S(2)}) collective-permute-start(bf16[136,256]{1,0:T(8,128)(2,1)S(1)} %get-tuple-element.50), channel_id=1, source_target_pairs={{0,3},{1,2},{2,1},{3,0},{4,28},{5,29},{6,30},{7,31},{8,11},{9,10},... | collective-permute-start | bytes 208904 | tf_op jit(solution)/shard_map/ppermute | solution.py:341
  7.3 0.6 %collective-permute-start.4 = (bf16[136,256]{1,0:T(8,128)(2,1)S(1)}, bf16[136,256]{1,0:T(8,128)(2,1)S(1)}, u32[]{:S(2)}, u32[]{:S(2)}) collective-permute-start(bf16[136,256]{1,0:T(8,128)(2,1)S(1)} %get-tuple-element.50), channel_id=1, source_target_pairs={{0,1},{1,0},{2,3},{3,2},{4,12},{5,13},{6,14},{7,15},{8,9},{9,8},{1... | collective-permute-start | bytes 208904 | tf_op jit(solution)/shard_map/ppermute | solution.py:341
  7.9 1.7 %collective-permute-done.2 = bf16[136,256]{1,0:T(8,128)(2,1)S(1)} collective-permute-done((bf16[136,256]{1,0:T(8,128)(2,1)S(1)}, bf16[136,256]{1,0:T(8,128)(2,1)S(1)}, u32[]{:S(2)}, u32[]{:S(2)}) %collective-permute-start.2) | collective-permute-done | bytes 69664 | tf_op jit(solution)/shard_map/ppermute | solution.py:341
  9.7 2.8 %collective-permute-done.3 = bf16[136,256]{1,0:T(8,128)(2,1)S(1)} collective-permute-done((bf16[136,256]{1,0:T(8,128)(2,1)S(1)}, bf16[136,256]{1,0:T(8,128)(2,1)S(1)}, u32[]{:S(2)}, u32[]{:S(2)}) %collective-permute-start.3) | collective-permute-done | bytes 69664 | tf_op jit(solution)/shard_map/ppermute | solution.py:341
  12.6 2.8 %collective-permute-start.6 = (bf16[544,256]{1,0:T(8,128)(2,1)S(1)}, bf16[544,256]{1,0:T(8,128)(2,1)S(1)}, u32[]{:S(2)}, u32[]{:S(2)}) collective-permute-start(bf16[544,256]{1,0:T(8,128)(2,1)S(1)} %constant_dynamic-update-slice_fusion.refs_4_.refs_3_), channel_id=1, source_target_pairs={{0,24},{1,25},{2,26},{3,27},{4,6},{5,7},{6,4},{7,5},{8,16},{9,17},... | collective-permute-start | bytes 835592 | tf_op jit(solution)/shard_map/ppermute | solution.py:341
  15.4 0.5 %collective-permute-start.7 = (bf16[544,256]{1,0:T(8,128)(2,1)S(1)}, bf16[544,256]{1,0:T(8,128)(2,1)S(1)}, u32[]{:S(2)}, u32[]{:S(2)}) collective-permute-start(bf16[544,256]{1,0:T(8,128)(2,1)S(1)} %constant_dynamic-update-slice_fusion.refs_4_.refs_3_), channel_id=1, source_target_pairs={{0,16},{1,17},{2,18},{3,19},{4,7},{5,6},{6,5},{7,4},{8,24},{9,25},... | collective-permute-start | bytes 835592 | tf_op jit(solution)/shard_map/ppermute | solution.py:341
  16.2 3.1 %scan_own.1 = (f32[8,1024]{1,0:T(8,128)S(1)}, f32[8,1024]{1,0:T(8,128)S(1)}, s32[16,128]{1,0:T(8,128)S(1)}, s32[16,128]{1,0:T(8,128)S(1)}, f32[1,256]{1,0:T(1,128)}) custom-call(bf16[1024,256]{1,0:T(8,128)(2,1)S(1)} %get-tuple-element.49.refs_0_, bf16[2048,256]{1,0:T(8,128)(2,1)S(1)} %copy-done.1, s32[2,1024]{1,0:T(2,128)S(1)} %copy-done, ...), custom_call_target="tpu_custom_call" | custom-call | flops 3000000000 | tf_op jit(solution)/shard_map/scan_own/pallas_call | solution.py:62
  19.3 0.9 %collective-permute-done.6.refs_4_ = bf16[544,256]{1,0:T(8,128)(2,1)S(1)} collective-permute-done((bf16[544,256]{1,0:T(8,128)(2,1)S(1)}, bf16[544,256]{1,0:T(8,128)(2,1)S(1)}, u32[]{:S(2)}, u32[]{:S(2)}) %collective-permute-start.6) | collective-permute-done | bytes 278560 | tf_op jit(solution)/shard_map/ppermute | solution.py:341
  20.2 1.3 %scan_both.1 = (f32[8,1024]{1,0:T(8,128)S(1)}, f32[32,128]{1,0:T(8,128)S(1)}, f32[8,1024]{1,0:T(8,128)S(1)}) custom-call(bf16[1024,256]{1,0:T(8,128)(2,1)S(1)} %get-tuple-element.49.refs_0_, bf16[1024,256]{1,0:T(8,128)(2,1)S(1)} %collective-permute-done.5.refs_1_.refs_0_, f32[8,1024]{1,0:T(8,128)S(1)} %get-tuple-element.52.refs_2_, ...), custom_call_target="tpu_custom_call" | custom-call | flops 1300000000 | tf_op jit(solution)/shard_map/scan_both/pallas_call | solution.py:62
  21.6 1.5 %collective-permute-done.7.refs_2_.refs_3_ = bf16[544,256]{1,0:T(8,128)(2,1)S(1)} collective-permute-done((bf16[544,256]{1,0:T(8,128)(2,1)S(1)}, bf16[544,256]{1,0:T(8,128)(2,1)S(1)}, u32[]{:S(2)}, u32[]{:S(2)}) %collective-permute-start.7) | collective-permute-done | bytes 278560 | tf_op jit(solution)/shard_map/ppermute | solution.py:341
  23.2 0.8 %scan_beside.1 = (f32[1,1024]{1,0:T(1,128)S(1)}, f32[1,256]{1,0:T(1,128)S(1)}) custom-call(bf16[1024,256]{1,0:T(8,128)(2,1)S(1)} %collective-permute-done.5.refs_1_.refs_0_, f32[8,1024]{1,0:T(8,128)S(1)} %get-tuple-element.54.refs_1_, bf16[544,256]{1,0:T(8,128)(2,1)S(1)} %collective-permute-done.7.refs_2_.refs_3_, ...), custom_call_target="tpu_custom_call" | custom-call | flops 900000000 | tf_op jit(solution)/shard_map/scan_beside/pallas_call | solution.py:62
  24.1 0.8 %scan_next.1.refs_1_ = f32[1,1024]{1,0:T(1,128)S(1)} custom-call(bf16[1024,256]{1,0:T(8,128)(2,1)S(1)} %get-tuple-element.49.refs_0_, f32[8,1024]{1,0:T(8,128)S(1)} %get-tuple-element.53.refs_1_, f32[1,256]{1,0:T(1,128)S(1)} %get-tuple-element.55.refs_2_, bf16[544,256]{1,0:T(8,128)(2,1)S(1)} %collective-permute-done.7.refs_2_.refs_3_, ...), custom_call_target="tpu_custom_call" | custom-call | flops 1019200000 | tf_op jit(solution)/shard_map/scan_next/pallas_call | solution.py:62
  25.2 0.7 %nearest.1 = (f32[1,1024]{1,0:T(1,128)S(1)}, f32[32,128]{1,0:T(8,128)}) custom-call(f32[8,1024]{1,0:T(8,128)S(1)} %get-tuple-element.51.refs_0_, f32[1,1024]{1,0:T(1,128)S(1)} %scan_next.1.refs_1_, f32[1,1024]{1,0:T(1,128)S(1)} %collective-permute-done.9.refs_2_), custom_call_target="tpu_custom_call" | custom-call | flops 500000000 | tf_op jit(solution)/shard_map/nearest/pallas_call | solution.py:62
  25.9 5.0 %all-to-all-start = ((f32[32,1,128]{2,1,0:T(1,128)}), f32[32,1,128]{2,1,0:T(1,128)S(1)}, u32[]{:S(2)}, u32[]{:S(2)}) async-start(f32[32,1,128]{2,1,0:T(1,128)} %bitcast.3), calls=%async_computation | async-start | bytes 32768 | tf_op jit(solution)/shard_map/all_to_all | solution.py:441
  30.9 6.4 %conditional.1 = ((f32[128,256]{1,0:T(8,128)}, f32[1,256]{1,0:T(1,128)S(1)})) conditional(s32[]{:T(128)} %convert_element_type.3, () %tuple.15, (f32[1,1024]{1,0:T(1,128)S(1)}, f32[32,128]{1,0:T(8,128)S(1)}, bf16[544,256]{1,0:T(8,128)(2,1)S(1)}, bf16[544,256]{1,0:T(8,128)(2,1)S(1)}, bf16[544,256]{1,0:T(8,128)(2,1)S(1)}, ...), branch_computations={%region_0.0_spmd, %region_1.0_spmd} | conditional | flops 3500000000 | bytes 852056 | solution.py:460
  30.9 1.1 %tally.1.refs_0_ = f32[32,128]{1,0:T(8,128)S(1)} custom-call(f32[1,1024]{1,0:T(1,128)S(1)} %get-tuple-element.20.refs_0_, f32[32,128]{1,0:T(8,128)S(1)} %get-tuple-element.21.refs_1_, bf16[544,256]{1,0:T(8,128)(2,1)S(1)} %get-tuple-element.22.refs_2_.refs_6_, bf16[544,256]{1,0:T(8,128)(2,1)S(1)} %get-tuple-element.23.refs_3_.refs_8_, ...), custom_call_target="tpu_custom_call" | custom-call | flops 1200000000 | tf_op jit(solution)/shard_map/cond/branch_1_fun/tally/pallas_call | solution.py:62
  32.2 0.9 %collective-permute-done.refs_1_ = f32[32,128]{1,0:T(8,128)S(1)} collective-permute-done((f32[32,128]{1,0:T(8,128)S(1)}, f32[32,128]{1,0:T(8,128)S(1)}, u32[]{:S(2)}, u32[]{:S(2)}) %collective-permute-start) | collective-permute-done | bytes 16416 | tf_op jit(solution)/shard_map/cond/branch_1_fun/ppermute | solution.py:341
  33.2 1.8 %lloyd.1 = (f32[128,384]{1,0:T(8,128)S(1)}, f32[128,384]{1,0:T(8,128)S(1)}) custom-call(f32[32,128]{1,0:T(8,128)S(1)} %tally.1.refs_0_, f32[32,128]{1,0:T(8,128)S(1)} %collective-permute-done.refs_1_, s32[32,128]{1,0:T(8,128)S(1)} %get-tuple-element.25.refs_2_, s32[16,128]{1,0:T(8,128)S(1)} %get-tuple-element.26.refs_3_, ...), custom_call_target="tpu_custom_call" | custom-call | flops 1800000000 | tf_op jit(solution)/shard_map/cond/branch_1_fun/lloyd/pallas_call | solution.py:62
  34.9 0.3 collective-permute-start.1
  35.3 1.2 %collective-permute-done.1.refs_1_ = f32[128,384]{1,0:T(8,128)S(1)} collective-permute-done((f32[128,384]{1,0:T(8,128)S(1)}, f32[128,384]{1,0:T(8,128)S(1)}, u32[]{:S(2)}, u32[]{:S(2)}) %collective-permute-start.1) | collective-permute-done | bytes 196640 | tf_op jit(solution)/shard_map/cond/branch_1_fun/ppermute | solution.py:341
  36.5 0.8 %new_centres.1 = (f32[128,256]{1,0:T(8,128)}, f32[1,256]{1,0:T(1,128)S(1)}) custom-call(f32[128,384]{1,0:T(8,128)S(1)} %get-tuple-element.30.refs_0_, f32[128,384]{1,0:T(8,128)S(1)} %collective-permute-done.1.refs_1_), custom_call_target="tpu_custom_call" | custom-call | flops 500000000 | tf_op jit(solution)/shard_map/cond/branch_1_fun/new_centres/pallas_call | solution.py:62
  37.2 0.8 %all-to-all-done = f32[32,1,128]{2,1,0:T(1,128)S(1)} async-done(((f32[32,1,128]{2,1,0:T(1,128)}), f32[32,1,128]{2,1,0:T(1,128)S(1)}, u32[]{:S(2)}, u32[]{:S(2)}) %all-to-all-start) | async-done | bytes 16416 | tf_op jit(solution)/shard_map/all_to_all | solution.py:441
  38.0 0.7 %finish.1 = f32[1,1024]{1,0:T(1,128)} custom-call(f32[1,1024]{1,0:T(1,128)S(1)} %get-tuple-element.57.refs_0_, f32[32,128]{1,0:T(8,128)S(1)} %bitcast.7, f32[1,256]{1,0:T(1,128)S(1)} %get-tuple-element.62.refs_2_), custom_call_target="tpu_custom_call" | custom-call | flops 600000000 | tf_op jit(solution)/shard_map/finish/pallas_call | solution.py:62
  (23 shorter events, 1.2 us)
Async XLA Ops:
  0.6 15.5 %copy-start.1 = (bf16[2048,256]{1,0:T(8,128)(2,1)S(1)}, bf16[2048,256]{1,0:T(8,128)(2,1)}, u32[]{:S(2)}) copy-start(bf16[2048,256]{1,0:T(8,128)(2,1)} %refs_1_.3) | copy-start | bytes 3145732
  2.2 7.5 %collective-permute-start.2 = (bf16[136,256]{1,0:T(8,128)(2,1)S(1)}, bf16[136,256]{1,0:T(8,128)(2,1)S(1)}, u32[]{:S(2)}, u32[]{:S(2)}) collective-permute-start(bf16[136,256]{1,0:T(8,128)(2,1)S(1)} %get-tuple-element.50), channel_id=1, source_target_pairs={{0,3},{1,2},{2,1},{3,0},{4,28},{5,29},{6,30},{7,31},{8,11},{9,10},... | collective-permute-start | bytes 208904 | tf_op jit(solution)/shard_map/ppermute | solution.py:341
  7.3 5.2 %collective-permute-start.3 = (bf16[136,256]{1,0:T(8,128)(2,1)S(1)}, bf16[136,256]{1,0:T(8,128)(2,1)S(1)}, u32[]{:S(2)}, u32[]{:S(2)}) collective-permute-start(bf16[136,256]{1,0:T(8,128)(2,1)S(1)} %get-tuple-element.50), channel_id=1, source_target_pairs={{0,2},{1,3},{2,0},{3,1},{4,20},{5,21},{6,22},{7,23},{8,10},{9,11},... | collective-permute-start | bytes 208904 | tf_op jit(solution)/shard_map/ppermute | solution.py:341
  7.3 5.2 %collective-permute-start.4 = (bf16[136,256]{1,0:T(8,128)(2,1)S(1)}, bf16[136,256]{1,0:T(8,128)(2,1)S(1)}, u32[]{:S(2)}, u32[]{:S(2)}) collective-permute-start(bf16[136,256]{1,0:T(8,128)(2,1)S(1)} %get-tuple-element.50), channel_id=1, source_target_pairs={{0,1},{1,0},{2,3},{3,2},{4,12},{5,13},{6,14},{7,15},{8,9},{9,8},{1... | collective-permute-start | bytes 208904 | tf_op jit(solution)/shard_map/ppermute | solution.py:341
  7.9 12.3 %collective-permute-start.5 = (bf16[1024,256]{1,0:T(8,128)(2,1)S(1)}, bf16[1024,256]{1,0:T(8,128)(2,1)S(1)}, u32[]{:S(2)}, u32[]{:S(2)}) collective-permute-start(bf16[1024,256]{1,0:T(8,128)(2,1)S(1)} %get-tuple-element.49.refs_0_), channel_id=1, source_target_pairs={{0,4},{1,5},{2,6},{3,7},{4,0},{5,1},{6,2},{7,3},{8,12},{9,13},{10,... | collective-permute-start | bytes 1572872 | tf_op jit(solution)/shard_map/ppermute | solution.py:341
  12.5 3.6 %copy-start.2 = (s32[4096,1]{0,1:T(1,128)S(1)}, s32[4096,1]{0,1:T(1,128)}, u32[]{:S(2)}) copy-start(s32[4096,1]{0,1:T(1,128)} %param.11) | copy-start | bytes 49156
  12.6 3.6 %copy-start = (s32[2,1024]{1,0:T(2,128)S(1)}, s32[2,1024]{1,0:T(2,128)}, u32[]{:S(2)}) copy-start(s32[2,1024]{1,0:T(2,128)} %refs_2_.1) | copy-start | bytes 24580
  12.6 7.6 %collective-permute-start.6 = (bf16[544,256]{1,0:T(8,128)(2,1)S(1)}, bf16[544,256]{1,0:T(8,128)(2,1)S(1)}, u32[]{:S(2)}, u32[]{:S(2)}) collective-permute-start(bf16[544,256]{1,0:T(8,128)(2,1)S(1)} %constant_dynamic-update-slice_fusion.refs_4_.refs_3_), channel_id=1, source_target_pairs={{0,24},{1,25},{2,26},{3,27},{4,6},{5,7},{6,4},{7,5},{8,16},{9,17},... | collective-permute-start | bytes 835592 | tf_op jit(solution)/shard_map/ppermute | solution.py:341
  15.4 7.7 %collective-permute-start.7 = (bf16[544,256]{1,0:T(8,128)(2,1)S(1)}, bf16[544,256]{1,0:T(8,128)(2,1)S(1)}, u32[]{:S(2)}, u32[]{:S(2)}) collective-permute-start(bf16[544,256]{1,0:T(8,128)(2,1)S(1)} %constant_dynamic-update-slice_fusion.refs_4_.refs_3_), channel_id=1, source_target_pairs={{0,16},{1,17},{2,18},{3,19},{4,7},{5,6},{6,5},{7,4},{8,24},{9,25},... | collective-permute-start | bytes 835592 | tf_op jit(solution)/shard_map/ppermute | solution.py:341
  15.9 7.3 %collective-permute-start.8 = (bf16[544,256]{1,0:T(8,128)(2,1)S(1)}, bf16[544,256]{1,0:T(8,128)(2,1)S(1)}, u32[]{:S(2)}, u32[]{:S(2)}) collective-permute-start(bf16[544,256]{1,0:T(8,128)(2,1)S(1)} %constant_dynamic-update-slice_fusion.refs_4_.refs_3_), channel_id=1, source_target_pairs={{0,8},{1,9},{2,10},{3,11},{4,5},{5,4},{6,7},{7,6},{8,0},{9,1},{10,... | collective-permute-start | bytes 835592 | tf_op jit(solution)/shard_map/ppermute | solution.py:341
  24.0 1.2 %collective-permute-start.9 = (f32[1,1024]{1,0:T(1,128)S(1)}, f32[1,1024]{1,0:T(1,128)S(1)}, u32[]{:S(2)}, u32[]{:S(2)}) collective-permute-start(f32[1,1024]{1,0:T(1,128)S(1)} %get-tuple-element.56), channel_id=1, source_target_pairs={{0,4},{1,5},{2,6},{3,7},{4,0},{5,1},{6,2},{7,3},{8,12},{9,13},{10,... | collective-permute-start | bytes 12296 | tf_op jit(solution)/shard_map/ppermute | solution.py:341
  25.9 12.1 %all-to-all-start = ((f32[32,1,128]{2,1,0:T(1,128)}), f32[32,1,128]{2,1,0:T(1,128)S(1)}, u32[]{:S(2)}, u32[]{:S(2)}) async-start(f32[32,1,128]{2,1,0:T(1,128)} %bitcast.3), calls=%async_computation | async-start | bytes 32768 | tf_op jit(solution)/shard_map/all_to_all | solution.py:441
  32.0 1.2 %collective-permute-start = (f32[32,128]{1,0:T(8,128)S(1)}, f32[32,128]{1,0:T(8,128)S(1)}, u32[]{:S(2)}, u32[]{:S(2)}) collective-permute-start(f32[32,128]{1,0:T(8,128)S(1)} %tally.1.refs_0_), channel_id=1, source_target_pairs={{0,4},{1,5},{2,6},{3,7},{4,0},{5,1},{6,2},{7,3},{8,12},{9,13},{10,... | collective-permute-start | bytes 49160 | tf_op jit(solution)/shard_map/cond/branch_1_fun/ppermute | solution.py:341
  34.9 1.5 %collective-permute-start.1 = (f32[128,384]{1,0:T(8,128)S(1)}, f32[128,384]{1,0:T(8,128)S(1)}, u32[]{:S(2)}, u32[]{:S(2)}) collective-permute-start(f32[128,384]{1,0:T(8,128)S(1)} %get-tuple-element.31), channel_id=1, source_target_pairs={{0,4},{1,5},{2,6},{3,7},{4,0},{5,1},{6,2},{7,3},{8,12},{9,13},{10,... | collective-permute-start | bytes 589832 | tf_op jit(solution)/shard_map/cond/branch_1_fun/ppermute | solution.py:341
